TPU v7x, 128 devices: a whole 4x4x4 slice. The times are simulated.
128 devices in a mesh: ctx: 8 (over x_lo, y), img: 16 (over x_hi, z, core).
Axes of the slice: x: 4 (x_hi: 2, x_lo: 2; x = x_hi * 2 + x_lo), y: 4, z: 4, core: 2. Of those that a mesh axis runs over, the one named last changes fastest.
Arguments:
- patches: bfloat16 [8, 6144, 1280], P('ctx', 'img')
- window_ids: int32 [8, 6144], P('ctx', 'img'), may hold values from 0 to 49151, as said below
- counts: int32 [8], P('ctx'), may hold values from 3072 to 6144, as said below
- gain_one: bfloat16 [1280], replicated, may hold values from 0.099609375 to 1.8984375
- w_qkv1: bfloat16 [3, 1280, 1280], replicated
- w_out1: bfloat16 [1280, 1280], replicated, may hold values from -0.625 to 0.625
- gain_two: bfloat16 [1280], replicated, may hold values from 0.099609375 to 1.8984375
- w_qkv2: bfloat16 [3, 1280, 1280], P(None, None, 'img')
- w_out2: bfloat16 [1280, 1280], replicated, may hold values from -2.5 to 2.5
- gain_out: bfloat16 [1280], replicated, may hold values from 0.099609375 to 1.8984375
- slots: int32 [12288], P(('ctx', 'img')), may hold values from 0 to 12287, as said below
Outputs:
- context_rows: bfloat16 [12288, 5120], P(('ctx', 'img'))
Inputs may be any that keep to these rules, and one draw needn't show every extreme that they name: `window_ids`: patches with equal ids form one window: consecutive patches inside one device's block of 384 patches of one image, at most 64 of them, and some window has exactly 64; different windows have different ids. Patches of image i at positions counts[i] and later are padding. Some image is full. slots holds every row number once. The merged rows of one device (aligned blocks of 96 entries) go to exactly 48 devices' blocks of context rows, 2 to each of them.
All inputs are finite; a program needn't handle non-finite values.
Results may differ from a plain program's by a relative error of at most 0.019.
Values may be sent and summed in bfloat16 or wider, within the bound.
No kernel may reach another device: no remote copies, remote signals or barrier semaphores. Data moves between devices by JAX's collectives and lax.ppermute only.
A program may use at most 192 MiB of HBM per device.

v0:
```python
import math

import jax
import jax.numpy as jnp
from jax import lax
from jax.sharding import PartitionSpec as P

HEAD_DIM = 80
D = 1280


EPSILON = 1e-06
MASKED_SCORE = -1e30


def normed(values, gain):
    values = values.astype(jnp.float32)
    return (
        values
        * lax.rsqrt(jnp.mean(values * values, axis=-1, keepdims=True) + EPSILON)
        * gain.astype(jnp.float32)
    )


def split_heads(row_block):
    return row_block.reshape(row_block.shape[0], -1, HEAD_DIM)


def attend_block(query_heads, key_heads, value_heads, allowed):
    scores = jnp.einsum(
        "qhd,khd->hqk", query_heads, key_heads, preferred_element_type=jnp.float32
    ) * HEAD_DIM ** (-0.5)
    scores = jnp.where(allowed[None], scores, MASKED_SCORE)
    maxima = jnp.max(scores, axis=-1)
    weights = jnp.where(allowed[None], jnp.exp(scores - maxima[:, :, None]), 0.0)
    totals = jnp.sum(weights, axis=-1)
    summed = jnp.einsum(
        "hqk,khd->qhd",
        weights.astype(jnp.bfloat16),
        value_heads,
        preferred_element_type=jnp.float32,
    )
    return (maxima, totals, summed)


def finish(totals, summed):
    return (summed / totals.T[:, :, None]).astype(jnp.bfloat16).reshape(summed.shape[0], -1)


def on_device(
    patches, window_ids, counts, gain_one, w_qkv1, w_out1, gain_two, w_qkv2, w_out2, gain_out, slots
):
    first = patches[0].astype(jnp.float32)
    patch_rows = first.shape[0]
    hidden = normed(first, gain_one).astype(jnp.bfloat16)
    projected = jnp.einsum(
        "pd,tde->tpe", hidden, w_qkv1, preferred_element_type=jnp.float32
    ).astype(jnp.bfloat16)
    local_ids = window_ids[0]
    allowed = local_ids[:, None] == local_ids[None, :]
    maxima, totals, summed = attend_block(
        split_heads(projected[0]), split_heads(projected[1]), split_heads(projected[2]), allowed
    )
    attended = finish(totals, summed)
    second = (first + jnp.dot(attended, w_out1, preferred_element_type=jnp.float32)).astype(
        jnp.bfloat16
    )
    hidden = normed(second, gain_two).astype(jnp.bfloat16)
    key_count = counts[0]
    projected = jnp.einsum(
        "pd,tde->tpe",
        hidden,
        lax.all_gather(w_qkv2, "img", axis=2, tiled=True),
        preferred_element_type=jnp.float32,
    ).astype(jnp.bfloat16)
    query_heads = split_heads(projected[0])
    head_count = query_heads.shape[1]
    start_state = (
        jnp.full((head_count, patch_rows), MASKED_SCORE, jnp.float32),
        jnp.zeros((head_count, patch_rows), jnp.float32),
        jnp.zeros((patch_rows, head_count, HEAD_DIM), jnp.float32),
    )
    carried = start_state
    key_part = lax.all_gather(projected[1], "img", axis=0, tiled=True)
    value_part = lax.all_gather(projected[2], "img", axis=0, tiled=True)
    row_count = key_part.shape[0]
    block_rows = math.gcd(row_count, 512)
    step_count = row_count // block_rows
    key_blocks = key_part.reshape(step_count, block_rows, head_count, HEAD_DIM)
    value_blocks = value_part.reshape(step_count, block_rows, head_count, HEAD_DIM)
    positions = block_rows * jnp.arange(step_count, dtype=jnp.int32)

    def one_step(running, inputs):
        key_block, value_block, position = inputs
        key_valid = position + jnp.arange(block_rows, dtype=jnp.int32) < key_count
        block_allowed = jnp.broadcast_to(key_valid[None, :], (patch_rows, block_rows))
        block_max, block_total, block_sum = attend_block(
            query_heads, key_block, value_block, block_allowed
        )
        old_max, old_total, old_sum = running
        new_max = jnp.maximum(old_max, block_max)
        old_scale = jnp.exp(old_max - new_max)
        block_scale = jnp.exp(block_max - new_max)
        new_total = old_total * old_scale + block_total * block_scale
        new_sum = old_sum * old_scale.T[:, :, None] + block_sum * block_scale.T[:, :, None]
        return ((new_max, new_total, new_sum), None)

    carried, unused = lax.scan(one_step, carried, (key_blocks, value_blocks, positions))
    final_max, totals, summed = carried
    attended = finish(totals, summed)
    third = second.astype(jnp.float32) + jnp.dot(
        attended, w_out2, preferred_element_type=jnp.float32
    )
    merged = normed(third, gain_out).astype(jnp.bfloat16).reshape(patch_rows // 4, 4 * D)
    merged_rows = merged.shape[0]
    ctx_count = lax.axis_size("ctx")
    img_count = lax.axis_size("img")
    device_count = ctx_count * img_count
    capacity = max(2, 2 * merged_rows // device_count)
    target = slots // merged_rows
    local_slot = slots % merged_rows
    row_order = jnp.arange(merged_rows, dtype=jnp.int32)
    earlier = (target[:, None] == target[None, :]) & (row_order[None, :] < row_order[:, None])
    rank_within = jnp.sum(earlier.astype(jnp.int32), axis=1)
    bucket = target * capacity + rank_within
    send_rows = (
        jnp.zeros((device_count * capacity, merged.shape[1]), jnp.bfloat16).at[bucket].set(merged)
    )
    send_slots = jnp.full((device_count * capacity,), -1, jnp.int32).at[bucket].set(local_slot)
    got_rows, got_slots = (
        lax.all_to_all(
            send_rows.reshape(device_count, capacity, merged.shape[1]),
            ("ctx", "img"),
            split_axis=0,
            concat_axis=0,
            tiled=True,
        ),
        lax.all_to_all(
            send_slots.reshape(device_count, capacity),
            ("ctx", "img"),
            split_axis=0,
            concat_axis=0,
            tiled=True,
        ),
    )
    got_rows = got_rows.reshape(-1, merged.shape[1])
    got_slots = got_slots.reshape(-1)
    placed = jnp.where(got_slots >= 0, got_slots, merged_rows)
    return jnp.zeros_like(merged).at[placed].set(got_rows, mode="drop")


def solution(mesh):
    return jax.shard_map(
        on_device,
        mesh=mesh,
        in_specs=(
            P("ctx", "img", None),
            P("ctx", "img"),
            P("ctx"),
            P(),
            P(),
            P(),
            P(),
            P(None, None, "img"),
            P(),
            P(),
            P(("ctx", "img")),
        ),
        out_specs=P(("ctx", "img"), None),
        check_vma=False,
    )
```

profile of v0, /device:TPU:1, one launch (start us, length us, event | category | flops | bytes accessed | tf_op | source)
XLA Modules:
  0.0 759.4 jit_solution(6473816601243954970)
XLA Ops:
  9.7 8.2 %fusion.31 = bf16[3,384,1280]{2,1,0:T(8,128)(2,1)S(1)} fusion(bf16[3,1280,1280]{2,1,0:T(8,128)(2,1)} %param.17, bf16[1,384,1280]{2,1,0:T(8,128)(2,1)} %param.13, f32[1280]{0:T(1024)S(1)} %convert_element_type.61, f32[384]{0:T(512)S(1)} %add_rsqrt_fusion.2), kind=kOutput, calls=%fused_computation.45 | convolution fusion | flops 3778314240 | bytes 13769216 | tf_op jit(solution)/shard_map/pd,tde->tpe/dot_general | solution.py:56
  26.8 7.9 %fusion.65 = (f32[16,384]{1,0:T(8,128)S(1)}, bf16[16,384,384]{1,2,0:T(8,128)(2,1)}) fusion(pred[384,384]{0,1:T(8,128)(4,1)S(1)} %broadcast_compare_fusion, bf16[384,16,80]{0,2,1:T(8,128)(2,1)} %bitcast.98, bf16[384,16,80]{0,2,1:T(8,128)(2,1)} %bitcast.100), kind=kOutput, calls=%fused_computation.96 | convolution fusion | flops 391643520 | bytes 6856704 | tf_op jit(solution)/shard_map/sub | solution.py:35
  41.0 51.8 %all-gather.6.cloned.1.call-done = bf16[3,1280,1280]{1,2,0:T(8,128)(2,1)} async-done(((bf16[3,1280,80]{1,2,0:T(8,128)(2,1)}), bf16[3,1280,1280]{1,2,0:T(8,128)(2,1)}) %all-gather.6.cloned.1.call-update) | async-done | bytes 9830416 | tf_op jit(solution)/shard_map/all_gather | solution.py:73
  92.8 8.2 %fusion.32 = bf16[3,384,1280]{2,1,0:T(8,128)(2,1)S(1)} fusion(bf16[3,1280,1280]{1,2,0:T(8,128)(2,1)} %all-gather.6.cloned.1.call-done, bf16[384,1280]{1,0:T(8,128)(2,1)} %get-tuple-element.156, f32[1280]{0:T(1024)S(1)} %convert_element_type.69, f32[384]{0:T(512)S(1)} %add_rsqrt_fusion.1), kind=kOutput, calls=%fused_computation.46 | convolution fusion | flops 3778314240 | bytes 13769216 | tf_op jit(solution)/shard_map/pd,tde->tpe/dot_general | solution.py:70
  105.1 5.9 all-to-all-start
  111.7 94.0 %all-gather.8.cloned.1.call-done = bf16[1,6144,1280]{2,1,0:T(8,128)(2,1)} async-done(((bf16[1,384,1280]{2,1,0:T(8,128)(2,1)}), bf16[1,6144,1280]{2,1,0:T(8,128)(2,1)}) %all-gather.8.cloned.1.call-update) | async-done | bytes 15728656 | tf_op jit(solution)/shard_map/all_gather | solution.py:84
  205.7 43.9 %reshape.165 = bf16[12,512,16,80]{3,2,1,0:T(8,128)(2,1)} reshape(bf16[1,6144,1280]{2,1,0:T(8,128)(2,1)} %all-gather.8.cloned.1.call-done) | data formatting | bytes 31457280 | tf_op jit(solution)/shard_map/reshape | solution.py:89
  249.6 29.5 %copy.50 = bf16[12,512,16,80]{1,3,2,0:T(8,128)(2,1)} copy(bf16[12,512,16,80]{3,2,1,0:T(8,128)(2,1)} %reshape.165) | data formatting | bytes 31457280
  279.1 31.4 %all-gather.10.cloned.1.call-done = bf16[1,6144,1280]{2,1,0:T(8,128)(2,1)} async-done(((bf16[1,384,1280]{2,1,0:T(8,128)(2,1)}), bf16[1,6144,1280]{2,1,0:T(8,128)(2,1)}) %all-gather.10.cloned.1.call-update) | async-done | bytes 15728656 | tf_op jit(solution)/shard_map/all_gather | solution.py:85
  310.4 43.8 %reshape.166 = bf16[12,512,16,80]{3,2,1,0:T(8,128)(2,1)} reshape(bf16[1,6144,1280]{2,1,0:T(8,128)(2,1)} %all-gather.10.cloned.1.call-done) | data formatting | bytes 31457280 | tf_op jit(solution)/shard_map/reshape | solution.py:90
  354.2 29.4 %copy.51 = bf16[12,512,16,80]{1,3,2,0:T(8,128)(2,1)} copy(bf16[12,512,16,80]{3,2,1,0:T(8,128)(2,1)} %reshape.166) | data formatting | bytes 31457280
  383.6 301.6 %while.15 = (s32[]{:T(128)}, f32[16,384]{1,0:T(8,128)S(1)}, f32[16,384]{1,0:T(8,128)S(1)}, f32[384,16,80]{0,2,1:T(8,128)}, s32[12]{0:T(128)S(1)}, /*index=5*/s32...) while((s32[]{:T(128)}, f32[16,384]{1,0:T(8,128)S(1)}, ...), condition=%wide.region_9.10_spmd.clone, body=%wide.region_6.9_spmd.clone.sunk | while | flops 1049543680 | bytes 96087720 | solution.py:108
  385.4 4.7 bitcast_reduce_fusion.2
  398.4 9.8 %fusion.92 = f32[384,16,80]{0,2,1:T(8,128)} fusion(f32[384,16,80]{0,2,1:T(8,128)} %get-tuple-element.242, f32[16,512,384]{2,1,0:T(8,128)} %copy-done.2, f32[16,384]{1,0:T(8,128)S(1)} %get-tuple-element.222, pred[512]{0:T(512)(128)(4,1)S(1)} %add_compare_fusion.2, bf16[12,512,16,80]{1,3,2,0:T(8,128)(2,1)} %get-tuple-element.258, ...), kind=kOutput, calls=%fused_computation.14.clone.1 | convolution fusion | flops 521011200 | bytes 17901056 | tf_op jit(solution)/shard_map/while/body/eval_jaxpr/hqk,khd->qhd/dot_general | solution.py:37
  410.0 4.7 bitcast_reduce_fusion.2
  423.0 10.3 %fusion.92 = f32[384,16,80]{0,2,1:T(8,128)} fusion(f32[384,16,80]{0,2,1:T(8,128)} %get-tuple-element.242, f32[16,512,384]{2,1,0:T(8,128)} %copy-done.2, f32[16,384]{1,0:T(8,128)S(1)} %get-tuple-element.222, pred[512]{0:T(512)(128)(4,1)S(1)} %add_compare_fusion.2, bf16[12,512,16,80]{1,3,2,0:T(8,128)(2,1)} %get-tuple-element.258, ...), kind=kOutput, calls=%fused_computation.14.clone.1 | convolution fusion | flops 521011200 | bytes 17901056 | tf_op jit(solution)/shard_map/while/body/eval_jaxpr/hqk,khd->qhd/dot_general | solution.py:37
  448.2 10.3 %fusion.92 = f32[384,16,80]{0,2,1:T(8,128)} fusion(f32[384,16,80]{0,2,1:T(8,128)} %get-tuple-element.242, f32[16,512,384]{2,1,0:T(8,128)} %copy-done.2, f32[16,384]{1,0:T(8,128)S(1)} %get-tuple-element.222, pred[512]{0:T(512)(128)(4,1)S(1)} %add_compare_fusion.2, bf16[12,512,16,80]{1,3,2,0:T(8,128)(2,1)} %get-tuple-element.258, ...), kind=kOutput, calls=%fused_computation.14.clone.1 | convolution fusion | flops 521011200 | bytes 17901056 | tf_op jit(solution)/shard_map/while/body/eval_jaxpr/hqk,khd->qhd/dot_general | solution.py:37
  473.3 10.3 %fusion.92 = f32[384,16,80]{0,2,1:T(8,128)} fusion(f32[384,16,80]{0,2,1:T(8,128)} %get-tuple-element.242, f32[16,512,384]{2,1,0:T(8,128)} %copy-done.2, f32[16,384]{1,0:T(8,128)S(1)} %get-tuple-element.222, pred[512]{0:T(512)(128)(4,1)S(1)} %add_compare_fusion.2, bf16[12,512,16,80]{1,3,2,0:T(8,128)(2,1)} %get-tuple-element.258, ...), kind=kOutput, calls=%fused_computation.14.clone.1 | convolution fusion | flops 521011200 | bytes 17901056 | tf_op jit(solution)/shard_map/while/body/eval_jaxpr/hqk,khd->qhd/dot_general | solution.py:37
  485.5 4.7 bitcast_reduce_fusion.2
  498.5 10.3 %fusion.92 = f32[384,16,80]{0,2,1:T(8,128)} fusion(f32[384,16,80]{0,2,1:T(8,128)} %get-tuple-element.242, f32[16,512,384]{2,1,0:T(8,128)} %copy-done.2, f32[16,384]{1,0:T(8,128)S(1)} %get-tuple-element.222, pred[512]{0:T(512)(128)(4,1)S(1)} %add_compare_fusion.2, bf16[12,512,16,80]{1,3,2,0:T(8,128)(2,1)} %get-tuple-element.258, ...), kind=kOutput, calls=%fused_computation.14.clone.1 | convolution fusion | flops 521011200 | bytes 17901056 | tf_op jit(solution)/shard_map/while/body/eval_jaxpr/hqk,khd->qhd/dot_general | solution.py:37
  523.7 10.3 %fusion.92 = f32[384,16,80]{0,2,1:T(8,128)} fusion(f32[384,16,80]{0,2,1:T(8,128)} %get-tuple-element.242, f32[16,512,384]{2,1,0:T(8,128)} %copy-done.2, f32[16,384]{1,0:T(8,128)S(1)} %get-tuple-element.222, pred[512]{0:T(512)(128)(4,1)S(1)} %add_compare_fusion.2, bf16[12,512,16,80]{1,3,2,0:T(8,128)(2,1)} %get-tuple-element.258, ...), kind=kOutput, calls=%fused_computation.14.clone.1 | convolution fusion | flops 521011200 | bytes 17901056 | tf_op jit(solution)/shard_map/while/body/eval_jaxpr/hqk,khd->qhd/dot_general | solution.py:37
  548.8 10.3 %fusion.92 = f32[384,16,80]{0,2,1:T(8,128)} fusion(f32[384,16,80]{0,2,1:T(8,128)} %get-tuple-element.242, f32[16,512,384]{2,1,0:T(8,128)} %copy-done.2, f32[16,384]{1,0:T(8,128)S(1)} %get-tuple-element.222, pred[512]{0:T(512)(128)(4,1)S(1)} %add_compare_fusion.2, bf16[12,512,16,80]{1,3,2,0:T(8,128)(2,1)} %get-tuple-element.258, ...), kind=kOutput, calls=%fused_computation.14.clone.1 | convolution fusion | flops 521011200 | bytes 17901056 | tf_op jit(solution)/shard_map/while/body/eval_jaxpr/hqk,khd->qhd/dot_general | solution.py:37
  561.0 4.7 bitcast_reduce_fusion.2
  574.0 10.3 %fusion.92 = f32[384,16,80]{0,2,1:T(8,128)} fusion(f32[384,16,80]{0,2,1:T(8,128)} %get-tuple-element.242, f32[16,512,384]{2,1,0:T(8,128)} %copy-done.2, f32[16,384]{1,0:T(8,128)S(1)} %get-tuple-element.222, pred[512]{0:T(512)(128)(4,1)S(1)} %add_compare_fusion.2, bf16[12,512,16,80]{1,3,2,0:T(8,128)(2,1)} %get-tuple-element.258, ...), kind=kOutput, calls=%fused_computation.14.clone.1 | convolution fusion | flops 521011200 | bytes 17901056 | tf_op jit(solution)/shard_map/while/body/eval_jaxpr/hqk,khd->qhd/dot_general | solution.py:37
  599.1 10.3 %fusion.92 = f32[384,16,80]{0,2,1:T(8,128)} fusion(f32[384,16,80]{0,2,1:T(8,128)} %get-tuple-element.242, f32[16,512,384]{2,1,0:T(8,128)} %copy-done.2, f32[16,384]{1,0:T(8,128)S(1)} %get-tuple-element.222, pred[512]{0:T(512)(128)(4,1)S(1)} %add_compare_fusion.2, bf16[12,512,16,80]{1,3,2,0:T(8,128)(2,1)} %get-tuple-element.258, ...), kind=kOutput, calls=%fused_computation.14.clone.1 | convolution fusion | flops 521011200 | bytes 17901056 | tf_op jit(solution)/shard_map/while/body/eval_jaxpr/hqk,khd->qhd/dot_general | solution.py:37
  624.3 10.3 %fusion.92 = f32[384,16,80]{0,2,1:T(8,128)} fusion(f32[384,16,80]{0,2,1:T(8,128)} %get-tuple-element.242, f32[16,512,384]{2,1,0:T(8,128)} %copy-done.2, f32[16,384]{1,0:T(8,128)S(1)} %get-tuple-element.222, pred[512]{0:T(512)(128)(4,1)S(1)} %add_compare_fusion.2, bf16[12,512,16,80]{1,3,2,0:T(8,128)(2,1)} %get-tuple-element.258, ...), kind=kOutput, calls=%fused_computation.14.clone.1 | convolution fusion | flops 521011200 | bytes 17901056 | tf_op jit(solution)/shard_map/while/body/eval_jaxpr/hqk,khd->qhd/dot_general | solution.py:37
  649.5 10.3 %fusion.92 = f32[384,16,80]{0,2,1:T(8,128)} fusion(f32[384,16,80]{0,2,1:T(8,128)} %get-tuple-element.242, f32[16,512,384]{2,1,0:T(8,128)} %copy-done.2, f32[16,384]{1,0:T(8,128)S(1)} %get-tuple-element.222, pred[512]{0:T(512)(128)(4,1)S(1)} %add_compare_fusion.2, bf16[12,512,16,80]{1,3,2,0:T(8,128)(2,1)} %get-tuple-element.258, ...), kind=kOutput, calls=%fused_computation.14.clone.1 | convolution fusion | flops 521011200 | bytes 17901056 | tf_op jit(solution)/shard_map/while/body/eval_jaxpr/hqk,khd->qhd/dot_general | solution.py:37
  674.6 10.3 %fusion.92 = f32[384,16,80]{0,2,1:T(8,128)} fusion(f32[384,16,80]{0,2,1:T(8,128)} %get-tuple-element.242, f32[16,512,384]{2,1,0:T(8,128)} %copy-done.2, f32[16,384]{1,0:T(8,128)S(1)} %get-tuple-element.222, pred[512]{0:T(512)(128)(4,1)S(1)} %add_compare_fusion.2, bf16[12,512,16,80]{1,3,2,0:T(8,128)(2,1)} %get-tuple-element.258, ...), kind=kOutput, calls=%fused_computation.14.clone.1 | convolution fusion | flops 521011200 | bytes 17901056 | tf_op jit(solution)/shard_map/while/body/eval_jaxpr/hqk,khd->qhd/dot_general | solution.py:37
  698.4 5.9 all-to-all-start.1
  706.0 33.9 %all-to-all-done.1 = bf16[128,2,5120]{2,1,0:T(2,128)(2,1)} async-done(((bf16[128,2,5120]{2,1,0:T(2,128)(2,1)}), bf16[128,2,5120]{2,1,0:T(2,128)(2,1)}, u32[]{:S(2)}, u32[]{:S(2)}) %all-to-all-start.1) | async-done | bytes 2621472 | tf_op jit(solution)/shard_map/all_to_all | solution.py:131
  739.9 6.5 reshape.153
  746.4 6.1 scatter_custom_fusion.2
  (161 shorter events, 196.6 us)
Async XLA Ops:
  6.5 31.9 %copy-start = (bf16[1280,1280]{1,0:T(8,128)(2,1)S(1)}, bf16[1280,1280]{1,0:T(8,128)(2,1)}, u32[]{:S(2)}) copy-start(bf16[1280,1280]{1,0:T(8,128)(2,1)} %param.18) | copy-start | bytes 9830404
  6.5 86.3 %all-gather.6.cloned.1.call-start = ((), (), s32[]{:S(2)}) async-start(), calls=%async_computation.2 | async-start | bytes 10444800 | tf_op jit(solution)/shard_map/all_gather | solution.py:73
  7.3 198.5 %all-gather.8.cloned.1.call-start = ((), (), s32[]{:S(2)}) async-start(), calls=%async_computation.3 | async-start | bytes 16711680 | tf_op jit(solution)/shard_map/all_gather | solution.py:84
  19.6 7.0 copy-start.4
  19.6 7.0 copy-start.6
  34.7 3.8 copy-start.3
  101.0 2.3 copy-start.7
  101.0 10.0 %copy-start.5 = (bf16[1280]{0:T(1024)(128)(2,1)S(1)}, bf16[1280]{0:T(1024)(128)(2,1)}, u32[]{:S(2)}) copy-start(bf16[1280]{0:T(1024)(128)(2,1)} %param.22) | copy-start | bytes 7684
  102.5 207.9 %all-gather.10.cloned.1.call-start = ((), (), s32[]{:S(2)}) async-start(), calls=%async_computation.4 | async-start | bytes 16711680 | tf_op jit(solution)/shard_map/all_gather | solution.py:85
  105.1 593.3 %all-to-all-start = ((s32[128,1,2]{2,1,0:T(1,128)}), s32[128,1,2]{2,1,0:T(1,128)S(1)}, u32[]{:S(2)}, u32[]{:S(2)}) async-start(s32[128,1,2]{2,1,0:T(1,128)} %bitcast), calls=%async_computation | async-start | bytes 131072 | tf_op jit(solution)/shard_map/all_to_all | solution.py:138
  390.1 4.6 copy-start.2
  414.8 4.6 copy-start.2
  439.9 4.6 copy-start.2
  465.1 4.6 copy-start.2
  490.2 4.6 copy-start.2
  515.4 4.6 copy-start.2
  540.5 4.6 copy-start.2
  565.7 4.6 copy-start.2
  590.9 4.6 copy-start.2
  616.0 4.6 copy-start.2
  641.2 4.6 copy-start.2
  666.3 4.6 copy-start.2
  698.4 41.4 %all-to-all-start.1 = ((bf16[128,2,5120]{2,1,0:T(2,128)(2,1)}), bf16[128,2,5120]{2,1,0:T(2,128)(2,1)}, u32[]{:S(2)}, u32[]{:S(2)}) async-start(bf16[128,2,5120]{2,1,0:T(2,128)(2,1)} %reshape.130), calls=%async_computation.1 | async-start | bytes 5242880 | tf_op jit(solution)/shard_map/all_to_all | solution.py:131
  704.9 47.6 %copy-start.1 = (bf16[1280,1280]{1,0:T(8,128)(2,1)S(1)}, bf16[1280,1280]{1,0:T(8,128)(2,1)}, u32[]{:S(2)}) copy-start(bf16[1280,1280]{1,0:T(8,128)(2,1)} %param.18) | copy-start | bytes 9830404
Sparse Core Ops, SparseCore 0:
  9.9 82.8 all-gather.5
  102.7 103.0 all-gather.7
  208.2 102.1 all-gather.9
where the time goes:
time: 767 us; the launch traced here: 759 us
  local copies, waits for them, and re-layouts  242 us (32%)
  matrix products  214 us (28%)
  waiting for transfers between devices  212 us (28%)
  other arithmetic  64.9 us (8%)
  between operations  13.8 us (2%)
  starting transfers between devices  11.8 us (2%)
    dot_general x13, matrix products, attend_block(): jnp.einsum('hqk,khd->qhd', weights.astype(jnp.bfloat16), value_heads, pre...  127 us
    all_gather x1, waiting for transfers between devices, on_device(): key_part = lax.all_gather(projected[1], 'img', axis=0, tiled=True)  94 us
    unnamed x16, local copies, waits for them, and re-layouts  58.9 us
    dot_general x12, matrix products, attend_block(): jnp.einsum('qhd,khd->hqk', query_heads, key_heads, preferred_element_type...  56.5 us
    while x36, local copies, waits for them, and re-layouts  54.8 us
    all_gather x1, waiting for transfers between devices, on_device(): lax.all_gather(w_qkv2, 'img', axis=2, tiled=True)  51.8 us
    reshape x1, local copies, waits for them, and re-layouts, on_device(): key_blocks = key_part.reshape(step_count, block_rows, head_count, HEAD_DIM)  43.9 us
    reshape x1, local copies, waits for them, and re-layouts, on_device(): value_part.reshape(step_count, block_rows, head_count, HEAD_DIM)  43.8 us
  transfers between devices with their start and end apart: 5, of which 4 were waited for; matrix products, arithmetic and copies ran while one was open for 58% of the time, Pallas kernels for 0%

commit v1 on v0

v1 whole, which is shorter than its diff:
```python
import functools
import math

import jax
import jax.numpy as jnp
from jax import lax
from jax.experimental import pallas as pl
from jax.experimental.pallas import tpu as pltpu
from jax.sharding import PartitionSpec as P

HEAD_DIM = 80
D = 1280
EPSILON = 1e-06
MASKED_SCORE = -1e30
F32 = jnp.float32
BF16 = jnp.bfloat16
Q_SCALE = HEAD_DIM ** (-0.5) * math.log2(math.e)
SAFE_BOUND = 64.0
SAFE_VALUE = 2.0**40
VMEM_LIMIT = 56 * 1024 * 1024
NT = (((1,), (1,)), ((), ()))
TN = (((0,), (0,)), ((), ()))


def normed(values, gain):
    values = values.astype(F32)
    return (
        values
        * lax.rsqrt(jnp.mean(values * values, axis=-1, keepdims=True) + EPSILON)
        * gain.astype(F32)
    )


def split_heads(row_block):
    return row_block.reshape(row_block.shape[0], -1, HEAD_DIM)


def attend_block(query_heads, key_heads, value_heads, allowed):
    scores = jnp.einsum(
        "qhd,khd->hqk", query_heads, key_heads, preferred_element_type=F32
    ) * HEAD_DIM ** (-0.5)
    scores = jnp.where(allowed[None], scores, MASKED_SCORE)
    maxima = jnp.max(scores, axis=-1)
    weights = jnp.where(allowed[None], jnp.exp(scores - maxima[:, :, None]), 0.0)
    totals = jnp.sum(weights, axis=-1)
    summed = jnp.einsum(
        "hqk,khd->qhd", weights.astype(BF16), value_heads, preferred_element_type=F32
    )
    return (maxima, totals, summed)


def finish(totals, summed):
    return (summed / totals.T[:, :, None]).astype(BF16).reshape(summed.shape[0], -1)


def whole(count):
    return [pl.BlockSpec(memory_space=pltpu.VMEM)] * count


def device_perm(move):
    pairs = []
    for i in range(128):
        c, g = divmod(i, 16)
        x_lo, y = divmod(c, 4)
        x_hi, r = divmod(g, 8)
        z, core = divmod(r, 2)
        x2, y2, z2, core2 = move(x_hi * 2 + x_lo, y, z, core)
        x2, y2, z2 = x2 % 4, y2 % 4, z2 % 4
        pairs.append((i, ((x2 % 2) * 4 + y2) * 16 + ((x2 // 2) * 4 + z2) * 2 + core2))
    return pairs


OTHER_X = {0: 3, 3: 0, 1: 2, 2: 1}
Z_UP = device_perm(lambda x, y, z, core: (x, y, z + 1, core))
Z_DOWN = device_perm(lambda x, y, z, core: (x, y, z - 1, core))
X_OTHER = device_perm(lambda x, y, z, core: (OTHER_X[x], y, z, core))
CORE_SWAP = device_perm(lambda x, y, z, core: (x, y, z, 1 - core))
BOTH = ("ctx", "img")
SHARD_OFFSETS = ((0, 0), (0, -1), (0, 1), (1, 0), (1, -1), (1, 1), (0, -2), (1, -2))


def gather_parity(shard):
    below = lax.ppermute(shard, BOTH, Z_UP)
    above = lax.ppermute(shard, BOTH, Z_DOWN)
    other = lax.ppermute(shard, BOTH, X_OTHER)
    other_below = lax.ppermute(other, BOTH, Z_UP)
    other_above = lax.ppermute(other, BOTH, Z_DOWN)
    far = lax.ppermute(below, BOTH, Z_UP)
    other_far = lax.ppermute(far, BOTH, X_OTHER)
    return [shard, below, above, other, other_below, other_above, far, other_far]


def project_kernel(order_ref, h_even_ref, h_odd_ref, *refs):
    out_ref = refs[8]
    rows = h_even_ref.shape[0]
    part = lax.broadcasted_iota(jnp.int32, (3 * HEAD_DIM, 1), 0)
    scale = jnp.where(part < HEAD_DIM, Q_SCALE, 1.0).astype(F32)
    for n in range(8):
        weights = refs[n][...]
        target = order_ref[n]
        for half, h_ref in enumerate((h_even_ref, h_odd_ref)):
            product = lax.dot_general(weights, h_ref[...], NT, preferred_element_type=F32)
            out_ref[target, :, half * rows : (half + 1) * rows] = (product * scale).astype(BF16)


def project(order, h_even, h_odd, shards):
    rows = h_even.shape[0]
    return pl.pallas_call(
        project_kernel,
        out_shape=jax.ShapeDtypeStruct((8, 3 * HEAD_DIM, 2 * rows), BF16),
        in_specs=[pl.BlockSpec(memory_space=pltpu.SMEM)] + whole(10),
        out_specs=pl.BlockSpec(memory_space=pltpu.VMEM),
        compiler_params=pltpu.CompilerParams(vmem_limit_bytes=VMEM_LIMIT),
    )(order, h_even, h_odd, *shards)


def attention_kernel(count_ref, q_ref, all_ref, out_ref, k_ref, v_ref, bound_ref, *, block):
    chips, features, rows = all_ref.shape
    total = chips * rows
    depth = HEAD_DIM

    @pl.when(pl.program_id(0) == 0)
    def _():
        count = count_ref[0]
        key_zero = all_ref[0, depth : 2 * depth, 0:1].astype(F32)
        q_most = jnp.zeros((1, rows), F32)
        k_most = jnp.zeros((1, rows), F32)
        v_most = jnp.zeros((HEAD_DIM, rows), F32)
        for chip in range(chips):
            position = chip * rows + lax.broadcasted_iota(jnp.int32, (1, rows), 1)
            valid = position < count
            keys = jnp.where(valid, all_ref[chip, depth : 2 * depth, :].astype(F32), key_zero)
            values = jnp.where(valid, all_ref[chip, 2 * depth :, :].astype(F32), 0.0)
            queries = all_ref[chip, 0:depth, :].astype(F32)
            q_most = jnp.maximum(q_most, jnp.sum(queries * queries, axis=0, keepdims=True))
            k_most = jnp.maximum(k_most, jnp.sum(keys * keys, axis=0, keepdims=True))
            v_most = jnp.maximum(v_most, jnp.abs(values))
            keys = jnp.concatenate([keys, jnp.zeros((128 - depth, rows), F32)], axis=0)
            k_ref[chip * rows : (chip + 1) * rows, :] = keys.astype(BF16).T
            v_ref[0:depth, chip * rows : (chip + 1) * rows] = values.astype(BF16)
            v_ref[depth:, chip * rows : (chip + 1) * rows] = jnp.where(
                (lax.broadcasted_iota(jnp.int32, (16, rows), 0) == 0) & valid, 1.0, 0.0
            ).astype(BF16)
        bound_ref[0] = jnp.max(q_most) * jnp.max(k_most)
        bound_ref[1] = jnp.max(v_most)

    queries = q_ref[0, 0:depth, :]
    queries = jnp.concatenate([queries, jnp.zeros((128 - depth, rows), BF16)], axis=0)
    small = (bound_ref[0] < SAFE_BOUND * SAFE_BOUND) & (bound_ref[1] < SAFE_VALUE)

    def store(acc):
        result = acc[0:depth] / acc[depth : depth + 1]
        half = rows // 2
        out_ref[0] = result[:, 0:half].astype(BF16)
        out_ref[1] = result[:, half:].astype(BF16)

    @pl.when(small)
    def _():
        acc = None
        for start in range(0, total, block):
            scores = jnp.dot(k_ref[start : start + block, :], queries, preferred_element_type=F32)
            weights = jnp.exp2(scores).astype(BF16)
            part = jnp.dot(v_ref[:, start : start + block], weights, preferred_element_type=F32)
            acc = part if acc is None else acc + part
        store(acc)

    @pl.when(jnp.logical_not(small))
    def _():
        def step(index, carried):
            most, acc = carried
            start = pl.multiple_of(index * block, block)
            scores = jnp.dot(
                k_ref[pl.ds(start, block), :], queries, preferred_element_type=F32
            )
            new_most = jnp.maximum(most, jnp.max(scores, axis=0, keepdims=True))
            weights = jnp.exp2(scores - new_most).astype(BF16)
            part = jnp.dot(
                v_ref[:, pl.ds(start, block)], weights, preferred_element_type=F32
            )
            return new_most, acc * jnp.exp2(most - new_most) + part

        start_state = (
            jnp.full((1, rows), MASKED_SCORE, F32),
            jnp.zeros((depth + 16, rows), F32),
        )
        store(lax.fori_loop(0, total // block, step, start_state)[1])


def attend_full(count, received):
    chips, features, rows = received.shape
    total = chips * rows
    return pl.pallas_call(
        functools.partial(attention_kernel, block=512),
        out_shape=jax.ShapeDtypeStruct((2 * chips, HEAD_DIM, rows // 2), BF16),
        grid=(chips,),
        in_specs=[
            pl.BlockSpec(memory_space=pltpu.SMEM),
            pl.BlockSpec((1, features, rows), lambda i: (i, 0, 0)),
            pl.BlockSpec(memory_space=pltpu.VMEM),
        ],
        out_specs=pl.BlockSpec((2, HEAD_DIM, rows // 2), lambda i: (i, 0, 0)),
        scratch_shapes=[
            pltpu.VMEM((total, 128), BF16),
            pltpu.VMEM((HEAD_DIM + 16, total), BF16),
            pltpu.SMEM((2,), F32),
        ],
        compiler_params=pltpu.CompilerParams(vmem_limit_bytes=VMEM_LIMIT),
    )(count, received, received)


def merge_kernel(bucket_ref, a_ref, x_ref, w_ref, gain_ref, out_ref):
    attended = a_ref[...]
    third = x_ref[...].astype(F32) + lax.dot_general(
        attended, w_ref[...], TN, preferred_element_type=F32
    )
    merged = normed(third, gain_ref[...]).astype(BF16)
    places, patches = out_ref.shape[0], merged.shape[0]
    chosen = lax.broadcasted_iota(jnp.int32, (places, patches), 0) == bucket_ref[...]
    out_ref[...] = jnp.dot(
        chosen.astype(BF16), merged, preferred_element_type=F32
    ).astype(BF16)


def merge(bucket, attended, second, w_out, gain, places):
    return pl.pallas_call(
        merge_kernel,
        out_shape=jax.ShapeDtypeStruct((places, D), BF16),
        in_specs=whole(5),
        out_specs=pl.BlockSpec(memory_space=pltpu.VMEM),
        compiler_params=pltpu.CompilerParams(vmem_limit_bytes=VMEM_LIMIT),
    )(bucket, attended, second, w_out, gain)


def place_kernel(target_ref, got_ref, out_ref):
    rows = out_ref.shape[0]
    got = got_ref[...]
    row = 4 * lax.broadcasted_iota(jnp.int32, (rows, got.shape[0]), 0)
    for j in range(4):
        chosen = (row + j) == target_ref[...]
        out_ref[:, j * D : (j + 1) * D] = jnp.dot(
            chosen.astype(BF16), got, preferred_element_type=F32
        ).astype(BF16)


def place(target, got, rows):
    return pl.pallas_call(
        place_kernel,
        out_shape=jax.ShapeDtypeStruct((rows, 4 * D), BF16),
        in_specs=whole(2),
        out_specs=pl.BlockSpec(memory_space=pltpu.VMEM),
        compiler_params=pltpu.CompilerParams(vmem_limit_bytes=VMEM_LIMIT),
    )(target, got)


def on_device(
    patches, window_ids, counts, gain_one, w_qkv1, w_out1, gain_two, w_qkv2, w_out2, gain_out, slots
):
    me = lax.axis_index("img")
    my_x, my_z, my_core = me // 8, (me // 2) % 4, me % 2
    shard = jnp.swapaxes(w_qkv2, 1, 2).reshape(3 * HEAD_DIM, D)
    shards = gather_parity(shard)
    order = jnp.stack([((my_x + dx) % 2) * 4 + (my_z + dz) % 4 for dx, dz in SHARD_OFFSETS])

    merged_rows = slots.shape[0]
    device_count = 128
    capacity = 2
    owner = slots // merged_rows
    local_slot = slots % merged_rows
    row_order = jnp.arange(merged_rows, dtype=jnp.int32)
    earlier = (owner[:, None] == owner[None, :]) & (row_order[None, :] < row_order[:, None])
    bucket = owner * capacity + jnp.sum(earlier.astype(jnp.int32), axis=1)
    quarter = jnp.arange(4, dtype=jnp.int32)
    bucket_rows = (4 * bucket[:, None] + quarter[None, :]).reshape(1, 4 * merged_rows)
    hits = bucket[:, None] == jnp.arange(device_count * capacity, dtype=jnp.int32)[None, :]
    send_slots = jnp.sum(jnp.where(hits, local_slot[:, None] + 1, 0), axis=0) - 1
    got_slots = lax.all_to_all(
        send_slots.reshape(device_count, capacity), BOTH, split_axis=0, concat_axis=0, tiled=True
    )
    target_rows = (4 * got_slots.reshape(-1)[:, None] + quarter[None, :]).reshape(1, -1)

    first = patches[0].astype(F32)
    hidden = normed(first, gain_one).astype(BF16)
    projected = jnp.einsum("pd,tde->tpe", hidden, w_qkv1, preferred_element_type=F32).astype(BF16)
    local_ids = window_ids[0]
    allowed = local_ids[:, None] == local_ids[None, :]
    maxima, totals, summed = attend_block(
        split_heads(projected[0]), split_heads(projected[1]), split_heads(projected[2]), allowed
    )
    attended = finish(totals, summed)
    second = (first + jnp.dot(attended, w_out1, preferred_element_type=F32)).astype(BF16)
    hidden = normed(second, gain_two).astype(BF16)

    partner = lax.ppermute(hidden, BOTH, CORE_SWAP)
    even = my_core == 0
    projected = project(
        order, jnp.where(even, hidden, partner), jnp.where(even, partner, hidden), shards
    )
    groups = [[2 * chip + core for chip in range(8)] for core in range(2)]
    received = lax.all_to_all(
        projected, "img", split_axis=0, concat_axis=0, tiled=True, axis_index_groups=groups
    )
    attended = attend_full(counts, received)
    attended = lax.all_to_all(attended, "img", split_axis=0, concat_axis=0, tiled=True)
    send = merge(
        bucket_rows,
        attended.reshape(D, -1),
        second,
        w_out2,
        gain_out.reshape(1, D),
        device_count * capacity * 4,
    )
    got = lax.all_to_all(
        send.reshape(device_count, capacity * 4, D), BOTH, split_axis=0, concat_axis=0, tiled=True
    )
    return place(target_rows, got.reshape(-1, D), merged_rows)


def solution(mesh):
    return jax.shard_map(
        on_device,
        mesh=mesh,
        in_specs=(
            P("ctx", "img", None),
            P("ctx", "img"),
            P("ctx"),
            P(),
            P(),
            P(),
            P(),
            P(None, None, "img"),
            P(),
            P(),
            P(("ctx", "img")),
        ),
        out_specs=P(("ctx", "img"), None),
        check_vma=False,
    )
```

time: 767 us -> 282 us (0.37)
  local copies, waits for them, and re-layouts: 242 us -> 13 us
  matrix products: 214 us -> 21.4 us
  waiting for transfers between devices: 212 us -> 106 us
  Pallas kernels: 0 us -> 91.4 us
  other arithmetic: 64.9 us -> 7.55 us
  starting transfers between devices: 11.8 us -> 41 us
  between operations: 13.8 us -> 0.83 us
    dot_general x29 -> x3, matrix products: 206 us -> 13.6 us  [the longest x1 8.21 us: on_device(): jnp.einsum('pd,tde->tpe', hidden, w_qkv1, preferred_element_type=F32)]
    all_gather x3 -> x0, waiting for transfers between devices: 177 us -> none  [the longest x1 94 us: on_device(): key_part = lax.all_gather(projected[1], 'img', axis=0, tiled=True)]
    reshape x6 -> x1, local copies, waits for them, and re-layouts: 98.3 us -> 0.6 us  [on_device(): gain_out.reshape(1, D)]
    pallas_call x0 -> x4, Pallas kernels: none -> 91.4 us  [the longest x1 69.4 us: attend_full(): pl.pallas_call(functools.partial(attention_kernel, block=512), out_shape=...]
    unnamed x16 -> x14, local copies, waits for them, and re-layouts: 58.9 us -> 0.97 us
    while x36 -> x0, local copies, waits for them, and re-layouts: 54.8 us -> none
    all_to_all x2 -> x4, waiting for transfers between devices: 33.9 us -> 85.2 us  [the longest x1 34.6 us: on_device(): lax.all_to_all(projected, 'img', split_axis=0, concat_axis=0, tiled=True,...]
    reduce_sum x13 -> x2, other arithmetic: 43.7 us -> 0.28 us  [the longest x1 0.17 us: on_device(): bucket = owner * capacity + jnp.sum(earlier.astype(jnp.int32), axis=1)]
  transfers between devices with their start and end apart: 5 -> 12, of which waited for: 4 -> 8; matrix products, arithmetic and copies ran while one was open for 58% -> 15% of each run, Pallas kernels for 0% -> 3%
where the time goes in v1:
time: 282 us; the launch traced here: 281 us
  waiting for transfers between devices  106 us (38%)
  Pallas kernels  91.4 us (32%)
  starting transfers between devices  41 us (15%)
  matrix products  21.4 us (8%)
  local copies, waits for them, and re-layouts  13 us (5%)
  other arithmetic  7.55 us (3%)
    pallas_call x1, Pallas kernels, attend_full(): pl.pallas_call(functools.partial(attention_kernel, block=512), out_shape=...  69.4 us
    all_to_all x1, waiting for transfers between devices, on_device(): lax.all_to_all(projected, 'img', split_axis=0, concat_axis=0, tiled=True,...  34.6 us
    all_to_all x1, waiting for transfers between devices, on_device(): lax.all_to_all(send.reshape(device_count, capacity * 4, D), BOTH, split_a...  34.4 us
    all_to_all x1, waiting for transfers between devices, on_device(): lax.all_to_all(attended, 'img', split_axis=0, concat_axis=0, tiled=True)  15.5 us
    ppermute x1, waiting for transfers between devices, gather_parity(): other = lax.ppermute(shard, BOTH, X_OTHER)  11.9 us
    pallas_call x1, Pallas kernels, project(): pl.pallas_call(project_kernel, out_shape=jax.ShapeDtypeStruct((8, 3 * HEA...  9.98 us
    all_to_all x1, starting transfers between devices, on_device(): lax.all_to_all(send.reshape(device_count, capacity * 4, D), BOTH, split_a...  9.46 us
    dot_general x1, matrix products, on_device(): jnp.einsum('pd,tde->tpe', hidden, w_qkv1, preferred_element_type=F32)  8.21 us
  transfers between devices with their start and end apart: 12, of which 8 were waited for; matrix products, arithmetic and copies ran while one was open for 15% of the time, Pallas kernels for 3%

profile of v1, /device:TPU:1, one launch (start us, length us, event | category | flops | bytes accessed | tf_op | source)
XLA Modules:
  0.0 281.2 jit_solution(6998784449547219287)
XLA Ops:
  0.0 2.5 collective-permute-start.1
  3.2 1.5 fusion.12
  4.6 8.2 %fusion.7 = bf16[3,384,1280]{2,1,0:T(8,128)(2,1)S(1)} fusion(bf16[3,1280,1280]{2,1,0:T(8,128)(2,1)} %param.15, bf16[1,384,1280]{2,1,0:T(8,128)(2,1)} %param.11, f32[1280]{0:T(1024)S(1)} %convert_element_type.42, f32[384]{0:T(512)S(1)} %add_rsqrt_fusion.1), kind=kOutput, calls=%fused_computation.10 | convolution fusion | flops 3778314240 | bytes 13769216 | tf_op jit(solution)/shard_map/pd,tde->tpe/dot_general | solution.py:283
  12.9 1.7 fusion.29
  14.5 2.3 copy.27
  16.8 2.2 copy.28
  19.2 2.2 copy.26
  21.5 7.8 %fusion.30 = (f32[16,384]{1,0:T(8,128)S(1)}, bf16[16,384,384]{1,2,0:T(8,128)(2,1)}) fusion(pred[384,384]{0,1:T(8,128)(4,1)S(1)} %broadcast_compare_fusion, bf16[384,16,80]{0,2,1:T(8,128)(2,1)} %bitcast.47, bf16[384,16,80]{0,2,1:T(8,128)(2,1)} %bitcast.48), kind=kOutput, calls=%fused_computation.52 | convolution fusion | flops 391643520 | bytes 6856704 | tf_op jit(solution)/shard_map/sub | solution.py:44
  29.3 3.7 %fusion.15 = bf16[384,16,80]{0,2,1:T(8,128)(2,1)S(1)} fusion(bf16[384,16,80]{0,2,1:T(8,128)(2,1)} %bitcast.49, bf16[16,384,384]{1,2,0:T(8,128)(2,1)} %get-tuple-element.15, f32[384,16]{0,1:T(8,128)S(1)} %bitcast.51), kind=kOutput, calls=%fused_computation.24 | convolution fusion | flops 378470400 | bytes 6709248 | tf_op jit(solution)/shard_map/hqk,khd->qhd/dot_general | solution.py:46
  33.0 1.7 fusion.9
  35.7 1.2 fusion.11
  37.9 2.5 collective-permute-start.3
  40.4 1.6 collective-permute-start.6
  42.0 1.0 collective-permute-start.2
  43.0 11.9 %collective-permute-done.3.refs_3_ = bf16[240,1280]{1,0:T(8,128)(2,1)} collective-permute-done((bf16[240,1280]{1,0:T(8,128)(2,1)}, bf16[240,1280]{1,0:T(8,128)(2,1)}, u32[]{:S(2)}, u32[]{:S(2)}) %collective-permute-start.3) | collective-permute-done | bytes 614432 | tf_op jit(solution)/shard_map/ppermute | solution.py:85
  54.9 1.6 collective-permute-start.4
  56.5 1.0 collective-permute-start.5
  57.6 2.5 collective-permute-start.7
  60.7 3.3 %broadcast_select_fusion = (bf16[384,1280]{1,0:T(8,128)(2,1)}, bf16[384,1280]{1,0:T(8,128)(2,1)}) fusion(bf16[384,1280]{1,0:T(8,128)(2,1)} %collective-permute-done, pred[]{:T(512)S(6)} %eq.75, f32[1280]{0:T(1024)S(1)} %convert_element_type.50, f32[384]{0:T(512)S(1)} %add_rsqrt_fusion, bf16[384,1280]{1,0:T(8,128)(2,1)} %copy-done.1), kind=kLoop, calls=%fused_computation.29 | loop fusion | flops 2949120 | bytes 3938817 | tf_op jit(solution)/shard_map/jit(_where)/select_n | solution.py:296
  64.0 7.0 %collective-permute-done.4.refs_4_ = bf16[240,1280]{1,0:T(8,128)(2,1)} collective-permute-done((bf16[240,1280]{1,0:T(8,128)(2,1)}, bf16[240,1280]{1,0:T(8,128)(2,1)}, u32[]{:S(2)}, u32[]{:S(2)}) %collective-permute-start.4) | collective-permute-done | bytes 614432 | tf_op jit(solution)/shard_map/ppermute | solution.py:86
  71.1 2.0 collective-permute-done.7.refs_7_
  73.1 10.0 %shard_map.109 = bf16[8,240,768]{2,1,0:T(8,128)(2,1)} custom-call(s32[8]{0:T(128)} %stack.35.order_ref, bf16[384,1280]{1,0:T(8,128)(2,1)} %get-tuple-element.11.h_even_ref, bf16[384,1280]{1,0:T(8,128)(2,1)} %get-tuple-element.10.h_odd_ref, bf16[240,1280]{1,0:T(8,128)(2,1)} %bitcast.20.refs_0_, bf16[240,1280]{1,0:T(8,128)(2,1)} %collective-permute-done.1.refs_1_, ...), custom_call_target="tpu_custom_call" | custom-call | tf_op jit(solution)/shard_map/pallas_call | solution.py:108
  83.1 4.5 %all-to-all-start.1 = ((bf16[8,240,768]{2,1,0:T(8,128)(2,1)}), bf16[8,240,768]{2,1,0:T(8,128)(2,1)}, u32[]{:S(2)}, u32[]{:S(2)}) async-start(bf16[8,240,768]{2,1,0:T(8,128)(2,1)} %shard_map.109), calls=%async_computation.1 | async-start | bytes 5898240 | tf_op jit(solution)/shard_map/all_to_all | solution.py:299
  88.2 34.6 %all-to-all-done.1.q_ref.all_ref = bf16[8,240,768]{2,1,0:T(8,128)(2,1)} async-done(((bf16[8,240,768]{2,1,0:T(8,128)(2,1)}), bf16[8,240,768]{2,1,0:T(8,128)(2,1)}, u32[]{:S(2)}, u32[]{:S(2)}) %all-to-all-start.1) | async-done | bytes 2949152 | tf_op jit(solution)/shard_map/all_to_all | solution.py:299
  122.8 69.4 %shard_map.110 = bf16[16,80,384]{2,1,0:T(8,128)(2,1)} custom-call(s32[1]{0:T(128)S(6)} %copy.31.count_ref, bf16[8,240,768]{2,1,0:T(8,128)(2,1)} %all-to-all-done.1.q_ref.all_ref, bf16[8,240,768]{2,1,0:T(8,128)(2,1)} %all-to-all-done.1.q_ref.all_ref), custom_call_target="tpu_custom_call" | custom-call | tf_op jit(solution)/shard_map/pallas_call | solution.py:192
  192.2 6.0 %all-to-all-start.2 = ((bf16[16,80,384]{2,1,0:T(8,128)(2,1)}), bf16[16,80,384]{2,1,0:T(8,128)(2,1)}, u32[]{:S(2)}, u32[]{:S(2)}) async-start(bf16[16,80,384]{2,1,0:T(8,128)(2,1)} %shard_map.110), calls=%async_computation.2 | async-start | bytes 1966080 | tf_op jit(solution)/shard_map/all_to_all | solution.py:303
  199.3 15.5 %all-to-all-done.2 = bf16[16,80,384]{2,1,0:T(8,128)(2,1)} async-done(((bf16[16,80,384]{2,1,0:T(8,128)(2,1)}), bf16[16,80,384]{2,1,0:T(8,128)(2,1)}, u32[]{:S(2)}, u32[]{:S(2)}) %all-to-all-start.2) | async-done | bytes 983072 | tf_op jit(solution)/shard_map/all_to_all | solution.py:303
  214.8 7.3 %all-to-all-start = ((s32[128,1,2]{2,1,0:T(1,128)}), s32[128,1,2]{2,1,0:T(1,128)S(1)}, u32[]{:S(2)}, u32[]{:S(2)}) async-start(s32[128,1,2]{2,1,0:T(1,128)} %bitcast), calls=%async_computation | async-start | bytes 131072 | tf_op jit(solution)/shard_map/all_to_all | solution.py:276
  223.5 7.6 %shard_map.111 = bf16[1024,1280]{1,0:T(8,128)(2,1)} custom-call(s32[1,384]{1,0:T(1,128)} %add.179.bucket_ref, bf16[1280,384]{1,0:T(8,128)(2,1)} %bitcast.22.a_ref, bf16[384,1280]{1,0:T(8,128)(2,1)} %copy-done.1, bf16[1280,1280]{1,0:T(8,128)(2,1)} %w_ref.1, bf16[1,1280]{1,0:T(2,128)(2,1)} %reshape.152.gain_ref), custom_call_target="tpu_custom_call" | custom-call | tf_op jit(solution)/shard_map/pallas_call | solution.py:225
  231.7 9.5 %all-to-all-start.3 = ((bf16[128,8,1280]{2,1,0:T(8,128)(2,1)}), bf16[128,8,1280]{2,1,0:T(8,128)(2,1)}, u32[]{:S(2)}, u32[]{:S(2)}) async-start(bf16[128,8,1280]{2,1,0:T(8,128)(2,1)} %bitcast.46), calls=%async_computation.3 | async-start | bytes 5242880 | tf_op jit(solution)/shard_map/all_to_all | solution.py:312
  242.4 34.4 %all-to-all-done.3 = bf16[128,8,1280]{2,1,0:T(8,128)(2,1)} async-done(((bf16[128,8,1280]{2,1,0:T(8,128)(2,1)}), bf16[128,8,1280]{2,1,0:T(8,128)(2,1)}, u32[]{:S(2)}, u32[]{:S(2)}) %all-to-all-start.3) | async-done | bytes 2621472 | tf_op jit(solution)/shard_map/all_to_all | solution.py:312
  276.7 4.5 %shard_map.112 = bf16[96,5120]{1,0:T(8,128)(2,1)} custom-call(s32[1,1024]{1,0:T(1,128)} %add.175.target_ref, bf16[1024,1280]{1,0:T(8,128)(2,1)} %bitcast.24.got_ref), custom_call_target="tpu_custom_call" | custom-call | tf_op jit(solution)/shard_map/pallas_call | solution.py:246
  (41 shorter events, 7.9 us)
Async XLA Ops:
  0.0 33.0 %copy-start = (bf16[1280,1280]{1,0:T(8,128)(2,1)S(1)}, bf16[1280,1280]{1,0:T(8,128)(2,1)}, u32[]{:S(2)}) copy-start(bf16[1280,1280]{1,0:T(8,128)(2,1)} %param.16) | copy-start | bytes 9830404
  0.0 40.3 %collective-permute-start.1 = (bf16[240,1280]{1,0:T(8,128)(2,1)}, bf16[240,1280]{1,0:T(8,128)(2,1)}, u32[]{:S(2)}, u32[]{:S(2)}) collective-permute-start(bf16[240,1280]{1,0:T(8,128)(2,1)} %bitcast.20.refs_0_), channel_id=1, source_target_pairs={{0,2},{1,3},{2,4},{3,5},{4,6},{5,7},{6,0},{7,1},{8,10},{9,11},{10,... | collective-permute-start | bytes 1843208 | tf_op jit(solution)/shard_map/ppermute | solution.py:83
  14.5 4.5 %copy-start.5 = (s32[1,384]{1,0:T(1,128)S(1)}, s32[1,384]{1,0:T(1,128)}, u32[]{:S(2)}) copy-start(s32[1,384]{1,0:T(1,128)} %param.12) | copy-start | bytes 4612
  29.3 3.7 %copy-start.2 = (bf16[1,384,1280]{2,1,0:T(8,128)(2,1)S(1)}, bf16[1,384,1280]{2,1,0:T(8,128)(2,1)}, u32[]{:S(2)}) copy-start(bf16[1,384,1280]{2,1,0:T(8,128)(2,1)} %param.11) | copy-start | bytes 2949124
  33.0 1.7 copy-start.3
  34.7 1.0 copy-start.1
  36.9 23.8 %collective-permute-start = (bf16[384,1280]{1,0:T(8,128)(2,1)}, bf16[384,1280]{1,0:T(8,128)(2,1)}, u32[]{:S(2)}, u32[]{:S(2)}) collective-permute-start(bf16[384,1280]{1,0:T(8,128)(2,1)} %fusion.11), channel_id=1, source_target_pairs={{0,1},{1,0},{2,3},{3,2},{4,5},{5,4},{6,7},{7,6},{8,9},{9,8},{10,11... | collective-permute-start | bytes 2949128 | tf_op jit(solution)/shard_map/ppermute | solution.py:293
  37.9 17.0 %collective-permute-start.3 = (bf16[240,1280]{1,0:T(8,128)(2,1)}, bf16[240,1280]{1,0:T(8,128)(2,1)}, u32[]{:S(2)}, u32[]{:S(2)}) collective-permute-start(bf16[240,1280]{1,0:T(8,128)(2,1)} %bitcast.20.refs_0_), channel_id=1, source_target_pairs={{0,72},{1,73},{2,74},{3,75},{4,76},{5,77},{6,78},{7,79},{8,64},{9,... | collective-permute-start | bytes 1843208 | tf_op jit(solution)/shard_map/ppermute | solution.py:85
  40.4 17.2 %collective-permute-start.6 = (bf16[240,1280]{1,0:T(8,128)(2,1)}, bf16[240,1280]{1,0:T(8,128)(2,1)}, u32[]{:S(2)}, u32[]{:S(2)}) collective-permute-start(bf16[240,1280]{1,0:T(8,128)(2,1)} %collective-permute-done.1.refs_1_), channel_id=1, source_target_pairs={{0,2},{1,3},{2,4},{3,5},{4,6},{5,7},{6,0},{7,1},{8,10},{9,11},{10,... | collective-permute-start | bytes 1843208 | tf_op jit(solution)/shard_map/ppermute | solution.py:88
  42.0 22.0 %collective-permute-start.2 = (bf16[240,1280]{1,0:T(8,128)(2,1)}, bf16[240,1280]{1,0:T(8,128)(2,1)}, u32[]{:S(2)}, u32[]{:S(2)}) collective-permute-start(bf16[240,1280]{1,0:T(8,128)(2,1)} %bitcast.20.refs_0_), channel_id=1, source_target_pairs={{0,6},{1,7},{2,0},{3,1},{4,2},{5,3},{6,4},{7,5},{8,14},{9,15},{10,... | collective-permute-start | bytes 1843208 | tf_op jit(solution)/shard_map/ppermute | solution.py:84
  54.9 16.1 %collective-permute-start.4 = (bf16[240,1280]{1,0:T(8,128)(2,1)}, bf16[240,1280]{1,0:T(8,128)(2,1)}, u32[]{:S(2)}, u32[]{:S(2)}) collective-permute-start(bf16[240,1280]{1,0:T(8,128)(2,1)} %collective-permute-done.3.refs_3_), channel_id=1, source_target_pairs={{0,2},{1,3},{2,4},{3,5},{4,6},{5,7},{6,0},{7,1},{8,10},{9,11},{10,... | collective-permute-start | bytes 1843208 | tf_op jit(solution)/shard_map/ppermute | solution.py:86
  56.5 14.6 %collective-permute-start.5 = (bf16[240,1280]{1,0:T(8,128)(2,1)}, bf16[240,1280]{1,0:T(8,128)(2,1)}, u32[]{:S(2)}, u32[]{:S(2)}) collective-permute-start(bf16[240,1280]{1,0:T(8,128)(2,1)} %collective-permute-done.3.refs_3_), channel_id=1, source_target_pairs={{0,6},{1,7},{2,0},{3,1},{4,2},{5,3},{6,4},{7,5},{8,14},{9,15},{10,... | collective-permute-start | bytes 1843208 | tf_op jit(solution)/shard_map/ppermute | solution.py:87
  57.6 15.5 %collective-permute-start.7 = (bf16[240,1280]{1,0:T(8,128)(2,1)}, bf16[240,1280]{1,0:T(8,128)(2,1)}, u32[]{:S(2)}, u32[]{:S(2)}) collective-permute-start(bf16[240,1280]{1,0:T(8,128)(2,1)} %collective-permute-done.6.refs_6_), channel_id=1, source_target_pairs={{0,72},{1,73},{2,74},{3,75},{4,76},{5,77},{6,78},{7,79},{8,64},{9,... | collective-permute-start | bytes 1843208 | tf_op jit(solution)/shard_map/ppermute | solution.py:89
  83.1 39.7 %all-to-all-start.1 = ((bf16[8,240,768]{2,1,0:T(8,128)(2,1)}), bf16[8,240,768]{2,1,0:T(8,128)(2,1)}, u32[]{:S(2)}, u32[]{:S(2)}) async-start(bf16[8,240,768]{2,1,0:T(8,128)(2,1)} %shard_map.109), calls=%async_computation.1 | async-start | bytes 5898240 | tf_op jit(solution)/shard_map/all_to_all | solution.py:299
  88.2 110.0 %copy-start.6 = (s32[96]{0:T(128)S(1)}, s32[96]{0:T(128)}, u32[]{:S(2)}) copy-start(s32[96]{0:T(128)} %param.21) | copy-start | bytes 1156
  88.2 134.7 %copy-start.4 = (bf16[1280]{0:T(1024)(128)(2,1)S(1)}, bf16[1280]{0:T(1024)(128)(2,1)}, u32[]{:S(2)}) copy-start(bf16[1280]{0:T(1024)(128)(2,1)} %param.20) | copy-start | bytes 7684
  192.2 22.6 %all-to-all-start.2 = ((bf16[16,80,384]{2,1,0:T(8,128)(2,1)}), bf16[16,80,384]{2,1,0:T(8,128)(2,1)}, u32[]{:S(2)}, u32[]{:S(2)}) async-start(bf16[16,80,384]{2,1,0:T(8,128)(2,1)} %shard_map.110), calls=%async_computation.2 | async-start | bytes 1966080 | tf_op jit(solution)/shard_map/all_to_all | solution.py:303
  214.8 16.9 %all-to-all-start = ((s32[128,1,2]{2,1,0:T(1,128)}), s32[128,1,2]{2,1,0:T(1,128)S(1)}, u32[]{:S(2)}, u32[]{:S(2)}) async-start(s32[128,1,2]{2,1,0:T(1,128)} %bitcast), calls=%async_computation | async-start | bytes 131072 | tf_op jit(solution)/shard_map/all_to_all | solution.py:276
  231.7 45.0 %all-to-all-start.3 = ((bf16[128,8,1280]{2,1,0:T(8,128)(2,1)}), bf16[128,8,1280]{2,1,0:T(8,128)(2,1)}, u32[]{:S(2)}, u32[]{:S(2)}) async-start(bf16[128,8,1280]{2,1,0:T(8,128)(2,1)} %bitcast.46), calls=%async_computation.3 | async-start | bytes 5242880 | tf_op jit(solution)/shard_map/all_to_all | solution.py:312

commit v2 on v1

--- a/solution.py
+++ b/solution.py
@@ -31,30 +31,97 @@
     )
 
 
-def split_heads(row_block):
-    return row_block.reshape(row_block.shape[0], -1, HEAD_DIM)
-
-
-def attend_block(query_heads, key_heads, value_heads, allowed):
-    scores = jnp.einsum(
-        "qhd,khd->hqk", query_heads, key_heads, preferred_element_type=F32
-    ) * HEAD_DIM ** (-0.5)
-    scores = jnp.where(allowed[None], scores, MASKED_SCORE)
-    maxima = jnp.max(scores, axis=-1)
-    weights = jnp.where(allowed[None], jnp.exp(scores - maxima[:, :, None]), 0.0)
-    totals = jnp.sum(weights, axis=-1)
-    summed = jnp.einsum(
-        "hqk,khd->qhd", weights.astype(BF16), value_heads, preferred_element_type=F32
-    )
-    return (maxima, totals, summed)
-
-
-def finish(totals, summed):
-    return (summed / totals.T[:, :, None]).astype(BF16).reshape(summed.shape[0], -1)
-
-
 def whole(count):
     return [pl.BlockSpec(memory_space=pltpu.VMEM)] * count
+
+
+def layer_one_kernel(
+    ids_row_ref, ids_column_ref, x_ref, gain_one_ref, gain_two_ref, w_qkv_ref, w_out_hbm,
+    second_ref, hidden_ref, h_ref, q_ref, k_ref, a_ref, w_out_ref, sem,
+):
+    step = pl.program_id(0)
+    copy = pltpu.make_async_copy(w_out_hbm, w_out_ref, sem)
+
+    @pl.when(step == 0)
+    def _():
+        copy.start()
+        h_ref[...] = normed(x_ref[0], gain_one_ref[...]).astype(BF16)
+
+    def project_one():
+        return jnp.dot(h_ref[...], w_qkv_ref[0], preferred_element_type=F32).astype(BF16)
+
+    @pl.when(step == 0)
+    def _():
+        q_ref[...] = project_one()
+
+    @pl.when(step == 1)
+    def _():
+        k_ref[...] = project_one()
+
+    @pl.when(step == 2)
+    def _():
+        values_all = project_one()
+        allowed = ids_column_ref[...] == ids_row_ref[...]
+        rows = allowed.shape[0]
+        tiles = {}
+        for head in range(D // HEAD_DIM):
+            begin, end = head * HEAD_DIM, (head + 1) * HEAD_DIM
+            low, high = begin // 128 * 128, (end + 127) // 128 * 128
+            lane = low + lax.broadcasted_iota(jnp.int32, (1, high - low), 1)
+            mine = (lane >= begin) & (lane < end)
+            keys = jnp.where(mine, k_ref[:, low:high], 0.0).astype(BF16)
+            values = values_all[:, low:high]
+            scores = lax.dot_general(
+                q_ref[:, low:high], keys, NT, preferred_element_type=F32
+            ) * HEAD_DIM ** (-0.5)
+            scores = jnp.where(allowed, scores, MASKED_SCORE)
+            most = jnp.max(scores, axis=1, keepdims=True)
+            weights = jnp.exp(scores - most)
+            total = jnp.sum(weights, axis=1, keepdims=True)
+            result = jnp.dot(weights.astype(BF16), values, preferred_element_type=F32) / total
+            for tile in range(low, high, 128):
+                piece = result[:, tile - low : tile - low + 128]
+                if tile in tiles:
+                    piece = jnp.where(mine[:, tile - low : tile - low + 128], piece, tiles[tile])
+                tiles[tile] = piece
+                if tile + 128 <= end:
+                    a_ref[:, tile : tile + 128] = tiles.pop(tile).astype(BF16)
+        copy.wait()
+        second = x_ref[0].astype(F32) + jnp.dot(
+            a_ref[...], w_out_ref[...], preferred_element_type=F32
+        )
+        second = second.astype(BF16)
+        second_ref[...] = second
+        hidden_ref[...] = normed(second, gain_two_ref[...]).astype(BF16)
+
+
+def layer_one(ids, patches, gain_one, gain_two, w_qkv, w_out):
+    rows = patches.shape[1]
+    fixed = lambda *shape: pl.BlockSpec(shape, lambda i: (0,) * len(shape))
+    return pl.pallas_call(
+        layer_one_kernel,
+        out_shape=[jax.ShapeDtypeStruct((rows, D), BF16)] * 2,
+        grid=(3,),
+        in_specs=[
+            fixed(1, rows),
+            fixed(rows, 1),
+            fixed(1, rows, D),
+            fixed(1, D),
+            fixed(1, D),
+            pl.BlockSpec((1, D, D), lambda i: (i, 0, 0)),
+            pl.BlockSpec(memory_space=pl.ANY),
+        ],
+        out_specs=[fixed(rows, D)] * 2,
+        scratch_shapes=[pltpu.VMEM((rows, D), BF16)] * 4
+        + [pltpu.VMEM((D, D), BF16), pltpu.SemaphoreType.DMA],
+        compiler_params=pltpu.CompilerParams(vmem_limit_bytes=VMEM_LIMIT),
+        cost_estimate=pl.CostEstimate(
+            flops=6 * 10**9, bytes_accessed=16 * 10**6, transcendentals=3 * 10**6
+        ),
+    )(
+        ids, ids.reshape(rows, 1), patches, gain_one.reshape(1, D), gain_two.reshape(1, D),
+        w_qkv, w_out,
+    )
 
 
 def device_perm(move):
@@ -76,42 +143,78 @@
 X_OTHER = device_perm(lambda x, y, z, core: (OTHER_X[x], y, z, core))
 CORE_SWAP = device_perm(lambda x, y, z, core: (x, y, z, 1 - core))
 BOTH = ("ctx", "img")
-SHARD_OFFSETS = ((0, 0), (0, -1), (0, 1), (1, 0), (1, -1), (1, 1), (0, -2), (1, -2))
-
-
-def gather_parity(shard):
+NEAR_OFFSETS = ((0, 0), (0, -1), (0, 1), (1, 0))
+FAR_OFFSETS = ((1, -1), (1, 1), (0, 2), (1, 2))
+
+
+def near_shards(shard):
     below = lax.ppermute(shard, BOTH, Z_UP)
     above = lax.ppermute(shard, BOTH, Z_DOWN)
     other = lax.ppermute(shard, BOTH, X_OTHER)
+    return [shard, below, above, other]
+
+
+def far_shards(near):
+    shard, below, above, other = near
+    half = 128
+    far_top = lax.ppermute(below[:half], BOTH, Z_UP)
+    far_bottom = lax.ppermute(above[half:], BOTH, Z_DOWN)
     other_below = lax.ppermute(other, BOTH, Z_UP)
     other_above = lax.ppermute(other, BOTH, Z_DOWN)
-    far = lax.ppermute(below, BOTH, Z_UP)
-    other_far = lax.ppermute(far, BOTH, X_OTHER)
-    return [shard, below, above, other, other_below, other_above, far, other_far]
-
-
-def project_kernel(order_ref, h_even_ref, h_odd_ref, *refs):
-    out_ref = refs[8]
-    rows = h_even_ref.shape[0]
+    other_far_top = lax.ppermute(far_top, BOTH, X_OTHER)
+    other_far_bottom = lax.ppermute(far_bottom, BOTH, X_OTHER)
+    return [other_below, other_above, far_top, far_bottom, other_far_top, other_far_bottom]
+
+
+def project_kernel(order_ref, h_own_ref, h_partner_ref, *refs, parts, aliased):
+    count = sum(parts)
+    weights_refs = refs[:count]
+    out_hbm, done_ref, sem = refs[count + aliased :]
+    rows = h_own_ref.shape[0]
     part = lax.broadcasted_iota(jnp.int32, (3 * HEAD_DIM, 1), 0)
     scale = jnp.where(part < HEAD_DIM, Q_SCALE, 1.0).astype(F32)
-    for n in range(8):
-        weights = refs[n][...]
-        target = order_ref[n]
-        for half, h_ref in enumerate((h_even_ref, h_odd_ref)):
-            product = lax.dot_general(weights, h_ref[...], NT, preferred_element_type=F32)
-            out_ref[target, :, half * rows : (half + 1) * rows] = (product * scale).astype(BF16)
-
-
-def project(order, h_even, h_odd, shards):
-    rows = h_even.shape[0]
+    core = order_ref[len(parts)]
+    copies = []
+    first = 0
+    for n, pieces in enumerate(parts):
+        begin = 0
+        for weights_ref in weights_refs[first : first + pieces]:
+            end = begin + weights_ref.shape[0]
+            for side, h_ref in ((core, h_own_ref), (1 - core, h_partner_ref)):
+                product = lax.dot_general(
+                    weights_ref[...], h_ref[...], NT, preferred_element_type=F32
+                )
+                at = pl.multiple_of(side * rows, 128)
+                done_ref[n, begin:end, pl.ds(at, rows)] = (product * scale[begin:end]).astype(BF16)
+            begin = end
+        first += pieces
+        copy = pltpu.make_async_copy(done_ref.at[n], out_hbm.at[order_ref[n]], sem.at[n])
+        copy.start()
+        copies.append(copy)
+    for copy in copies:
+        copy.wait()
+
+
+def project(order, h_own, h_partner, shards, parts, into=None):
+    rows = h_own.shape[0]
+    aliased = 0 if into is None else 1
     return pl.pallas_call(
-        project_kernel,
+        functools.partial(project_kernel, parts=parts, aliased=aliased),
         out_shape=jax.ShapeDtypeStruct((8, 3 * HEAD_DIM, 2 * rows), BF16),
-        in_specs=[pl.BlockSpec(memory_space=pltpu.SMEM)] + whole(10),
-        out_specs=pl.BlockSpec(memory_space=pltpu.VMEM),
+        in_specs=[pl.BlockSpec(memory_space=pltpu.SMEM)]
+        + whole(2 + len(shards))
+        + [pl.BlockSpec(memory_space=pl.ANY)] * aliased,
+        out_specs=pl.BlockSpec(memory_space=pl.ANY),
+        scratch_shapes=[
+            pltpu.VMEM((len(parts), 3 * HEAD_DIM, 2 * rows), BF16),
+            pltpu.SemaphoreType.DMA((len(parts),)),
+        ],
+        input_output_aliases={3 + len(shards): 0} if aliased else {},
         compiler_params=pltpu.CompilerParams(vmem_limit_bytes=VMEM_LIMIT),
-    )(order, h_even, h_odd, *shards)
+        cost_estimate=pl.CostEstimate(
+            flops=2 * 10**9, bytes_accessed=6 * 10**6, transcendentals=0
+        ),
+    )(order, h_own, h_partner, *shards, *([into] if aliased else []))
 
 
 def attention_kernel(count_ref, q_ref, all_ref, out_ref, k_ref, v_ref, bound_ref, *, block):
@@ -190,7 +293,7 @@
     chips, features, rows = received.shape
     total = chips * rows
     return pl.pallas_call(
-        functools.partial(attention_kernel, block=512),
+        functools.partial(attention_kernel, block=1024),
         out_shape=jax.ShapeDtypeStruct((2 * chips, HEAD_DIM, rows // 2), BF16),
         grid=(chips,),
         in_specs=[
@@ -258,8 +361,12 @@
     me = lax.axis_index("img")
     my_x, my_z, my_core = me // 8, (me // 2) % 4, me % 2
     shard = jnp.swapaxes(w_qkv2, 1, 2).reshape(3 * HEAD_DIM, D)
-    shards = gather_parity(shard)
-    order = jnp.stack([((my_x + dx) % 2) * 4 + (my_z + dz) % 4 for dx, dz in SHARD_OFFSETS])
+    near = near_shards(shard)
+    far = far_shards(near)
+
+    def order_of(offsets):
+        targets = [((my_x + dx) % 2) * 4 + (my_z + dz) % 4 for dx, dz in offsets]
+        return jnp.stack(targets + [my_core])
 
     merged_rows = slots.shape[0]
     device_count = 128
@@ -278,22 +385,13 @@
     )
     target_rows = (4 * got_slots.reshape(-1)[:, None] + quarter[None, :]).reshape(1, -1)
 
-    first = patches[0].astype(F32)
-    hidden = normed(first, gain_one).astype(BF16)
-    projected = jnp.einsum("pd,tde->tpe", hidden, w_qkv1, preferred_element_type=F32).astype(BF16)
-    local_ids = window_ids[0]
-    allowed = local_ids[:, None] == local_ids[None, :]
-    maxima, totals, summed = attend_block(
-        split_heads(projected[0]), split_heads(projected[1]), split_heads(projected[2]), allowed
-    )
-    attended = finish(totals, summed)
-    second = (first + jnp.dot(attended, w_out1, preferred_element_type=F32)).astype(BF16)
-    hidden = normed(second, gain_two).astype(BF16)
+    second, hidden = layer_one(window_ids, patches, gain_one, gain_two, w_qkv1, w_out1)
 
     partner = lax.ppermute(hidden, BOTH, CORE_SWAP)
-    even = my_core == 0
+    projected = project(order_of(NEAR_OFFSETS), hidden, partner, near, (1, 1, 1, 1))
+    far, target_rows, bucket_rows = lax.optimization_barrier((far, target_rows, bucket_rows))
     projected = project(
-        order, jnp.where(even, hidden, partner), jnp.where(even, partner, hidden), shards
+        order_of(FAR_OFFSETS), hidden, partner, far, (1, 1, 2, 2), into=projected
     )
     groups = [[2 * chip + core for chip in range(8)] for core in range(2)]
     received = lax.all_to_all(

time: 282 us -> 254 us (0.901)
  waiting for transfers between devices: 106 us -> 54.7 us
  blocking collectives: 0 us -> 41.9 us
  matrix products: 21.4 us -> 0 us
  Pallas kernels: 91.4 us -> 104 us
  starting transfers between devices: 41 us -> 34.5 us
  other arithmetic: 7.55 us -> 2.53 us
    all_to_all x0 -> x1, blocking collectives: none -> 41.9 us  [on_device(): lax.all_to_all(send.reshape(device_count, capacity * 4, D), BOTH, split_a...]
    all_to_all x1 -> x0, waiting for transfers between devices: 34.4 us -> none  [on_device(): lax.all_to_all(send.reshape(device_count, capacity * 4, D), BOTH, split_a...]
    ppermute x7 -> x9, waiting for transfers between devices: 20.9 us -> 4.15 us  [the longest x1 2.74 us: far_shards(): other_below = lax.ppermute(other, BOTH, Z_UP)]
    dot_general x3 -> x0, matrix products: 13.6 us -> none  [the longest x1 8.21 us: on_device(): jnp.einsum('pd,tde->tpe', hidden, w_qkv1, preferred_element_type=F32)]
    pallas_call x2 -> x4, Pallas kernels: 79.3 us -> 92.2 us  [the longest x1 63.7 us: attend_full(): pl.pallas_call(functools.partial(attention_kernel, block=1024), out_shape...]
    all_to_all x1 -> x0, starting transfers between devices: 9.46 us -> none  [on_device(): lax.all_to_all(send.reshape(device_count, capacity * 4, D), BOTH, split_a...]
    slice x4 -> x2, local copies, waits for them, and re-layouts: 8.42 us -> 0.04 us  [the longest x1 0.02 us: far_shards(): far_top = lax.ppermute(below[:half], BOTH, Z_UP)]
    sub x1 -> x0, matrix products: 7.81 us -> none  [attend_block(): scores - maxima[:, :, None]]
  transfers between devices with their start and end apart: 12 -> 13, of which waited for: 8 -> 4; matrix products, arithmetic and copies ran while one was open for 15% -> 5% of each run, Pallas kernels for 3% -> 9%
where the time goes in v2:
time: 254 us; the launch traced here: 253 us
  Pallas kernels  104 us (41%)
  waiting for transfers between devices  54.7 us (22%)
  blocking collectives  41.9 us (16%)
  starting transfers between devices  34.5 us (14%)
  local copies, waits for them, and re-layouts  14.2 us (6%)
    pallas_call x1, Pallas kernels, attend_full(): pl.pallas_call(functools.partial(attention_kernel, block=1024), out_shape...  63.7 us
    all_to_all x1, blocking collectives, on_device(): lax.all_to_all(send.reshape(device_count, capacity * 4, D), BOTH, split_a...  41.9 us
    all_to_all x1, waiting for transfers between devices, on_device(): lax.all_to_all(projected, 'img', split_axis=0, concat_axis=0, tiled=True,...  34.6 us
    pallas_call x1, Pallas kernels, layer_one(): pl.pallas_call(layer_one_kernel, out_shape=[jax.ShapeDtypeStruct((rows, D...  16.1 us
    all_to_all x1, waiting for transfers between devices, on_device(): lax.all_to_all(attended, 'img', split_axis=0, concat_axis=0, tiled=True)  15.9 us
    pallas_call x2, Pallas kernels, project(): pl.pallas_call(functools.partial(project_kernel, parts=parts, aliased=ali...  12.4 us
    pallas_call x1, Pallas kernels, merge(): pl.pallas_call(merge_kernel, out_shape=jax.ShapeDtypeStruct((places, D),...  7.56 us
    all_to_all x1, starting transfers between devices, on_device(): lax.all_to_all(attended, 'img', split_axis=0, concat_axis=0, tiled=True)  5.98 us
  transfers between devices with their start and end apart: 13, of which 4 were waited for; matrix products, arithmetic and copies ran while one was open for 5% of the time, Pallas kernels for 9%

profile of v2, /device:TPU:1, one launch (start us, length us, event | category | flops | bytes accessed | tf_op | source)
XLA Modules:
  0.0 253.0 jit_solution(12531824240638586169)
XLA Ops:
  0.0 3.3 %collective-permute-start = (bf16[240,1280]{1,0:T(8,128)(2,1)}, bf16[240,1280]{1,0:T(8,128)(2,1)}, u32[]{:S(2)}, u32[]{:S(2)}) collective-permute-start(bf16[240,1280]{1,0:T(8,128)(2,1)} %bitcast.21), channel_id=1, source_target_pairs={{0,72},{1,73},{2,74},{3,75},{4,76},{5,77},{6,78},{7,79},{8,64},{9,... | collective-permute-start | bytes 1843208 | tf_op jit(solution)/shard_map/ppermute | solution.py:153
  3.3 1.6 collective-permute-start.3
  4.9 2.1 collective-permute-start.5
  7.1 1.5 copy.17.ids_column_ref
  8.6 1.3 reshape.105.gain_one_ref
  9.8 1.3 reshape.106.gain_two_ref
  11.1 16.1 %shard_map.109 = (bf16[384,1280]{1,0:T(8,128)(2,1)}, bf16[384,1280]{1,0:T(8,128)(2,1)}) custom-call(s32[1,384]{1,0:T(1,128)} %ids_row_ref.1, s32[384,1]{1,0:T(8,128)} %copy.17.ids_column_ref, bf16[1,384,1280]{2,1,0:T(8,128)(2,1)} %x_ref.1, bf16[1,1280]{1,0:T(2,128)(2,1)} %reshape.105.gain_one_ref, bf16[1,1280]{1,0:T(2,128)(2,1)} %reshape.106.gain_two_ref, ...), custom_call_target="tpu_custom_call" | custom-call | flops 6000000000 | bytes 16000000 | tf_op jit(solution)/shard_map/pallas_call | solution.py:101
  27.2 1.3 collective-permute-start.9
  30.2 5.9 %all-to-all-start = ((s32[128,1,2]{2,1,0:T(1,128)}), s32[128,1,2]{2,1,0:T(1,128)S(1)}, u32[]{:S(2)}, u32[]{:S(2)}) async-start(s32[128,1,2]{2,1,0:T(1,128)} %bitcast.3), calls=%async_computation | async-start | bytes 131072 | tf_op jit(solution)/shard_map/all_to_all | solution.py:383
  36.1 0.8 copy-done.8
  37.0 1.6 collective-permute-start.4
  38.6 1.9 collective-permute-start.6
  40.8 2.3 collective-permute-start.2
  46.0 0.8 multiply_reduce_fusion
  46.8 1.0 mul.43
  47.8 2.5 collective-permute-start.8
  50.3 0.8 collective-permute-start.7
  51.9 1.0 copy-done.2
  52.9 5.8 %shard_map.110.refs_6_ = bf16[8,240,768]{2,1,0:T(8,128)(2,1)} custom-call(s32[5]{0:T(128)} %stack.44.order_ref, bf16[384,1280]{1,0:T(8,128)(2,1)} %get-tuple-element.17.h_own_ref, bf16[384,1280]{1,0:T(8,128)(2,1)} %copy-done.2, bf16[240,1280]{1,0:T(8,128)(2,1)} %bitcast.24, bf16[240,1280]{1,0:T(8,128)(2,1)} %copy-done.8, bf16[240,1280]{1,0:T(8,128)(2,1)} %copy-done.9, ...), custom_call_target="tpu_custom_call" | custom-call | flops 2000000000 | bytes 6000000 | tf_op jit(solution)/shard_map/pallas_call | solution.py:201
  58.7 2.7 %collective-permute-done.1.refs_0_ = bf16[240,1280]{1,0:T(8,128)(2,1)S(1)} collective-permute-done((bf16[240,1280]{1,0:T(8,128)(2,1)}, bf16[240,1280]{1,0:T(8,128)(2,1)S(1)}, u32[]{:S(2)}, u32[]{:S(2)}) %collective-permute-start.1) | collective-permute-done | bytes 614432 | tf_op jit(solution)/shard_map/ppermute | solution.py:162
  61.4 1.4 collective-permute-done.7.refs_4_
  63.6 6.6 %shard_map.111 = bf16[8,240,768]{2,1,0:T(8,128)(2,1)} custom-call(s32[5]{0:T(128)} %stack.39.order_ref, bf16[384,1280]{1,0:T(8,128)(2,1)} %get-tuple-element.17.h_own_ref, bf16[384,1280]{1,0:T(8,128)(2,1)} %copy-done.2, bf16[240,1280]{1,0:T(8,128)(2,1)} %copy-done.3, bf16[240,1280]{1,0:T(8,128)(2,1)} %copy-done.4, ...), custom_call_target="tpu_custom_call", output_to_operand_aliasing={{}: (9, {})} | custom-call | flops 2000000000 | bytes 6000000 | tf_op jit(solution)/shard_map/pallas_call | solution.py:201
  70.2 4.9 %all-to-all-start.1 = ((bf16[8,240,768]{2,1,0:T(8,128)(2,1)}), bf16[8,240,768]{2,1,0:T(8,128)(2,1)S(1)}, u32[]{:S(2)}, u32[]{:S(2)}) async-start(bf16[8,240,768]{2,1,0:T(8,128)(2,1)} %shard_map.111), calls=%async_computation.1 | async-start | bytes 5898240 | tf_op jit(solution)/shard_map/all_to_all | solution.py:397
  75.7 34.6 %all-to-all-done.1.q_ref.all_ref = bf16[8,240,768]{2,1,0:T(8,128)(2,1)S(1)} async-done(((bf16[8,240,768]{2,1,0:T(8,128)(2,1)}), bf16[8,240,768]{2,1,0:T(8,128)(2,1)S(1)}, u32[]{:S(2)}, u32[]{:S(2)}) %all-to-all-start.1) | async-done | bytes 2949152 | tf_op jit(solution)/shard_map/all_to_all | solution.py:397
  110.3 1.6 copy-done
  111.9 63.7 %shard_map.112 = bf16[16,80,384]{2,1,0:T(8,128)(2,1)} custom-call(s32[1]{0:T(128)S(6)} %copy.19.count_ref, bf16[8,240,768]{2,1,0:T(8,128)(2,1)} %copy-done, bf16[8,240,768]{2,1,0:T(8,128)(2,1)} %copy-done), custom_call_target="tpu_custom_call" | custom-call | tf_op jit(solution)/shard_map/pallas_call | solution.py:295
  175.6 6.0 %all-to-all-start.2 = ((bf16[16,80,384]{2,1,0:T(8,128)(2,1)}), bf16[16,80,384]{2,1,0:T(8,128)(2,1)S(1)}, u32[]{:S(2)}, u32[]{:S(2)}) async-start(bf16[16,80,384]{2,1,0:T(8,128)(2,1)} %shard_map.112), calls=%async_computation.2 | async-start | bytes 1966080 | tf_op jit(solution)/shard_map/all_to_all | solution.py:401
  182.2 15.9 %all-to-all-done.2 = bf16[16,80,384]{2,1,0:T(8,128)(2,1)S(1)} async-done(((bf16[16,80,384]{2,1,0:T(8,128)(2,1)}), bf16[16,80,384]{2,1,0:T(8,128)(2,1)S(1)}, u32[]{:S(2)}, u32[]{:S(2)}) %all-to-all-start.2) | async-done | bytes 983072 | tf_op jit(solution)/shard_map/all_to_all | solution.py:401
  198.1 0.9 copy-done.1
  199.1 7.6 %shard_map.113 = bf16[1024,1280]{1,0:T(8,128)(2,1)} custom-call(s32[1,384]{1,0:T(1,128)} %add.160.bucket_ref, bf16[1280,384]{1,0:T(8,128)(2,1)} %bitcast.19, bf16[384,1280]{1,0:T(8,128)(2,1)} %get-tuple-element.24.x_ref, bf16[1280,1280]{1,0:T(8,128)(2,1)} %w_ref.1, bf16[1,1280]{1,0:T(2,128)(2,1)} %reshape.108.gain_ref), custom_call_target="tpu_custom_call" | custom-call | tf_op jit(solution)/shard_map/pallas_call | solution.py:328
  206.6 41.9 %all_to_all.21 = bf16[128,8,1280]{2,1,0:T(8,128)(2,1)} all-to-all(bf16[128,8,1280]{2,1,0:T(8,128)(2,1)} %bitcast.17), channel_id=1, replica_groups=mesh['ctx'=8,'img'=16] {'ctx','img'}, dimensions={0} | all-to-all | bytes 5242880 | tf_op jit(solution)/shard_map/all_to_all | solution.py:410
  248.6 4.5 %shard_map.114 = bf16[96,5120]{1,0:T(8,128)(2,1)} custom-call(s32[1,1024]{1,0:T(1,128)} %add.156.target_ref, bf16[1024,1280]{1,0:T(8,128)(2,1)} %bitcast.18), custom_call_target="tpu_custom_call" | custom-call | tf_op jit(solution)/shard_map/pallas_call | solution.py:349
  (45 shorter events, 7.0 us)
Async XLA Ops:
  0.0 40.4 %collective-permute-start = (bf16[240,1280]{1,0:T(8,128)(2,1)}, bf16[240,1280]{1,0:T(8,128)(2,1)}, u32[]{:S(2)}, u32[]{:S(2)}) collective-permute-start(bf16[240,1280]{1,0:T(8,128)(2,1)} %bitcast.21), channel_id=1, source_target_pairs={{0,72},{1,73},{2,74},{3,75},{4,76},{5,77},{6,78},{7,79},{8,64},{9,... | collective-permute-start | bytes 1843208 | tf_op jit(solution)/shard_map/ppermute | solution.py:153
  3.3 32.8 %collective-permute-start.3 = (bf16[240,1280]{1,0:T(8,128)(2,1)}, bf16[240,1280]{1,0:T(8,128)(2,1)S(1)}, u32[]{:S(2)}, u32[]{:S(2)}) collective-permute-start(bf16[240,1280]{1,0:T(8,128)(2,1)} %bitcast.22), channel_id=1, source_target_pairs={{0,2},{1,3},{2,4},{3,5},{4,6},{5,7},{6,0},{7,1},{8,10},{9,11},{10,... | collective-permute-start | bytes 1843208 | tf_op jit(solution)/shard_map/ppermute | solution.py:151
  4.9 33.6 %collective-permute-start.5 = (bf16[240,1280]{1,0:T(8,128)(2,1)}, bf16[240,1280]{1,0:T(8,128)(2,1)S(1)}, u32[]{:S(2)}, u32[]{:S(2)}) collective-permute-start(bf16[240,1280]{1,0:T(8,128)(2,1)} %bitcast.23), channel_id=1, source_target_pairs={{0,6},{1,7},{2,0},{3,1},{4,2},{5,3},{6,4},{7,5},{8,14},{9,15},{10,... | collective-permute-start | bytes 1843208 | tf_op jit(solution)/shard_map/ppermute | solution.py:152
  11.1 17.4 %copy-start.11 = (s32[96]{0:T(128)S(1)}, s32[96]{0:T(128)}, u32[]{:S(2)}) copy-start(s32[96]{0:T(128)} %param.21) | copy-start | bytes 1156
  27.2 24.7 %collective-permute-start.9 = (bf16[384,1280]{1,0:T(8,128)(2,1)}, bf16[384,1280]{1,0:T(8,128)(2,1)S(1)}, u32[]{:S(2)}, u32[]{:S(2)}) collective-permute-start(bf16[384,1280]{1,0:T(8,128)(2,1)} %get-tuple-element.17.h_own_ref), channel_id=1, source_target_pairs={{0,1},{1,0},{2,3},{3,2},{4,5},{5,4},{6,7},{7,6},{8,9},{9,8},{10,11... | collective-permute-start | bytes 2949128 | tf_op jit(solution)/shard_map/ppermute | solution.py:390
  30.2 15.7 %all-to-all-start = ((s32[128,1,2]{2,1,0:T(1,128)}), s32[128,1,2]{2,1,0:T(1,128)S(1)}, u32[]{:S(2)}, u32[]{:S(2)}) async-start(s32[128,1,2]{2,1,0:T(1,128)} %bitcast.3), calls=%async_computation | async-start | bytes 131072 | tf_op jit(solution)/shard_map/all_to_all | solution.py:383
  36.1 0.8 copy-start.8
  37.0 13.3 %collective-permute-start.4 = (bf16[128,1280]{1,0:T(8,128)(2,1)S(1)}, bf16[128,1280]{1,0:T(8,128)(2,1)S(1)}, u32[]{:S(2)}, u32[]{:S(2)}) collective-permute-start(bf16[128,1280]{1,0:T(8,128)(2,1)S(1)} %slice.8), channel_id=1, source_target_pairs={{0,2},{1,3},{2,4},{3,5},{4,6},{5,7},{6,0},{7,1},{8,10},{9,11},{10,... | collective-permute-start | bytes 983048 | tf_op jit(solution)/shard_map/ppermute | solution.py:160
  38.5 1.9 copy-start.9
  38.6 9.2 %collective-permute-start.6 = (bf16[112,1280]{1,0:T(8,128)(2,1)S(1)}, bf16[112,1280]{1,0:T(8,128)(2,1)S(1)}, u32[]{:S(2)}, u32[]{:S(2)}) collective-permute-start(bf16[112,1280]{1,0:T(8,128)(2,1)S(1)} %slice.9), channel_id=1, source_target_pairs={{0,6},{1,7},{2,0},{3,1},{4,2},{5,3},{6,4},{7,5},{8,14},{9,15},{10,... | collective-permute-start | bytes 860168 | tf_op jit(solution)/shard_map/ppermute | solution.py:161
  40.4 21.0 %collective-permute-start.1 = (bf16[240,1280]{1,0:T(8,128)(2,1)}, bf16[240,1280]{1,0:T(8,128)(2,1)S(1)}, u32[]{:S(2)}, u32[]{:S(2)}) collective-permute-start(bf16[240,1280]{1,0:T(8,128)(2,1)} %collective-permute-done.refs_3_), channel_id=1, source_target_pairs={{0,2},{1,3},{2,4},{3,5},{4,6},{5,7},{6,0},{7,1},{8,10},{9,11},{10,... | collective-permute-start | bytes 1843208 | tf_op jit(solution)/shard_map/ppermute | solution.py:162
  40.8 20.6 %collective-permute-start.2 = (bf16[240,1280]{1,0:T(8,128)(2,1)}, bf16[240,1280]{1,0:T(8,128)(2,1)S(1)}, u32[]{:S(2)}, u32[]{:S(2)}) collective-permute-start(bf16[240,1280]{1,0:T(8,128)(2,1)} %collective-permute-done.refs_3_), channel_id=1, source_target_pairs={{0,6},{1,7},{2,0},{3,1},{4,2},{5,3},{6,4},{7,5},{8,14},{9,15},{10,... | collective-permute-start | bytes 1843208 | tf_op jit(solution)/shard_map/ppermute | solution.py:163
  47.8 15.1 %copy-start.7 = (bf16[112,1280]{1,0:T(8,128)(2,1)}, bf16[112,1280]{1,0:T(8,128)(2,1)S(1)}, u32[]{:S(2)}) copy-start(bf16[112,1280]{1,0:T(8,128)(2,1)S(1)} %collective-permute-done.6.refs_3_) | copy-start | bytes 860164
  47.8 10.9 %collective-permute-start.8 = (bf16[112,1280]{1,0:T(8,128)(2,1)S(1)}, bf16[112,1280]{1,0:T(8,128)(2,1)}, u32[]{:S(2)}, u32[]{:S(2)}) collective-permute-start(bf16[112,1280]{1,0:T(8,128)(2,1)S(1)} %collective-permute-done.6.refs_3_), channel_id=1, source_target_pairs={{0,72},{1,73},{2,74},{3,75},{4,76},{5,77},{6,78},{7,79},{8,64},{9,... | collective-permute-start | bytes 860168 | tf_op jit(solution)/shard_map/ppermute | solution.py:165
  50.3 12.5 %copy-start.5 = (bf16[128,1280]{1,0:T(8,128)(2,1)}, bf16[128,1280]{1,0:T(8,128)(2,1)S(1)}, u32[]{:S(2)}) copy-start(bf16[128,1280]{1,0:T(8,128)(2,1)S(1)} %collective-permute-done.4.refs_2_) | copy-start | bytes 983044
  50.3 12.5 %collective-permute-start.7 = (bf16[128,1280]{1,0:T(8,128)(2,1)S(1)}, bf16[128,1280]{1,0:T(8,128)(2,1)S(1)}, u32[]{:S(2)}, u32[]{:S(2)}) collective-permute-start(bf16[128,1280]{1,0:T(8,128)(2,1)S(1)} %collective-permute-done.4.refs_2_), channel_id=1, source_target_pairs={{0,72},{1,73},{2,74},{3,75},{4,76},{5,77},{6,78},{7,79},{8,64},{9,... | collective-permute-start | bytes 983048 | tf_op jit(solution)/shard_map/ppermute | solution.py:164
  51.9 1.0 copy-start.2
  61.4 1.4 copy-start.3
  61.4 1.4 copy-start.4
  62.9 0.7 copy-start.6
  70.2 40.1 %all-to-all-start.1 = ((bf16[8,240,768]{2,1,0:T(8,128)(2,1)}), bf16[8,240,768]{2,1,0:T(8,128)(2,1)S(1)}, u32[]{:S(2)}, u32[]{:S(2)}) async-start(bf16[8,240,768]{2,1,0:T(8,128)(2,1)} %shard_map.111), calls=%async_computation.1 | async-start | bytes 5898240 | tf_op jit(solution)/shard_map/all_to_all | solution.py:397
  75.7 105.9 %copy-start.10 = (bf16[1280]{0:T(1024)(128)(2,1)S(1)}, bf16[1280]{0:T(1024)(128)(2,1)}, u32[]{:S(2)}) copy-start(bf16[1280]{0:T(1024)(128)(2,1)} %param.20) | copy-start | bytes 7684
  110.3 1.6 copy-start
  175.6 22.5 %all-to-all-start.2 = ((bf16[16,80,384]{2,1,0:T(8,128)(2,1)}), bf16[16,80,384]{2,1,0:T(8,128)(2,1)S(1)}, u32[]{:S(2)}, u32[]{:S(2)}) async-start(bf16[16,80,384]{2,1,0:T(8,128)(2,1)} %shard_map.112), calls=%async_computation.2 | async-start | bytes 1966080 | tf_op jit(solution)/shard_map/all_to_all | solution.py:401
  198.1 0.9 copy-start.1

commit v3 on v2

--- a/solution.py
+++ b/solution.py
@@ -27,7 +27,7 @@
     return (
         values
         * lax.rsqrt(jnp.mean(values * values, axis=-1, keepdims=True) + EPSILON)
-        * gain.astype(F32)
+        * gain.astype(F32).reshape(1, -1)
     )
 
 
@@ -36,7 +36,7 @@
 
 
 def layer_one_kernel(
-    ids_row_ref, ids_column_ref, x_ref, gain_one_ref, gain_two_ref, w_qkv_ref, w_out_hbm,
+    ids_ref, x_ref, gain_one_ref, gain_two_ref, w_qkv_ref, w_out_hbm,
     second_ref, hidden_ref, h_ref, q_ref, k_ref, a_ref, w_out_ref, sem,
 ):
     step = pl.program_id(0)
@@ -61,8 +61,9 @@
     @pl.when(step == 2)
     def _():
         values_all = project_one()
-        allowed = ids_column_ref[...] == ids_row_ref[...]
-        rows = allowed.shape[0]
+        rows = ids_ref.shape[1]
+        ids = jnp.broadcast_to(ids_ref[...], (8, rows))
+        allowed = ids.T[:, 0:1] == ids[0:1]
         tiles = {}
         for head in range(D // HEAD_DIM):
             begin, end = head * HEAD_DIM, (head + 1) * HEAD_DIM
@@ -104,10 +105,9 @@
         grid=(3,),
         in_specs=[
             fixed(1, rows),
-            fixed(rows, 1),
             fixed(1, rows, D),
-            fixed(1, D),
-            fixed(1, D),
+            fixed(D),
+            fixed(D),
             pl.BlockSpec((1, D, D), lambda i: (i, 0, 0)),
             pl.BlockSpec(memory_space=pl.ANY),
         ],
@@ -119,8 +119,7 @@
             flops=6 * 10**9, bytes_accessed=16 * 10**6, transcendentals=3 * 10**6
         ),
     )(
-        ids, ids.reshape(rows, 1), patches, gain_one.reshape(1, D), gain_two.reshape(1, D),
-        w_qkv, w_out,
+        ids, patches, gain_one, gain_two, w_qkv, w_out
     )
 
 
@@ -169,25 +168,23 @@
 def project_kernel(order_ref, h_own_ref, h_partner_ref, *refs, parts, aliased):
     count = sum(parts)
     weights_refs = refs[:count]
-    out_hbm, done_ref, sem = refs[count + aliased :]
+    out_hbm, w_ref, h_ref, done_ref, sem = refs[count + aliased :]
     rows = h_own_ref.shape[0]
-    part = lax.broadcasted_iota(jnp.int32, (3 * HEAD_DIM, 1), 0)
+    wide = 3 * HEAD_DIM
+    core = order_ref[len(parts)]
+    for side, ref in ((core, h_own_ref), (1 - core, h_partner_ref)):
+        h_ref[pl.ds(pl.multiple_of(side * rows, 16), rows), :] = ref[...]
+    at = 0
+    for weights_ref in weights_refs:
+        w_ref[at : at + weights_ref.shape[0], :] = weights_ref[...]
+        at += weights_ref.shape[0]
+    part = lax.broadcasted_iota(jnp.int32, (len(parts) * wide, 1), 0) % wide
     scale = jnp.where(part < HEAD_DIM, Q_SCALE, 1.0).astype(F32)
-    core = order_ref[len(parts)]
+    product = lax.dot_general(w_ref[...], h_ref[...], NT, preferred_element_type=F32)
+    product = (product * scale).astype(BF16)
     copies = []
-    first = 0
-    for n, pieces in enumerate(parts):
-        begin = 0
-        for weights_ref in weights_refs[first : first + pieces]:
-            end = begin + weights_ref.shape[0]
-            for side, h_ref in ((core, h_own_ref), (1 - core, h_partner_ref)):
-                product = lax.dot_general(
-                    weights_ref[...], h_ref[...], NT, preferred_element_type=F32
-                )
-                at = pl.multiple_of(side * rows, 128)
-                done_ref[n, begin:end, pl.ds(at, rows)] = (product * scale[begin:end]).astype(BF16)
-            begin = end
-        first += pieces
+    for n in range(len(parts)):
+        done_ref[n] = product[n * wide : (n + 1) * wide]
         copy = pltpu.make_async_copy(done_ref.at[n], out_hbm.at[order_ref[n]], sem.at[n])
         copy.start()
         copies.append(copy)
@@ -197,16 +194,19 @@
 
 def project(order, h_own, h_partner, shards, parts, into=None):
     rows = h_own.shape[0]
+    wide = 3 * HEAD_DIM
     aliased = 0 if into is None else 1
     return pl.pallas_call(
         functools.partial(project_kernel, parts=parts, aliased=aliased),
-        out_shape=jax.ShapeDtypeStruct((8, 3 * HEAD_DIM, 2 * rows), BF16),
+        out_shape=jax.ShapeDtypeStruct((8, wide, 2 * rows), BF16),
         in_specs=[pl.BlockSpec(memory_space=pltpu.SMEM)]
         + whole(2 + len(shards))
         + [pl.BlockSpec(memory_space=pl.ANY)] * aliased,
         out_specs=pl.BlockSpec(memory_space=pl.ANY),
         scratch_shapes=[
-            pltpu.VMEM((len(parts), 3 * HEAD_DIM, 2 * rows), BF16),
+            pltpu.VMEM((len(parts) * wide, D), BF16),
+            pltpu.VMEM((2 * rows, D), BF16),
+            pltpu.VMEM((len(parts), wide, 2 * rows), BF16),
             pltpu.SemaphoreType.DMA((len(parts),)),
         ],
         input_output_aliases={3 + len(shards): 0} if aliased else {},
@@ -336,13 +336,13 @@
 
 def place_kernel(target_ref, got_ref, out_ref):
     rows = out_ref.shape[0]
-    got = got_ref[...]
-    row = 4 * lax.broadcasted_iota(jnp.int32, (rows, got.shape[0]), 0)
-    for j in range(4):
-        chosen = (row + j) == target_ref[...]
-        out_ref[:, j * D : (j + 1) * D] = jnp.dot(
-            chosen.astype(BF16), got, preferred_element_type=F32
-        ).astype(BF16)
+    wide = got_ref.shape[1]
+    index = lax.broadcasted_iota(jnp.int32, (4 * rows, 1), 0)
+    wanted = 4 * (index % rows) + index // rows
+    chosen = (wanted == target_ref[...]).astype(BF16)
+    found = jnp.dot(chosen, got_ref[...], preferred_element_type=F32).astype(BF16)
+    for n in range(4):
+        out_ref[:, n * wide : (n + 1) * wide] = found[n * rows : (n + 1) * rows]
 
 
 def place(target, got, rows):
@@ -353,6 +353,48 @@
         out_specs=pl.BlockSpec(memory_space=pltpu.VMEM),
         compiler_params=pltpu.CompilerParams(vmem_limit_bytes=VMEM_LIMIT),
     )(target, got)
+
+
+def routes_kernel(me_ref, all_ref, own_ref, bucket_ref, target_ref):
+    devices, rows = all_ref.shape
+    places = target_ref.shape[1]
+    me = me_ref[0]
+    owner = jnp.broadcast_to(own_ref[...] // rows, (8, rows))
+    sender = owner.T[:, 0:1]
+    earlier = lax.broadcasted_iota(jnp.int32, (rows, rows), 0) < lax.broadcasted_iota(
+        jnp.int32, (rows, rows), 1
+    )
+    rank = jnp.sum(((sender == owner[0:1]) & earlier).astype(jnp.int32), axis=0, keepdims=True)
+    bucket = jnp.broadcast_to(4 * (2 * owner[0:1] + rank), (8, rows)).T[:, 0:1]
+    lane = lax.broadcasted_iota(jnp.int32, (rows, 4 * rows), 1)
+    mine = lane // 4 == lax.broadcasted_iota(jnp.int32, (rows, 4 * rows), 0)
+    bucket_ref[...] = jnp.sum(jnp.where(mine, bucket + lane % 4, 0), axis=0, keepdims=True)
+    hit = all_ref[...] // rows == me
+    place = all_ref[...] - me * rows
+    column = lax.broadcasted_iota(jnp.int32, (devices, rows), 1)
+    first = jnp.min(jnp.where(hit, column, rows), axis=1, keepdims=True)
+    slot_first = jnp.sum(jnp.where(hit & (column == first), place + 1, 0), axis=1, keepdims=True)
+    slot_second = jnp.sum(jnp.where(hit & (column > first), place + 1, 0), axis=1, keepdims=True)
+    lane = lax.broadcasted_iota(jnp.int32, (devices, places), 1)
+    source = lax.broadcasted_iota(jnp.int32, (devices, places), 0)
+    slot = jnp.where(lane // 4 % 2 == 0, slot_first, slot_second) - 1
+    value = jnp.where(lane // 8 == source, 4 * slot + lane % 4, 0)
+    target_ref[...] = jnp.sum(value, axis=0, keepdims=True)
+
+
+def routes(me, every, own, places):
+    rows = own.shape[1]
+    return pl.pallas_call(
+        routes_kernel,
+        out_shape=[
+            jax.ShapeDtypeStruct((1, 4 * rows), jnp.int32),
+            jax.ShapeDtypeStruct((1, places), jnp.int32),
+        ],
+        in_specs=[pl.BlockSpec(memory_space=pltpu.SMEM)] + whole(2),
+        out_specs=whole(2),
+        compiler_params=pltpu.CompilerParams(vmem_limit_bytes=VMEM_LIMIT),
+        cost_estimate=pl.CostEstimate(flops=10**6, bytes_accessed=10**6, transcendentals=0),
+    )(me, every, own)
 
 
 def on_device(
@@ -368,28 +410,12 @@
         targets = [((my_x + dx) % 2) * 4 + (my_z + dz) % 4 for dx, dz in offsets]
         return jnp.stack(targets + [my_core])
 
-    merged_rows = slots.shape[0]
-    device_count = 128
-    capacity = 2
-    owner = slots // merged_rows
-    local_slot = slots % merged_rows
-    row_order = jnp.arange(merged_rows, dtype=jnp.int32)
-    earlier = (owner[:, None] == owner[None, :]) & (row_order[None, :] < row_order[:, None])
-    bucket = owner * capacity + jnp.sum(earlier.astype(jnp.int32), axis=1)
-    quarter = jnp.arange(4, dtype=jnp.int32)
-    bucket_rows = (4 * bucket[:, None] + quarter[None, :]).reshape(1, 4 * merged_rows)
-    hits = bucket[:, None] == jnp.arange(device_count * capacity, dtype=jnp.int32)[None, :]
-    send_slots = jnp.sum(jnp.where(hits, local_slot[:, None] + 1, 0), axis=0) - 1
-    got_slots = lax.all_to_all(
-        send_slots.reshape(device_count, capacity), BOTH, split_axis=0, concat_axis=0, tiled=True
-    )
-    target_rows = (4 * got_slots.reshape(-1)[:, None] + quarter[None, :]).reshape(1, -1)
+    every_slots = lax.all_gather(slots.reshape(1, -1), BOTH, axis=0, tiled=True)
 
     second, hidden = layer_one(window_ids, patches, gain_one, gain_two, w_qkv1, w_out1)
 
     partner = lax.ppermute(hidden, BOTH, CORE_SWAP)
     projected = project(order_of(NEAR_OFFSETS), hidden, partner, near, (1, 1, 1, 1))
-    far, target_rows, bucket_rows = lax.optimization_barrier((far, target_rows, bucket_rows))
     projected = project(
         order_of(FAR_OFFSETS), hidden, partner, far, (1, 1, 2, 2), into=projected
     )
@@ -397,20 +423,19 @@
     received = lax.all_to_all(
         projected, "img", split_axis=0, concat_axis=0, tiled=True, axis_index_groups=groups
     )
+    every_slots, projected = lax.optimization_barrier((every_slots, projected))
+    places = 128 * 2 * 4
+    device = lax.axis_index("ctx") * 16 + me
+    bucket_rows, target_rows = routes(
+        device.reshape(1), every_slots, slots.reshape(1, -1), places
+    )
     attended = attend_full(counts, received)
     attended = lax.all_to_all(attended, "img", split_axis=0, concat_axis=0, tiled=True)
-    send = merge(
-        bucket_rows,
-        attended.reshape(D, -1),
-        second,
-        w_out2,
-        gain_out.reshape(1, D),
-        device_count * capacity * 4,
-    )
+    send = merge(bucket_rows, attended.reshape(D, -1), second, w_out2, gain_out, places)
     got = lax.all_to_all(
-        send.reshape(device_count, capacity * 4, D), BOTH, split_axis=0, concat_axis=0, tiled=True
-    )
-    return place(target_rows, got.reshape(-1, D), merged_rows)
+        send.reshape(128, 8, D), BOTH, split_axis=0, concat_axis=0, tiled=True
+    )
+    return place(target_rows, got.reshape(places, D), slots.shape[0])
 
 
 def solution(mesh):

time: 254 us -> 304 us (1.20)
  blocking collectives: 41.9 us -> 113 us
  starting transfers between devices: 34.5 us -> 24.6 us
  local copies, waits for them, and re-layouts: 14.2 us -> 7.64 us
    unnamed x0 -> x1, blocking collectives: none -> 71.9 us
    all_to_all x1, waiting for transfers between devices: 15.9 us -> 0.01 us  [on_device(): lax.all_to_all(attended, 'img', split_axis=0, concat_axis=0, tiled=True)]
    ppermute x1, waiting for transfers between devices: 0.01 us -> 11.7 us  [far_shards(): far_bottom = lax.ppermute(above[half:], BOTH, Z_DOWN)]
    ppermute x1, waiting for transfers between devices: 0.01 us -> 6.27 us  [far_shards(): far_top = lax.ppermute(below[:half], BOTH, Z_UP)]
    all_to_all x1 -> x0, starting transfers between devices: 5.87 us -> none  [on_device(): lax.all_to_all(send_slots.reshape(device_count, capacity), BOTH, split_ax...]
    reshape x4 -> x0, local copies, waits for them, and re-layouts: 4.65 us -> none  [the longest x1 1.49 us: layer_one(): ids.reshape(rows, 1)]
  transfers between devices with their start and end apart: 13 -> 12, of which waited for: 4 -> 4; matrix products, arithmetic and copies ran while one was open for 5% -> 1% of each run, Pallas kernels for 9% -> 8%
where the time goes in v3:
time: 304 us; the launch traced here: 303 us
  blocking collectives  113 us (37%)
  Pallas kernels  104 us (34%)
  waiting for transfers between devices  52.8 us (17%)
  starting transfers between devices  24.6 us (8%)
  local copies, waits for them, and re-layouts  7.64 us (3%)
    unnamed x1, blocking collectives  71.9 us
    pallas_call x1, Pallas kernels, attend_full(): pl.pallas_call(functools.partial(attention_kernel, block=1024), out_shape...  63.7 us
    all_to_all x1, blocking collectives, on_device(): lax.all_to_all(send.reshape(128, 8, D), BOTH, split_axis=0, concat_axis=0...  41.3 us
    all_to_all x1, waiting for transfers between devices, on_device(): lax.all_to_all(projected, 'img', split_axis=0, concat_axis=0, tiled=True,...  34.6 us
    pallas_call x1, Pallas kernels, layer_one(): pl.pallas_call(layer_one_kernel, out_shape=[jax.ShapeDtypeStruct((rows, D...  16.1 us
    ppermute x1, waiting for transfers between devices, far_shards(): far_bottom = lax.ppermute(above[half:], BOTH, Z_DOWN)  11.7 us
    pallas_call x2, Pallas kernels, project(): pl.pallas_call(functools.partial(project_kernel, parts=parts, aliased=ali...  10.9 us
    pallas_call x1, Pallas kernels, merge(): pl.pallas_call(merge_kernel, out_shape=jax.ShapeDtypeStruct((places, D),...  7.56 us
  transfers between devices with their start and end apart: 12, of which 4 were waited for; matrix products, arithmetic and copies ran while one was open for 1% of the time, Pallas kernels for 8%

profile of v3, /device:TPU:1, one launch (start us, length us, event | category | flops | bytes accessed | tf_op | source)
XLA Modules:
  0.0 303.0 jit_solution(6158685845807080786)
XLA Ops:
  0.0 3.3 %collective-permute-start.1 = (bf16[240,1280]{1,0:T(8,128)(2,1)}, bf16[240,1280]{1,0:T(8,128)(2,1)}, u32[]{:S(2)}, u32[]{:S(2)}) collective-permute-start(bf16[240,1280]{1,0:T(8,128)(2,1)} %bitcast.21), channel_id=1, source_target_pairs={{0,72},{1,73},{2,74},{3,75},{4,76},{5,77},{6,78},{7,79},{8,64},{9,... | collective-permute-start | bytes 1843208 | tf_op jit(solution)/shard_map/ppermute | solution.py:152
  3.3 1.6 collective-permute-start.4
  4.9 2.1 collective-permute-start.6
  7.1 16.1 %shard_map.109 = (bf16[384,1280]{1,0:T(8,128)(2,1)}, bf16[384,1280]{1,0:T(8,128)(2,1)}) custom-call(s32[1,384]{1,0:T(1,128)} %ids_ref.1, bf16[1,384,1280]{2,1,0:T(8,128)(2,1)} %x_ref.1, bf16[1280]{0:T(1024)(128)(2,1)} %gain_one_ref.1, bf16[1280]{0:T(1024)(128)(2,1)} %gain_two_ref.1, bf16[3,1280,1280]{2,1,0:T(8,128)(2,1)} %w_qkv_ref.1, ...), custom_call_target="tpu_custom_call" | custom-call | flops 6000000000 | bytes 16000000 | tf_op jit(solution)/shard_map/pallas_call | solution.py:102
  23.2 1.3 collective-permute-start
  24.5 0.3 collective-permute-start.5
  24.8 1.2 collective-permute-start.2
  26.0 1.5 collective-permute-start.3
  27.6 1.4 collective-permute-start.7
  29.0 6.3 %collective-permute-done.5.refs_2_ = bf16[128,1280]{1,0:T(8,128)(2,1)S(1)} collective-permute-done((bf16[128,1280]{1,0:T(8,128)(2,1)S(1)}, bf16[128,1280]{1,0:T(8,128)(2,1)S(1)}, u32[]{:S(2)}, u32[]{:S(2)}) %collective-permute-start.5) | collective-permute-done | bytes 327712 | tf_op jit(solution)/shard_map/ppermute | solution.py:159
  35.5 11.7 %collective-permute-done.7.refs_3_ = bf16[112,1280]{1,0:T(8,128)(2,1)S(1)} collective-permute-done((bf16[112,1280]{1,0:T(8,128)(2,1)S(1)}, bf16[112,1280]{1,0:T(8,128)(2,1)S(1)}, u32[]{:S(2)}, u32[]{:S(2)}) %collective-permute-start.7) | collective-permute-done | bytes 286752 | tf_op jit(solution)/shard_map/ppermute | solution.py:160
  47.4 0.6 stack.44.order_ref
  48.0 0.6 stack.39.order_ref
  48.7 1.0 copy-done.2
  49.6 5.4 %shard_map.110.refs_6_ = bf16[8,240,768]{2,1,0:T(8,128)(2,1)} custom-call(s32[5]{0:T(128)} %stack.44.order_ref, bf16[384,1280]{1,0:T(8,128)(2,1)} %get-tuple-element.10.h_own_ref, bf16[384,1280]{1,0:T(8,128)(2,1)} %copy-done.2, bf16[240,1280]{1,0:T(8,128)(2,1)} %bitcast.24, bf16[240,1280]{1,0:T(8,128)(2,1)} %copy-done.9, bf16[240,1280]{1,0:T(8,128)(2,1)} %copy-done.10, ...), custom_call_target="tpu_custom_call" | custom-call | flops 2000000000 | bytes 6000000 | tf_op jit(solution)/shard_map/pallas_call | solution.py:199
  55.3 0.7 copy-done.8
  56.0 0.2 copy-done.3
  56.5 0.7 copy-done.6
  57.2 5.4 %shard_map.111 = bf16[8,240,768]{2,1,0:T(8,128)(2,1)} custom-call(s32[5]{0:T(128)} %stack.39.order_ref, bf16[384,1280]{1,0:T(8,128)(2,1)} %get-tuple-element.10.h_own_ref, bf16[384,1280]{1,0:T(8,128)(2,1)} %copy-done.2, bf16[240,1280]{1,0:T(8,128)(2,1)} %copy-done.3, bf16[240,1280]{1,0:T(8,128)(2,1)} %copy-done.4, ...), custom_call_target="tpu_custom_call", output_to_operand_aliasing={{}: (9, {})} | custom-call | flops 2000000000 | bytes 6000000 | tf_op jit(solution)/shard_map/pallas_call | solution.py:199
  62.6 5.3 %all-to-all-start = ((bf16[8,240,768]{2,1,0:T(8,128)(2,1)}), bf16[8,240,768]{2,1,0:T(8,128)(2,1)S(1)}, u32[]{:S(2)}, u32[]{:S(2)}) async-start(bf16[8,240,768]{2,1,0:T(8,128)(2,1)} %shard_map.111), calls=%async_computation | async-start | bytes 5898240 | tf_op jit(solution)/shard_map/all_to_all | solution.py:423
  68.6 34.6 %all-to-all-done.q_ref.all_ref = bf16[8,240,768]{2,1,0:T(8,128)(2,1)S(1)} async-done(((bf16[8,240,768]{2,1,0:T(8,128)(2,1)}), bf16[8,240,768]{2,1,0:T(8,128)(2,1)S(1)}, u32[]{:S(2)}, u32[]{:S(2)}) %all-to-all-start) | async-done | bytes 2949152 | tf_op jit(solution)/shard_map/all_to_all | solution.py:423
  103.2 1.6 copy-done
  104.8 63.7 %shard_map.113 = bf16[16,80,384]{2,1,0:T(8,128)(2,1)} custom-call(s32[1]{0:T(128)S(6)} %copy.15.count_ref, bf16[8,240,768]{2,1,0:T(8,128)(2,1)} %copy-done, bf16[8,240,768]{2,1,0:T(8,128)(2,1)} %copy-done), custom_call_target="tpu_custom_call" | custom-call | tf_op jit(solution)/shard_map/pallas_call | solution.py:295
  168.5 6.0 %all-to-all-start.1 = ((bf16[16,80,384]{2,1,0:T(8,128)(2,1)}), bf16[16,80,384]{2,1,0:T(8,128)(2,1)S(1)}, u32[]{:S(2)}, u32[]{:S(2)}) async-start(bf16[16,80,384]{2,1,0:T(8,128)(2,1)} %shard_map.113), calls=%async_computation.1 | async-start | bytes 1966080 | tf_op jit(solution)/shard_map/all_to_all | solution.py:433
  174.5 0.3 dynamic-update-slice
  174.8 71.9 %all-reduce = s32[12288]{0:T(1024)S(1)} all-reduce(s32[12288]{0:T(1024)S(1)} %dynamic-update-slice), channel_id=2, replica_groups=mesh['ctx'=8,'img'=16] {'ctx','img'}, use_global_device_ids=true, to_apply=%add | all-reduce | flops 12288 | bytes 98304
  246.7 0.7 reshape.25.all_ref
  247.4 1.9 shard_map.112
  249.3 0.9 copy-done.1
  250.3 7.6 %shard_map.114 = bf16[1024,1280]{1,0:T(8,128)(2,1)} custom-call(s32[1,384]{1,0:T(1,128)} %get-tuple-element.13.bucket_ref, bf16[1280,384]{1,0:T(8,128)(2,1)} %bitcast.19, bf16[384,1280]{1,0:T(8,128)(2,1)} %get-tuple-element.14.x_ref, bf16[1280,1280]{1,0:T(8,128)(2,1)} %w_ref.1, bf16[1280]{0:T(1024)(128)(2,1)} %gain_ref.1), custom_call_target="tpu_custom_call" | custom-call | tf_op jit(solution)/shard_map/pallas_call | solution.py:328
  257.8 41.3 %all_to_all.15 = bf16[128,8,1280]{2,1,0:T(8,128)(2,1)} all-to-all(bf16[128,8,1280]{2,1,0:T(8,128)(2,1)} %bitcast.17), channel_id=1, replica_groups=mesh['ctx'=8,'img'=16] {'ctx','img'}, dimensions={0} | all-to-all | bytes 5242880 | tf_op jit(solution)/shard_map/all_to_all | solution.py:435
  299.1 3.9 %shard_map.115 = bf16[96,5120]{1,0:T(8,128)(2,1)} custom-call(s32[1,1024]{1,0:T(1,128)} %get-tuple-element.12.target_ref, bf16[1024,1280]{1,0:T(8,128)(2,1)} %bitcast.18), custom_call_target="tpu_custom_call" | custom-call | tf_op jit(solution)/shard_map/pallas_call | solution.py:349
  (32 shorter events, 0.9 us)
Async XLA Ops:
  0.0 24.8 %collective-permute-start.1 = (bf16[240,1280]{1,0:T(8,128)(2,1)}, bf16[240,1280]{1,0:T(8,128)(2,1)}, u32[]{:S(2)}, u32[]{:S(2)}) collective-permute-start(bf16[240,1280]{1,0:T(8,128)(2,1)} %bitcast.21), channel_id=1, source_target_pairs={{0,72},{1,73},{2,74},{3,75},{4,76},{5,77},{6,78},{7,79},{8,64},{9,... | collective-permute-start | bytes 1843208 | tf_op jit(solution)/shard_map/ppermute | solution.py:152
  3.3 21.2 %collective-permute-start.4 = (bf16[240,1280]{1,0:T(8,128)(2,1)}, bf16[240,1280]{1,0:T(8,128)(2,1)S(1)}, u32[]{:S(2)}, u32[]{:S(2)}) collective-permute-start(bf16[240,1280]{1,0:T(8,128)(2,1)} %bitcast.22), channel_id=1, source_target_pairs={{0,2},{1,3},{2,4},{3,5},{4,6},{5,7},{6,0},{7,1},{8,10},{9,11},{10,... | collective-permute-start | bytes 1843208 | tf_op jit(solution)/shard_map/ppermute | solution.py:150
  4.9 22.6 %collective-permute-start.6 = (bf16[240,1280]{1,0:T(8,128)(2,1)}, bf16[240,1280]{1,0:T(8,128)(2,1)S(1)}, u32[]{:S(2)}, u32[]{:S(2)}) collective-permute-start(bf16[240,1280]{1,0:T(8,128)(2,1)} %bitcast.23), channel_id=1, source_target_pairs={{0,6},{1,7},{2,0},{3,1},{4,2},{5,3},{6,4},{7,5},{8,14},{9,15},{10,... | collective-permute-start | bytes 1843208 | tf_op jit(solution)/shard_map/ppermute | solution.py:151
  23.2 25.5 %collective-permute-start = (bf16[384,1280]{1,0:T(8,128)(2,1)}, bf16[384,1280]{1,0:T(8,128)(2,1)S(1)}, u32[]{:S(2)}, u32[]{:S(2)}) collective-permute-start(bf16[384,1280]{1,0:T(8,128)(2,1)} %get-tuple-element.10.h_own_ref), channel_id=1, source_target_pairs={{0,1},{1,0},{2,3},{3,2},{4,5},{5,4},{6,7},{7,6},{8,9},{9,8},{10,11... | collective-permute-start | bytes 2949128 | tf_op jit(solution)/shard_map/ppermute | solution.py:417
  24.5 22.7 %copy-start.9 = (bf16[240,1280]{1,0:T(8,128)(2,1)}, bf16[240,1280]{1,0:T(8,128)(2,1)S(1)}, u32[]{:S(2)}) copy-start(bf16[240,1280]{1,0:T(8,128)(2,1)S(1)} %collective-permute-done.4.refs_1_) | copy-start | bytes 1843204
  24.5 10.8 %collective-permute-start.5 = (bf16[128,1280]{1,0:T(8,128)(2,1)S(1)}, bf16[128,1280]{1,0:T(8,128)(2,1)S(1)}, u32[]{:S(2)}, u32[]{:S(2)}) collective-permute-start(bf16[128,1280]{1,0:T(8,128)(2,1)S(1)} %slice.8), channel_id=1, source_target_pairs={{0,2},{1,3},{2,4},{3,5},{4,6},{5,7},{6,0},{7,1},{8,10},{9,11},{10,... | collective-permute-start | bytes 983048 | tf_op jit(solution)/shard_map/ppermute | solution.py:159
  24.8 30.5 %collective-permute-start.2 = (bf16[240,1280]{1,0:T(8,128)(2,1)}, bf16[240,1280]{1,0:T(8,128)(2,1)S(1)}, u32[]{:S(2)}, u32[]{:S(2)}) collective-permute-start(bf16[240,1280]{1,0:T(8,128)(2,1)} %collective-permute-done.1.refs_3_), channel_id=1, source_target_pairs={{0,2},{1,3},{2,4},{3,5},{4,6},{5,7},{6,0},{7,1},{8,10},{9,11},{10,... | collective-permute-start | bytes 1843208 | tf_op jit(solution)/shard_map/ppermute | solution.py:161
  26.0 29.3 %collective-permute-start.3 = (bf16[240,1280]{1,0:T(8,128)(2,1)}, bf16[240,1280]{1,0:T(8,128)(2,1)S(1)}, u32[]{:S(2)}, u32[]{:S(2)}) collective-permute-start(bf16[240,1280]{1,0:T(8,128)(2,1)} %collective-permute-done.1.refs_3_), channel_id=1, source_target_pairs={{0,6},{1,7},{2,0},{3,1},{4,2},{5,3},{6,4},{7,5},{8,14},{9,15},{10,... | collective-permute-start | bytes 1843208 | tf_op jit(solution)/shard_map/ppermute | solution.py:162
  27.5 19.9 %copy-start.10 = (bf16[240,1280]{1,0:T(8,128)(2,1)}, bf16[240,1280]{1,0:T(8,128)(2,1)S(1)}, u32[]{:S(2)}) copy-start(bf16[240,1280]{1,0:T(8,128)(2,1)S(1)} %collective-permute-done.6.refs_2_) | copy-start | bytes 1843204
  27.6 19.6 %collective-permute-start.7 = (bf16[112,1280]{1,0:T(8,128)(2,1)S(1)}, bf16[112,1280]{1,0:T(8,128)(2,1)S(1)}, u32[]{:S(2)}, u32[]{:S(2)}) collective-permute-start(bf16[112,1280]{1,0:T(8,128)(2,1)S(1)} %slice.9), channel_id=1, source_target_pairs={{0,6},{1,7},{2,0},{3,1},{4,2},{5,3},{6,4},{7,5},{8,14},{9,15},{10,... | collective-permute-start | bytes 860168 | tf_op jit(solution)/shard_map/ppermute | solution.py:160
  35.3 20.0 %copy-start.5 = (bf16[128,1280]{1,0:T(8,128)(2,1)}, bf16[128,1280]{1,0:T(8,128)(2,1)S(1)}, u32[]{:S(2)}) copy-start(bf16[128,1280]{1,0:T(8,128)(2,1)S(1)} %collective-permute-done.5.refs_2_) | copy-start | bytes 983044
  35.3 20.0 %collective-permute-start.8 = (bf16[128,1280]{1,0:T(8,128)(2,1)S(1)}, bf16[128,1280]{1,0:T(8,128)(2,1)S(1)}, u32[]{:S(2)}, u32[]{:S(2)}) collective-permute-start(bf16[128,1280]{1,0:T(8,128)(2,1)S(1)} %collective-permute-done.5.refs_2_), channel_id=1, source_target_pairs={{0,72},{1,73},{2,74},{3,75},{4,76},{5,77},{6,78},{7,79},{8,64},{9,... | collective-permute-start | bytes 983048 | tf_op jit(solution)/shard_map/ppermute | solution.py:163
  47.2 8.1 %copy-start.7 = (bf16[112,1280]{1,0:T(8,128)(2,1)}, bf16[112,1280]{1,0:T(8,128)(2,1)S(1)}, u32[]{:S(2)}) copy-start(bf16[112,1280]{1,0:T(8,128)(2,1)S(1)} %collective-permute-done.7.refs_3_) | copy-start | bytes 860164
  47.2 8.1 %collective-permute-start.9 = (bf16[112,1280]{1,0:T(8,128)(2,1)S(1)}, bf16[112,1280]{1,0:T(8,128)(2,1)S(1)}, u32[]{:S(2)}, u32[]{:S(2)}) collective-permute-start(bf16[112,1280]{1,0:T(8,128)(2,1)S(1)} %collective-permute-done.7.refs_3_), channel_id=1, source_target_pairs={{0,72},{1,73},{2,74},{3,75},{4,76},{5,77},{6,78},{7,79},{8,64},{9,... | collective-permute-start | bytes 860168 | tf_op jit(solution)/shard_map/ppermute | solution.py:164
  48.7 1.0 copy-start.2
  55.3 0.7 copy-start.8
  55.3 1.0 copy-start.3
  55.3 1.2 copy-start.4
  56.5 0.7 copy-start.6
  62.6 40.6 %all-to-all-start = ((bf16[8,240,768]{2,1,0:T(8,128)(2,1)}), bf16[8,240,768]{2,1,0:T(8,128)(2,1)S(1)}, u32[]{:S(2)}, u32[]{:S(2)}) async-start(bf16[8,240,768]{2,1,0:T(8,128)(2,1)} %shard_map.111), calls=%async_computation | async-start | bytes 5898240 | tf_op jit(solution)/shard_map/all_to_all | solution.py:423
  68.6 105.9 %copy-start.11 = (s32[96]{0:T(128)S(1)}, s32[96]{0:T(128)}, u32[]{:S(2)}) copy-start(s32[96]{0:T(128)} %param.21) | copy-start | bytes 1156
  103.2 1.6 copy-start
  168.5 80.8 %all-to-all-start.1 = ((bf16[16,80,384]{2,1,0:T(8,128)(2,1)}), bf16[16,80,384]{2,1,0:T(8,128)(2,1)S(1)}, u32[]{:S(2)}, u32[]{:S(2)}) async-start(bf16[16,80,384]{2,1,0:T(8,128)(2,1)} %shard_map.113), calls=%async_computation.1 | async-start | bytes 1966080 | tf_op jit(solution)/shard_map/all_to_all | solution.py:433
  249.3 0.9 copy-start.1

commit v4 on v3

--- a/solution.py
+++ b/solution.py
@@ -15,6 +15,7 @@
 F32 = jnp.float32
 BF16 = jnp.bfloat16
 Q_SCALE = HEAD_DIM ** (-0.5) * math.log2(math.e)
+TAG = 128
 SAFE_BOUND = 64.0
 SAFE_VALUE = 2.0**40
 VMEM_LIMIT = 56 * 1024 * 1024
@@ -158,20 +159,22 @@
     half = 128
     far_top = lax.ppermute(below[:half], BOTH, Z_UP)
     far_bottom = lax.ppermute(above[half:], BOTH, Z_DOWN)
+    far_top, far_bottom, other = lax.optimization_barrier((far_top, far_bottom, other))
+    other_far_top = lax.ppermute(far_top, BOTH, X_OTHER)
+    other_far_bottom = lax.ppermute(far_bottom, BOTH, X_OTHER)
     other_below = lax.ppermute(other, BOTH, Z_UP)
     other_above = lax.ppermute(other, BOTH, Z_DOWN)
-    other_far_top = lax.ppermute(far_top, BOTH, X_OTHER)
-    other_far_bottom = lax.ppermute(far_bottom, BOTH, X_OTHER)
     return [other_below, other_above, far_top, far_bottom, other_far_top, other_far_bottom]
 
 
-def project_kernel(order_ref, h_own_ref, h_partner_ref, *refs, parts, aliased):
+def project_kernel(h_own_ref, h_partner_ref, *refs, parts, offsets, aliased):
     count = sum(parts)
+    me = lax.axis_index("img")
+    my_x, my_z, core = me // 8, me // 2 % 4, me % 2
     weights_refs = refs[:count]
     out_hbm, w_ref, h_ref, done_ref, sem = refs[count + aliased :]
     rows = h_own_ref.shape[0]
     wide = 3 * HEAD_DIM
-    core = order_ref[len(parts)]
     for side, ref in ((core, h_own_ref), (1 - core, h_partner_ref)):
         h_ref[pl.ds(pl.multiple_of(side * rows, 16), rows), :] = ref[...]
     at = 0
@@ -185,22 +188,24 @@
     copies = []
     for n in range(len(parts)):
         done_ref[n] = product[n * wide : (n + 1) * wide]
-        copy = pltpu.make_async_copy(done_ref.at[n], out_hbm.at[order_ref[n]], sem.at[n])
+        target = (my_x + offsets[n][0]) % 2 * 4 + (my_z + offsets[n][1] + 4) % 4
+        copy = pltpu.make_async_copy(done_ref.at[n], out_hbm.at[target], sem.at[n])
         copy.start()
         copies.append(copy)
     for copy in copies:
         copy.wait()
 
 
-def project(order, h_own, h_partner, shards, parts, into=None):
+def project(offsets, h_own, h_partner, shards, parts, into=None):
     rows = h_own.shape[0]
     wide = 3 * HEAD_DIM
     aliased = 0 if into is None else 1
     return pl.pallas_call(
-        functools.partial(project_kernel, parts=parts, aliased=aliased),
+        functools.partial(
+            project_kernel, parts=parts, offsets=offsets, aliased=aliased
+        ),
         out_shape=jax.ShapeDtypeStruct((8, wide, 2 * rows), BF16),
-        in_specs=[pl.BlockSpec(memory_space=pltpu.SMEM)]
-        + whole(2 + len(shards))
+        in_specs=whole(2 + len(shards))
         + [pl.BlockSpec(memory_space=pl.ANY)] * aliased,
         out_specs=pl.BlockSpec(memory_space=pl.ANY),
         scratch_shapes=[
@@ -209,12 +214,12 @@
             pltpu.VMEM((len(parts), wide, 2 * rows), BF16),
             pltpu.SemaphoreType.DMA((len(parts),)),
         ],
-        input_output_aliases={3 + len(shards): 0} if aliased else {},
+        input_output_aliases={2 + len(shards): 0} if aliased else {},
         compiler_params=pltpu.CompilerParams(vmem_limit_bytes=VMEM_LIMIT),
         cost_estimate=pl.CostEstimate(
             flops=2 * 10**9, bytes_accessed=6 * 10**6, transcendentals=0
         ),
-    )(order, h_own, h_partner, *shards, *([into] if aliased else []))
+    )(h_own, h_partner, *shards, *([into] if aliased else []))
 
 
 def attention_kernel(count_ref, q_ref, all_ref, out_ref, k_ref, v_ref, bound_ref, *, block):
@@ -247,15 +252,16 @@
         bound_ref[0] = jnp.max(q_most) * jnp.max(k_most)
         bound_ref[1] = jnp.max(v_most)
 
-    queries = q_ref[0, 0:depth, :]
-    queries = jnp.concatenate([queries, jnp.zeros((128 - depth, rows), BF16)], axis=0)
+    taken = q_ref.shape[0]
+    queries = jnp.concatenate([q_ref[n, 0:depth, :] for n in range(taken)], axis=1)
+    queries = jnp.concatenate([queries, jnp.zeros((128 - depth, taken * rows), BF16)], axis=0)
     small = (bound_ref[0] < SAFE_BOUND * SAFE_BOUND) & (bound_ref[1] < SAFE_VALUE)
 
     def store(acc):
         result = acc[0:depth] / acc[depth : depth + 1]
         half = rows // 2
-        out_ref[0] = result[:, 0:half].astype(BF16)
-        out_ref[1] = result[:, half:].astype(BF16)
+        for n in range(2 * taken):
+            out_ref[n] = result[:, n * half : (n + 1) * half].astype(BF16)
 
     @pl.when(small)
     def _():
@@ -283,8 +289,8 @@
             return new_most, acc * jnp.exp2(most - new_most) + part
 
         start_state = (
-            jnp.full((1, rows), MASKED_SCORE, F32),
-            jnp.zeros((depth + 16, rows), F32),
+            jnp.full((1, taken * rows), MASKED_SCORE, F32),
+            jnp.zeros((depth + 16, taken * rows), F32),
         )
         store(lax.fori_loop(0, total // block, step, start_state)[1])
 
@@ -292,16 +298,17 @@
 def attend_full(count, received):
     chips, features, rows = received.shape
     total = chips * rows
-    return pl.pallas_call(
-        functools.partial(attention_kernel, block=1024),
+    taken = 2
+    return pl.pallas_call(
+        functools.partial(attention_kernel, block=512),
         out_shape=jax.ShapeDtypeStruct((2 * chips, HEAD_DIM, rows // 2), BF16),
-        grid=(chips,),
+        grid=(chips // taken,),
         in_specs=[
             pl.BlockSpec(memory_space=pltpu.SMEM),
-            pl.BlockSpec((1, features, rows), lambda i: (i, 0, 0)),
+            pl.BlockSpec((taken, features, rows), lambda i: (i, 0, 0)),
             pl.BlockSpec(memory_space=pltpu.VMEM),
         ],
-        out_specs=pl.BlockSpec((2, HEAD_DIM, rows // 2), lambda i: (i, 0, 0)),
+        out_specs=pl.BlockSpec((2 * taken, HEAD_DIM, rows // 2), lambda i: (i, 0, 0)),
         scratch_shapes=[
             pltpu.VMEM((total, 128), BF16),
             pltpu.VMEM((HEAD_DIM + 16, total), BF16),
@@ -311,12 +318,13 @@
     )(count, received, received)
 
 
-def merge_kernel(bucket_ref, a_ref, x_ref, w_ref, gain_ref, out_ref):
+def merge_kernel(bucket_ref, tag_ref, a_ref, x_ref, w_ref, gain_ref, out_ref):
     attended = a_ref[...]
     third = x_ref[...].astype(F32) + lax.dot_general(
         attended, w_ref[...], TN, preferred_element_type=F32
     )
     merged = normed(third, gain_ref[...]).astype(BF16)
+    merged = jnp.concatenate([merged, tag_ref[...]], axis=1)
     places, patches = out_ref.shape[0], merged.shape[0]
     chosen = lax.broadcasted_iota(jnp.int32, (places, patches), 0) == bucket_ref[...]
     out_ref[...] = jnp.dot(
@@ -324,42 +332,43 @@
     ).astype(BF16)
 
 
-def merge(bucket, attended, second, w_out, gain, places):
+def merge(bucket, tag, attended, second, w_out, gain, places):
     return pl.pallas_call(
         merge_kernel,
-        out_shape=jax.ShapeDtypeStruct((places, D), BF16),
-        in_specs=whole(5),
+        out_shape=jax.ShapeDtypeStruct((places, D + TAG), BF16),
+        in_specs=whole(6),
         out_specs=pl.BlockSpec(memory_space=pltpu.VMEM),
         compiler_params=pltpu.CompilerParams(vmem_limit_bytes=VMEM_LIMIT),
-    )(bucket, attended, second, w_out, gain)
-
-
-def place_kernel(target_ref, got_ref, out_ref):
+    )(bucket, tag, attended, second, w_out, gain)
+
+
+def place_kernel(got_ref, out_ref):
     rows = out_ref.shape[0]
-    wide = got_ref.shape[1]
+    places = got_ref.shape[0]
+    tag = got_ref[:, D:].astype(F32).T[0:1].astype(jnp.int32)
+    target = 4 * tag + lax.broadcasted_iota(jnp.int32, (1, places), 1) % 4
     index = lax.broadcasted_iota(jnp.int32, (4 * rows, 1), 0)
-    wanted = 4 * (index % rows) + index // rows
-    chosen = (wanted == target_ref[...]).astype(BF16)
-    found = jnp.dot(chosen, got_ref[...], preferred_element_type=F32).astype(BF16)
+    wanted = 4 * (index % rows + 1) + index // rows
+    chosen = (wanted == target).astype(BF16)
+    found = jnp.dot(chosen, got_ref[:, :D], preferred_element_type=F32).astype(BF16)
     for n in range(4):
-        out_ref[:, n * wide : (n + 1) * wide] = found[n * rows : (n + 1) * rows]
-
-
-def place(target, got, rows):
+        out_ref[:, n * D : (n + 1) * D] = found[n * rows : (n + 1) * rows]
+
+
+def place(got, rows):
     return pl.pallas_call(
         place_kernel,
         out_shape=jax.ShapeDtypeStruct((rows, 4 * D), BF16),
-        in_specs=whole(2),
+        in_specs=whole(1),
         out_specs=pl.BlockSpec(memory_space=pltpu.VMEM),
         compiler_params=pltpu.CompilerParams(vmem_limit_bytes=VMEM_LIMIT),
-    )(target, got)
-
-
-def routes_kernel(me_ref, all_ref, own_ref, bucket_ref, target_ref):
-    devices, rows = all_ref.shape
-    places = target_ref.shape[1]
-    me = me_ref[0]
-    owner = jnp.broadcast_to(own_ref[...] // rows, (8, rows))
+    )(got)
+
+
+def routes_kernel(slots_ref, bucket_ref, tag_ref):
+    rows = slots_ref.shape[1]
+    slots = jnp.broadcast_to(slots_ref[...], (8, rows))
+    owner = slots // rows
     sender = owner.T[:, 0:1]
     earlier = lax.broadcasted_iota(jnp.int32, (rows, rows), 0) < lax.broadcasted_iota(
         jnp.int32, (rows, rows), 1
@@ -369,73 +378,59 @@
     lane = lax.broadcasted_iota(jnp.int32, (rows, 4 * rows), 1)
     mine = lane // 4 == lax.broadcasted_iota(jnp.int32, (rows, 4 * rows), 0)
     bucket_ref[...] = jnp.sum(jnp.where(mine, bucket + lane % 4, 0), axis=0, keepdims=True)
-    hit = all_ref[...] // rows == me
-    place = all_ref[...] - me * rows
-    column = lax.broadcasted_iota(jnp.int32, (devices, rows), 1)
-    first = jnp.min(jnp.where(hit, column, rows), axis=1, keepdims=True)
-    slot_first = jnp.sum(jnp.where(hit & (column == first), place + 1, 0), axis=1, keepdims=True)
-    slot_second = jnp.sum(jnp.where(hit & (column > first), place + 1, 0), axis=1, keepdims=True)
-    lane = lax.broadcasted_iota(jnp.int32, (devices, places), 1)
-    source = lax.broadcasted_iota(jnp.int32, (devices, places), 0)
-    slot = jnp.where(lane // 4 % 2 == 0, slot_first, slot_second) - 1
-    value = jnp.where(lane // 8 == source, 4 * slot + lane % 4, 0)
-    target_ref[...] = jnp.sum(value, axis=0, keepdims=True)
-
-
-def routes(me, every, own, places):
-    rows = own.shape[1]
+    place = (slots - owner * rows + 1).T[:, 0:1].astype(F32)
+    patch = lax.broadcasted_iota(jnp.int32, (4 * rows, rows), 0) // 4
+    spread = (patch == lax.broadcasted_iota(jnp.int32, (4 * rows, rows), 1)).astype(BF16)
+    tag_ref[...] = jnp.dot(
+        spread,
+        jnp.broadcast_to(place, (rows, TAG)).astype(BF16),
+        preferred_element_type=F32,
+    ).astype(BF16)
+
+
+def routes(slots):
+    rows = slots.shape[0]
     return pl.pallas_call(
         routes_kernel,
         out_shape=[
             jax.ShapeDtypeStruct((1, 4 * rows), jnp.int32),
-            jax.ShapeDtypeStruct((1, places), jnp.int32),
+            jax.ShapeDtypeStruct((4 * rows, TAG), BF16),
         ],
-        in_specs=[pl.BlockSpec(memory_space=pltpu.SMEM)] + whole(2),
+        in_specs=whole(1),
         out_specs=whole(2),
         compiler_params=pltpu.CompilerParams(vmem_limit_bytes=VMEM_LIMIT),
         cost_estimate=pl.CostEstimate(flops=10**6, bytes_accessed=10**6, transcendentals=0),
-    )(me, every, own)
+    )(slots.reshape(1, rows))
 
 
 def on_device(
     patches, window_ids, counts, gain_one, w_qkv1, w_out1, gain_two, w_qkv2, w_out2, gain_out, slots
 ):
-    me = lax.axis_index("img")
-    my_x, my_z, my_core = me // 8, (me // 2) % 4, me % 2
     shard = jnp.swapaxes(w_qkv2, 1, 2).reshape(3 * HEAD_DIM, D)
     near = near_shards(shard)
     far = far_shards(near)
 
-    def order_of(offsets):
-        targets = [((my_x + dx) % 2) * 4 + (my_z + dz) % 4 for dx, dz in offsets]
-        return jnp.stack(targets + [my_core])
-
-    every_slots = lax.all_gather(slots.reshape(1, -1), BOTH, axis=0, tiled=True)
-
     second, hidden = layer_one(window_ids, patches, gain_one, gain_two, w_qkv1, w_out1)
 
     partner = lax.ppermute(hidden, BOTH, CORE_SWAP)
-    projected = project(order_of(NEAR_OFFSETS), hidden, partner, near, (1, 1, 1, 1))
+    projected = project(NEAR_OFFSETS, hidden, partner, near, (1, 1, 1, 1))
     projected = project(
-        order_of(FAR_OFFSETS), hidden, partner, far, (1, 1, 2, 2), into=projected
+        FAR_OFFSETS, hidden, partner, far, (1, 1, 2, 2), into=projected
     )
     groups = [[2 * chip + core for chip in range(8)] for core in range(2)]
     received = lax.all_to_all(
         projected, "img", split_axis=0, concat_axis=0, tiled=True, axis_index_groups=groups
     )
-    every_slots, projected = lax.optimization_barrier((every_slots, projected))
-    places = 128 * 2 * 4
-    device = lax.axis_index("ctx") * 16 + me
-    bucket_rows, target_rows = routes(
-        device.reshape(1), every_slots, slots.reshape(1, -1), places
-    )
+    slots, projected = lax.optimization_barrier((slots, projected))
+    bucket_rows, tag = routes(slots)
     attended = attend_full(counts, received)
     attended = lax.all_to_all(attended, "img", split_axis=0, concat_axis=0, tiled=True)
-    send = merge(bucket_rows, attended.reshape(D, -1), second, w_out2, gain_out, places)
+    places = 128 * 2 * 4
+    send = merge(bucket_rows, tag, attended.reshape(D, -1), second, w_out2, gain_out, places)
     got = lax.all_to_all(
-        send.reshape(128, 8, D), BOTH, split_axis=0, concat_axis=0, tiled=True
-    )
-    return place(target_rows, got.reshape(places, D), slots.shape[0])
+        send.reshape(128, 8, D + TAG), BOTH, split_axis=0, concat_axis=0, tiled=True
+    )
+    return place(got.reshape(places, D + TAG), slots.shape[0])
 
 
 def solution(mesh):

time: 304 us -> 240 us (0.79)
  blocking collectives: 113 us -> 44.4 us
  waiting for transfers between devices: 52.8 us -> 63.1 us
  Pallas kernels: 104 us -> 99.7 us
    unnamed x1 -> x0, blocking collectives: 71.9 us -> none
    all_to_all x1, waiting for transfers between devices: 0.01 us -> 14.8 us  [on_device(): lax.all_to_all(attended, 'img', split_axis=0, concat_axis=0, tiled=True)]
    ppermute x1, waiting for transfers between devices: 0.22 us -> 6.17 us  [far_shards(): other_far_bottom = lax.ppermute(far_bottom, BOTH, X_OTHER)]
    ppermute x1, waiting for transfers between devices: 11.7 us -> 5.91 us  [far_shards(): far_bottom = lax.ppermute(above[half:], BOTH, Z_DOWN)]
    ppermute x1, waiting for transfers between devices: 6.27 us -> 1.83 us  [far_shards(): far_top = lax.ppermute(below[:half], BOTH, Z_UP)]
    pallas_call x4, Pallas kernels: 82.1 us -> 77.9 us  [the longest x1 59.4 us: attend_full(): pl.pallas_call(functools.partial(attention_kernel, block=512), out_shape=...]
    all_to_all x1, blocking collectives: 41.3 us -> 44.4 us  [on_device(): lax.all_to_all(send.reshape(128, 8, D + TAG), BOTH, split_axis=0, concat_...]
  transfers between devices with their start and end apart: 12 -> 12, of which waited for: 4 -> 5; matrix products, arithmetic and copies ran while one was open for 1% -> 0% of each run, Pallas kernels for 8% -> 10%
where the time goes in v4:
time: 240 us
  Pallas kernels  99.7 us (42%)
  waiting for transfers between devices  63.1 us (26%)
  blocking collectives  44.4 us (18%)
  starting transfers between devices  26.6 us (11%)
  local copies, waits for them, and re-layouts  5.43 us (2%)
    pallas_call x1, Pallas kernels, attend_full(): pl.pallas_call(functools.partial(attention_kernel, block=512), out_shape=...  59.4 us
    all_to_all x1, blocking collectives, on_device(): lax.all_to_all(send.reshape(128, 8, D + TAG), BOTH, split_axis=0, concat_...  44.4 us
    all_to_all x1, waiting for transfers between devices, on_device(): lax.all_to_all(projected, 'img', split_axis=0, concat_axis=0, tiled=True,...  34.3 us
    pallas_call x1, Pallas kernels, layer_one(): pl.pallas_call(layer_one_kernel, out_shape=[jax.ShapeDtypeStruct((rows, D...  16.1 us
    all_to_all x1, waiting for transfers between devices, on_device(): lax.all_to_all(attended, 'img', split_axis=0, concat_axis=0, tiled=True)  14.8 us
    pallas_call x2, Pallas kernels, project(): pl.pallas_call(functools.partial(project_kernel, parts=parts, offsets=off...  10.7 us
    pallas_call x1, Pallas kernels, merge(): pl.pallas_call(merge_kernel, out_shape=jax.ShapeDtypeStruct((places, D +...  7.78 us
    ppermute x1, waiting for transfers between devices, far_shards(): other_far_bottom = lax.ppermute(far_bottom, BOTH, X_OTHER)  6.17 us
  transfers between devices with their start and end apart: 12, of which 5 were waited for; matrix products, arithmetic and copies ran while one was open for 0% of the time, Pallas kernels for 10%

profile of v4, /device:TPU:1, one launch (start us, length us, event | category | flops | bytes accessed | tf_op | source)
XLA Modules:
  0.0 240.0 jit_solution(11253386675941254378)
XLA Ops:
  0.0 2.5 %collective-permute-start.1 = (bf16[240,1280]{1,0:T(8,128)(2,1)}, bf16[240,1280]{1,0:T(8,128)(2,1)S(1)}, u32[]{:S(2)}, u32[]{:S(2)}) collective-permute-start(bf16[240,1280]{1,0:T(8,128)(2,1)} %bitcast.10), channel_id=1, source_target_pairs={{0,2},{1,3},{2,4},{3,5},{4,6},{5,7},{6,0},{7,1},{8,10},{9,11},{10,... | collective-permute-start | bytes 1843208 | tf_op jit(solution)/shard_map/ppermute | solution.py:151
  2.5 2.1 collective-permute-start.3
  4.6 2.5 %collective-permute-start.5 = (bf16[240,1280]{1,0:T(8,128)(2,1)}, bf16[240,1280]{1,0:T(8,128)(2,1)S(1)}, u32[]{:S(2)}, u32[]{:S(2)}) collective-permute-start(bf16[240,1280]{1,0:T(8,128)(2,1)} %bitcast.12), channel_id=1, source_target_pairs={{0,72},{1,73},{2,74},{3,75},{4,76},{5,77},{6,78},{7,79},{8,64},{9,... | collective-permute-start | bytes 1843208 | tf_op jit(solution)/shard_map/ppermute | solution.py:153
  7.1 16.1 %shard_map.109 = (bf16[384,1280]{1,0:T(8,128)(2,1)}, bf16[384,1280]{1,0:T(8,128)(2,1)}) custom-call(s32[1,384]{1,0:T(1,128)} %ids_ref.1, bf16[1,384,1280]{2,1,0:T(8,128)(2,1)} %x_ref.1, bf16[1280]{0:T(1024)(128)(2,1)} %gain_one_ref.1, bf16[1280]{0:T(1024)(128)(2,1)} %gain_two_ref.1, bf16[3,1280,1280]{2,1,0:T(8,128)(2,1)} %w_qkv_ref.1, ...), custom_call_target="tpu_custom_call" | custom-call | flops 6000000000 | bytes 16000000 | tf_op jit(solution)/shard_map/pallas_call | solution.py:103
  23.2 1.3 collective-permute-start
  24.5 0.0 collective-permute-done.1.refs_1_
  24.5 0.3 collective-permute-start.2
  24.8 2.7 %collective-permute-start.4 = (bf16[112,1280]{1,0:T(8,128)(2,1)S(1)}, bf16[112,1280]{1,0:T(8,128)(2,1)S(1)}, u32[]{:S(2)}, u32[]{:S(2)}) collective-permute-start(bf16[112,1280]{1,0:T(8,128)(2,1)S(1)} %slice.9), channel_id=1, source_target_pairs={{0,6},{1,7},{2,0},{3,1},{4,2},{5,3},{6,4},{7,5},{8,14},{9,15},{10,... | collective-permute-start | bytes 860168 | tf_op jit(solution)/shard_map/ppermute | solution.py:161
  27.5 5.9 %collective-permute-done.4.refs_3_ = bf16[112,1280]{1,0:T(8,128)(2,1)S(1)} collective-permute-done((bf16[112,1280]{1,0:T(8,128)(2,1)S(1)}, bf16[112,1280]{1,0:T(8,128)(2,1)S(1)}, u32[]{:S(2)}, u32[]{:S(2)}) %collective-permute-start.4) | collective-permute-done | bytes 286752 | tf_op jit(solution)/shard_map/ppermute | solution.py:161
  33.5 1.8 collective-permute-done.2.refs_2_
  35.3 2.7 %collective-permute-start.7 = (bf16[240,1280]{1,0:T(8,128)(2,1)S(1)}, bf16[240,1280]{1,0:T(8,128)(2,1)S(1)}, u32[]{:S(2)}, u32[]{:S(2)}) collective-permute-start(bf16[240,1280]{1,0:T(8,128)(2,1)S(1)} %collective-permute-done.5.refs_3_), channel_id=1, source_target_pairs={{0,6},{1,7},{2,0},{3,1},{4,2},{5,3},{6,4},{7,5},{8,14},{9,15},{10,... | collective-permute-start | bytes 1843208 | tf_op jit(solution)/shard_map/ppermute | solution.py:166
  38.0 0.2 collective-permute-start.8
  38.2 2.5 %collective-permute-start.9 = (bf16[112,1280]{1,0:T(8,128)(2,1)S(1)}, bf16[112,1280]{1,0:T(8,128)(2,1)S(1)}, u32[]{:S(2)}, u32[]{:S(2)}) collective-permute-start(bf16[112,1280]{1,0:T(8,128)(2,1)S(1)} %collective-permute-done.4.refs_3_), channel_id=1, source_target_pairs={{0,72},{1,73},{2,74},{3,75},{4,76},{5,77},{6,78},{7,79},{8,64},{9,... | collective-permute-start | bytes 860168 | tf_op jit(solution)/shard_map/ppermute | solution.py:164
  40.7 0.9 copy-done.2
  41.6 5.4 %shard_map.110.refs_6_ = bf16[8,240,768]{2,1,0:T(8,128)(2,1)} custom-call(bf16[384,1280]{1,0:T(8,128)(2,1)} %get-tuple-element.13.h_own_ref, bf16[384,1280]{1,0:T(8,128)(2,1)} %copy-done.2, bf16[240,1280]{1,0:T(8,128)(2,1)} %bitcast.13, bf16[240,1280]{1,0:T(8,128)(2,1)} %copy-done.9, bf16[240,1280]{1,0:T(8,128)(2,1)} %copy-done.10, bf16[240,1280]{1,0:T(8,128)(2,1)} %copy-done.11), custom_call_target="tpu_custom_call" | custom-call | flops 2000000000 | bytes 6000000 | tf_op jit(solution)/shard_map/pallas_call | solution.py:203
  47.0 6.2 %collective-permute-done.9.refs_5_ = bf16[112,1280]{1,0:T(8,128)(2,1)S(1)} collective-permute-done((bf16[112,1280]{1,0:T(8,128)(2,1)S(1)}, bf16[112,1280]{1,0:T(8,128)(2,1)S(1)}, u32[]{:S(2)}, u32[]{:S(2)}) %collective-permute-start.9) | collective-permute-done | bytes 286752 | tf_op jit(solution)/shard_map/ppermute | solution.py:164
  53.2 0.7 copy-done.8
  53.9 0.1 copy-done.6
  54.0 0.2 copy-done.3
  54.2 0.8 copy-done.4
  55.1 5.4 %shard_map.111 = bf16[8,240,768]{2,1,0:T(8,128)(2,1)} custom-call(bf16[384,1280]{1,0:T(8,128)(2,1)} %get-tuple-element.13.h_own_ref, bf16[384,1280]{1,0:T(8,128)(2,1)} %copy-done.2, bf16[240,1280]{1,0:T(8,128)(2,1)} %copy-done.3, bf16[240,1280]{1,0:T(8,128)(2,1)} %copy-done.4, bf16[128,1280]{1,0:T(8,128)(2,1)} %copy-done.5, ...), custom_call_target="tpu_custom_call", output_to_operand_aliasing={{}: (8, {})} | custom-call | flops 2000000000 | bytes 6000000 | tf_op jit(solution)/shard_map/pallas_call | solution.py:203
  60.4 3.9 %all-to-all-start = ((bf16[8,240,768]{2,1,0:T(8,128)(2,1)}), bf16[8,240,768]{2,1,0:T(8,128)(2,1)S(1)}, u32[]{:S(2)}, u32[]{:S(2)}) async-start(bf16[8,240,768]{2,1,0:T(8,128)(2,1)} %shard_map.111), calls=%async_computation | async-start | bytes 5898240 | tf_op jit(solution)/shard_map/all_to_all | solution.py:421
  65.0 34.3 %all-to-all-done.q_ref.all_ref = bf16[8,240,768]{2,1,0:T(8,128)(2,1)S(1)} async-done(((bf16[8,240,768]{2,1,0:T(8,128)(2,1)}), bf16[8,240,768]{2,1,0:T(8,128)(2,1)S(1)}, u32[]{:S(2)}, u32[]{:S(2)}) %all-to-all-start) | async-done | bytes 2949152 | tf_op jit(solution)/shard_map/all_to_all | solution.py:421
  99.3 1.6 copy-done
  100.9 59.4 %shard_map.113 = bf16[16,80,384]{2,1,0:T(8,128)(2,1)} custom-call(s32[1]{0:T(128)S(6)} %copy.14.count_ref, bf16[8,240,768]{2,1,0:T(8,128)(2,1)} %copy-done, bf16[8,240,768]{2,1,0:T(8,128)(2,1)} %copy-done), custom_call_target="tpu_custom_call" | custom-call | tf_op jit(solution)/shard_map/pallas_call | solution.py:302
  160.2 6.0 %all-to-all-start.1 = ((bf16[16,80,384]{2,1,0:T(8,128)(2,1)}), bf16[16,80,384]{2,1,0:T(8,128)(2,1)S(1)}, u32[]{:S(2)}, u32[]{:S(2)}) async-start(bf16[16,80,384]{2,1,0:T(8,128)(2,1)} %shard_map.113), calls=%async_computation.1 | async-start | bytes 1966080 | tf_op jit(solution)/shard_map/all_to_all | solution.py:427
  166.2 1.7 shard_map.112
  167.9 14.8 %all-to-all-done.1 = bf16[16,80,384]{2,1,0:T(8,128)(2,1)S(1)} async-done(((bf16[16,80,384]{2,1,0:T(8,128)(2,1)}), bf16[16,80,384]{2,1,0:T(8,128)(2,1)S(1)}, u32[]{:S(2)}, u32[]{:S(2)}) %all-to-all-start.1) | async-done | bytes 983072 | tf_op jit(solution)/shard_map/all_to_all | solution.py:427
  182.7 1.0 copy-done.1
  183.7 7.8 %shard_map.114 = bf16[1024,1408]{1,0:T(8,128)(2,1)} custom-call(s32[1,384]{1,0:T(1,128)} %get-tuple-element.18.bucket_ref, bf16[384,128]{1,0:T(8,128)(2,1)} %get-tuple-element.19.tag_ref, bf16[1280,384]{1,0:T(8,128)(2,1)} %bitcast.9, bf16[384,1280]{1,0:T(8,128)(2,1)} %get-tuple-element.20.x_ref, bf16[1280,1280]{1,0:T(8,128)(2,1)} %w_ref.1, ...), custom_call_target="tpu_custom_call" | custom-call | tf_op jit(solution)/shard_map/pallas_call | solution.py:336
  191.5 44.4 %all_to_all.15 = bf16[128,8,1408]{2,1,0:T(8,128)(2,1)} all-to-all(bf16[128,8,1408]{2,1,0:T(8,128)(2,1)} %bitcast.7), channel_id=1, replica_groups=mesh['ctx'=8,'img'=16] {'ctx','img'}, dimensions={0} | all-to-all | bytes 5767168 | tf_op jit(solution)/shard_map/all_to_all | solution.py:430
  235.9 4.0 %shard_map.115 = bf16[96,5120]{1,0:T(8,128)(2,1)} custom-call(bf16[1024,1408]{1,0:T(8,128)(2,1)} %bitcast.8), custom_call_target="tpu_custom_call" | custom-call | tf_op jit(solution)/shard_map/pallas_call | solution.py:359
  (26 shorter events, 0.1 us)
Async XLA Ops:
  0.0 24.5 %collective-permute-start.1 = (bf16[240,1280]{1,0:T(8,128)(2,1)}, bf16[240,1280]{1,0:T(8,128)(2,1)S(1)}, u32[]{:S(2)}, u32[]{:S(2)}) collective-permute-start(bf16[240,1280]{1,0:T(8,128)(2,1)} %bitcast.10), channel_id=1, source_target_pairs={{0,2},{1,3},{2,4},{3,5},{4,6},{5,7},{6,0},{7,1},{8,10},{9,11},{10,... | collective-permute-start | bytes 1843208 | tf_op jit(solution)/shard_map/ppermute | solution.py:151
  2.5 22.3 %collective-permute-start.3 = (bf16[240,1280]{1,0:T(8,128)(2,1)}, bf16[240,1280]{1,0:T(8,128)(2,1)S(1)}, u32[]{:S(2)}, u32[]{:S(2)}) collective-permute-start(bf16[240,1280]{1,0:T(8,128)(2,1)} %bitcast.11), channel_id=1, source_target_pairs={{0,6},{1,7},{2,0},{3,1},{4,2},{5,3},{6,4},{7,5},{8,14},{9,15},{10,... | collective-permute-start | bytes 1843208 | tf_op jit(solution)/shard_map/ppermute | solution.py:152
  4.6 22.9 %collective-permute-start.5 = (bf16[240,1280]{1,0:T(8,128)(2,1)}, bf16[240,1280]{1,0:T(8,128)(2,1)S(1)}, u32[]{:S(2)}, u32[]{:S(2)}) collective-permute-start(bf16[240,1280]{1,0:T(8,128)(2,1)} %bitcast.12), channel_id=1, source_target_pairs={{0,72},{1,73},{2,74},{3,75},{4,76},{5,77},{6,78},{7,79},{8,64},{9,... | collective-permute-start | bytes 1843208 | tf_op jit(solution)/shard_map/ppermute | solution.py:153
  23.2 17.5 %collective-permute-start = (bf16[384,1280]{1,0:T(8,128)(2,1)}, bf16[384,1280]{1,0:T(8,128)(2,1)S(1)}, u32[]{:S(2)}, u32[]{:S(2)}) collective-permute-start(bf16[384,1280]{1,0:T(8,128)(2,1)} %get-tuple-element.13.h_own_ref), channel_id=1, source_target_pairs={{0,1},{1,0},{2,3},{3,2},{4,5},{5,4},{6,7},{7,6},{8,9},{9,8},{10,11... | collective-permute-start | bytes 2949128 | tf_op jit(solution)/shard_map/ppermute | solution.py:415
  24.5 16.2 %copy-start.9 = (bf16[240,1280]{1,0:T(8,128)(2,1)}, bf16[240,1280]{1,0:T(8,128)(2,1)S(1)}, u32[]{:S(2)}) copy-start(bf16[240,1280]{1,0:T(8,128)(2,1)S(1)} %collective-permute-done.1.refs_1_) | copy-start | bytes 1843204
  24.5 10.8 %collective-permute-start.2 = (bf16[128,1280]{1,0:T(8,128)(2,1)S(1)}, bf16[128,1280]{1,0:T(8,128)(2,1)S(1)}, u32[]{:S(2)}, u32[]{:S(2)}) collective-permute-start(bf16[128,1280]{1,0:T(8,128)(2,1)S(1)} %slice.8), channel_id=1, source_target_pairs={{0,2},{1,3},{2,4},{3,5},{4,6},{5,7},{6,0},{7,1},{8,10},{9,11},{10,... | collective-permute-start | bytes 983048 | tf_op jit(solution)/shard_map/ppermute | solution.py:160
  24.8 15.9 %copy-start.10 = (bf16[240,1280]{1,0:T(8,128)(2,1)}, bf16[240,1280]{1,0:T(8,128)(2,1)S(1)}, u32[]{:S(2)}) copy-start(bf16[240,1280]{1,0:T(8,128)(2,1)S(1)} %collective-permute-done.3.refs_2_) | copy-start | bytes 1843204
  24.8 8.6 %collective-permute-start.4 = (bf16[112,1280]{1,0:T(8,128)(2,1)S(1)}, bf16[112,1280]{1,0:T(8,128)(2,1)S(1)}, u32[]{:S(2)}, u32[]{:S(2)}) collective-permute-start(bf16[112,1280]{1,0:T(8,128)(2,1)S(1)} %slice.9), channel_id=1, source_target_pairs={{0,6},{1,7},{2,0},{3,1},{4,2},{5,3},{6,4},{7,5},{8,14},{9,15},{10,... | collective-permute-start | bytes 860168 | tf_op jit(solution)/shard_map/ppermute | solution.py:161
  27.5 13.1 %copy-start.11 = (bf16[240,1280]{1,0:T(8,128)(2,1)}, bf16[240,1280]{1,0:T(8,128)(2,1)S(1)}, u32[]{:S(2)}) copy-start(bf16[240,1280]{1,0:T(8,128)(2,1)S(1)} %collective-permute-done.5.refs_3_) | copy-start | bytes 1843204
  33.4 19.7 %copy-start.7 = (bf16[112,1280]{1,0:T(8,128)(2,1)}, bf16[112,1280]{1,0:T(8,128)(2,1)S(1)}, u32[]{:S(2)}) copy-start(bf16[112,1280]{1,0:T(8,128)(2,1)S(1)} %collective-permute-done.4.refs_3_) | copy-start | bytes 860164
  35.3 17.9 %copy-start.5 = (bf16[128,1280]{1,0:T(8,128)(2,1)}, bf16[128,1280]{1,0:T(8,128)(2,1)S(1)}, u32[]{:S(2)}) copy-start(bf16[128,1280]{1,0:T(8,128)(2,1)S(1)} %collective-permute-done.2.refs_2_) | copy-start | bytes 983044
  35.3 17.9 %collective-permute-start.6 = (bf16[240,1280]{1,0:T(8,128)(2,1)S(1)}, bf16[240,1280]{1,0:T(8,128)(2,1)S(1)}, u32[]{:S(2)}, u32[]{:S(2)}) collective-permute-start(bf16[240,1280]{1,0:T(8,128)(2,1)S(1)} %collective-permute-done.5.refs_3_), channel_id=1, source_target_pairs={{0,2},{1,3},{2,4},{3,5},{4,6},{5,7},{6,0},{7,1},{8,10},{9,11},{10,... | collective-permute-start | bytes 1843208 | tf_op jit(solution)/shard_map/ppermute | solution.py:165
  35.3 17.9 %collective-permute-start.7 = (bf16[240,1280]{1,0:T(8,128)(2,1)S(1)}, bf16[240,1280]{1,0:T(8,128)(2,1)S(1)}, u32[]{:S(2)}, u32[]{:S(2)}) collective-permute-start(bf16[240,1280]{1,0:T(8,128)(2,1)S(1)} %collective-permute-done.5.refs_3_), channel_id=1, source_target_pairs={{0,6},{1,7},{2,0},{3,1},{4,2},{5,3},{6,4},{7,5},{8,14},{9,15},{10,... | collective-permute-start | bytes 1843208 | tf_op jit(solution)/shard_map/ppermute | solution.py:166
  38.0 15.2 %collective-permute-start.8 = (bf16[128,1280]{1,0:T(8,128)(2,1)S(1)}, bf16[128,1280]{1,0:T(8,128)(2,1)S(1)}, u32[]{:S(2)}, u32[]{:S(2)}) collective-permute-start(bf16[128,1280]{1,0:T(8,128)(2,1)S(1)} %collective-permute-done.2.refs_2_), channel_id=1, source_target_pairs={{0,72},{1,73},{2,74},{3,75},{4,76},{5,77},{6,78},{7,79},{8,64},{9,... | collective-permute-start | bytes 983048 | tf_op jit(solution)/shard_map/ppermute | solution.py:163
  38.2 15.0 %collective-permute-start.9 = (bf16[112,1280]{1,0:T(8,128)(2,1)S(1)}, bf16[112,1280]{1,0:T(8,128)(2,1)S(1)}, u32[]{:S(2)}, u32[]{:S(2)}) collective-permute-start(bf16[112,1280]{1,0:T(8,128)(2,1)S(1)} %collective-permute-done.4.refs_3_), channel_id=1, source_target_pairs={{0,72},{1,73},{2,74},{3,75},{4,76},{5,77},{6,78},{7,79},{8,64},{9,... | collective-permute-start | bytes 860168 | tf_op jit(solution)/shard_map/ppermute | solution.py:164
  40.7 0.9 copy-start.2
  53.1 0.7 copy-start.8
  53.1 0.9 copy-start.6
  53.2 1.1 copy-start.3
  54.2 0.8 copy-start.4
  60.4 38.8 %all-to-all-start = ((bf16[8,240,768]{2,1,0:T(8,128)(2,1)}), bf16[8,240,768]{2,1,0:T(8,128)(2,1)S(1)}, u32[]{:S(2)}, u32[]{:S(2)}) async-start(bf16[8,240,768]{2,1,0:T(8,128)(2,1)} %shard_map.111), calls=%async_computation | async-start | bytes 5898240 | tf_op jit(solution)/shard_map/all_to_all | solution.py:421
  99.3 1.6 copy-start
  160.2 22.5 %all-to-all-start.1 = ((bf16[16,80,384]{2,1,0:T(8,128)(2,1)}), bf16[16,80,384]{2,1,0:T(8,128)(2,1)S(1)}, u32[]{:S(2)}, u32[]{:S(2)}) async-start(bf16[16,80,384]{2,1,0:T(8,128)(2,1)} %shard_map.113), calls=%async_computation.1 | async-start | bytes 1966080 | tf_op jit(solution)/shard_map/all_to_all | solution.py:427
  182.7 1.0 copy-start.1

commit v5 on v4

--- a/solution.py
+++ b/solution.py
@@ -15,6 +15,8 @@
 F32 = jnp.float32
 BF16 = jnp.bfloat16
 Q_SCALE = HEAD_DIM ** (-0.5) * math.log2(math.e)
+WINDOW = 64
+QUERY_BLOCK = 384
 TAG = 128
 SAFE_BOUND = 64.0
 SAFE_VALUE = 2.0**40
@@ -45,18 +47,19 @@
 
     @pl.when(step == 0)
     def _():
+        h_ref[...] = normed(x_ref[0], gain_one_ref[...]).astype(BF16)
+
+    def project_one(scale=None):
+        product = jnp.dot(h_ref[...], w_qkv_ref[0], preferred_element_type=F32)
+        return (product if scale is None else product * scale).astype(BF16)
+
+    @pl.when(step == 0)
+    def _():
+        q_ref[...] = project_one(Q_SCALE)
+
+    @pl.when(step == 1)
+    def _():
         copy.start()
-        h_ref[...] = normed(x_ref[0], gain_one_ref[...]).astype(BF16)
-
-    def project_one():
-        return jnp.dot(h_ref[...], w_qkv_ref[0], preferred_element_type=F32).astype(BF16)
-
-    @pl.when(step == 0)
-    def _():
-        q_ref[...] = project_one()
-
-    @pl.when(step == 1)
-    def _():
         k_ref[...] = project_one()
 
     @pl.when(step == 2)
@@ -64,29 +67,46 @@
         values_all = project_one()
         rows = ids_ref.shape[1]
         ids = jnp.broadcast_to(ids_ref[...], (8, rows))
-        allowed = ids.T[:, 0:1] == ids[0:1]
+        ids_column = ids.T[:, 0:1]
+        spans = []
+        for start in range(0, rows, QUERY_BLOCK):
+            begin = max(start - WINDOW, 0)
+            end = min(start + QUERY_BLOCK + WINDOW, rows)
+            allowed = ids_column[start : start + QUERY_BLOCK] == ids[0:1, begin:end]
+            spans.append((start, begin, end, allowed))
         tiles = {}
-        for head in range(D // HEAD_DIM):
-            begin, end = head * HEAD_DIM, (head + 1) * HEAD_DIM
-            low, high = begin // 128 * 128, (end + 127) // 128 * 128
+        allowed = spans[0][3]
+
+        def window(head):
+            first, last = head * HEAD_DIM, (head + 1) * HEAD_DIM
+            low, high = first // 128 * 128, (last + 127) // 128 * 128
             lane = low + lax.broadcasted_iota(jnp.int32, (1, high - low), 1)
-            mine = (lane >= begin) & (lane < end)
+            return low, high, last, (lane >= first) & (lane < last)
+
+        def score(head):
+            low, high, last, mine = window(head)
             keys = jnp.where(mine, k_ref[:, low:high], 0.0).astype(BF16)
-            values = values_all[:, low:high]
-            scores = lax.dot_general(
-                q_ref[:, low:high], keys, NT, preferred_element_type=F32
-            ) * HEAD_DIM ** (-0.5)
-            scores = jnp.where(allowed, scores, MASKED_SCORE)
+            return lax.dot_general(q_ref[:, low:high], keys, NT, preferred_element_type=F32)
+
+        heads = D // HEAD_DIM
+        ahead = score(0)
+        for head in range(heads):
+            scores = jnp.where(allowed, ahead, MASKED_SCORE)
+            if head + 1 < heads:
+                ahead = score(head + 1)
+            low, high, last, mine = window(head)
             most = jnp.max(scores, axis=1, keepdims=True)
-            weights = jnp.exp(scores - most)
+            weights = jnp.exp2(scores - most)
             total = jnp.sum(weights, axis=1, keepdims=True)
-            result = jnp.dot(weights.astype(BF16), values, preferred_element_type=F32) / total
+            result = jnp.dot(
+                weights.astype(BF16), values_all[:, low:high], preferred_element_type=F32
+            ) * (1.0 / total)
             for tile in range(low, high, 128):
                 piece = result[:, tile - low : tile - low + 128]
                 if tile in tiles:
                     piece = jnp.where(mine[:, tile - low : tile - low + 128], piece, tiles[tile])
                 tiles[tile] = piece
-                if tile + 128 <= end:
+                if tile + 128 <= last:
                     a_ref[:, tile : tile + 128] = tiles.pop(tile).astype(BF16)
         copy.wait()
         second = x_ref[0].astype(F32) + jnp.dot(
@@ -143,8 +163,8 @@
 X_OTHER = device_perm(lambda x, y, z, core: (OTHER_X[x], y, z, core))
 CORE_SWAP = device_perm(lambda x, y, z, core: (x, y, z, 1 - core))
 BOTH = ("ctx", "img")
-NEAR_OFFSETS = ((0, 0), (0, -1), (0, 1), (1, 0))
-FAR_OFFSETS = ((1, -1), (1, 1), (0, 2), (1, 2))
+NEAR_OFFSETS = ((0, 0), (0, -1), (0, 1), (1, 0), (0, 2))
+FAR_OFFSETS = ((1, -1), (1, 1), (1, 2))
 
 
 def near_shards(shard):
@@ -164,7 +184,7 @@
     other_far_bottom = lax.ppermute(far_bottom, BOTH, X_OTHER)
     other_below = lax.ppermute(other, BOTH, Z_UP)
     other_above = lax.ppermute(other, BOTH, Z_DOWN)
-    return [other_below, other_above, far_top, far_bottom, other_far_top, other_far_bottom]
+    return [far_top, far_bottom], [other_below, other_above, other_far_top, other_far_bottom]
 
 
 def project_kernel(h_own_ref, h_partner_ref, *refs, parts, offsets, aliased):
@@ -408,15 +428,13 @@
 ):
     shard = jnp.swapaxes(w_qkv2, 1, 2).reshape(3 * HEAD_DIM, D)
     near = near_shards(shard)
-    far = far_shards(near)
+    far, last = far_shards(near)
 
     second, hidden = layer_one(window_ids, patches, gain_one, gain_two, w_qkv1, w_out1)
 
     partner = lax.ppermute(hidden, BOTH, CORE_SWAP)
-    projected = project(NEAR_OFFSETS, hidden, partner, near, (1, 1, 1, 1))
-    projected = project(
-        FAR_OFFSETS, hidden, partner, far, (1, 1, 2, 2), into=projected
-    )
+    projected = project(NEAR_OFFSETS, hidden, partner, near + far, (1, 1, 1, 1, 2))
+    projected = project(FAR_OFFSETS, hidden, partner, last, (1, 1, 2), into=projected)
     groups = [[2 * chip + core for chip in range(8)] for core in range(2)]
     received = lax.all_to_all(
         projected, "img", split_axis=0, concat_axis=0, tiled=True, axis_index_groups=groups

time: 240 us -> 238 us (level)
  transfers between devices with their start and end apart: 12 -> 12, of which waited for: 5 -> 5; matrix products, arithmetic and copies ran while one was open for 0% -> 0% of each run, Pallas kernels for 10% -> 9%
where the time goes in v5:
time: 238 us; the launch traced here: 237 us
  Pallas kernels  98 us (41%)
  waiting for transfers between devices  62.3 us (26%)
  blocking collectives  44.4 us (19%)
  starting transfers between devices  26.4 us (11%)
  local copies, waits for them, and re-layouts  5.45 us (2%)
    pallas_call x1, Pallas kernels, attend_full(): pl.pallas_call(functools.partial(attention_kernel, block=512), out_shape=...  59.4 us
    all_to_all x1, blocking collectives, on_device(): lax.all_to_all(send.reshape(128, 8, D + TAG), BOTH, split_axis=0, concat_...  44.4 us
    all_to_all x1, waiting for transfers between devices, on_device(): lax.all_to_all(projected, 'img', split_axis=0, concat_axis=0, tiled=True,...  34.3 us
    all_to_all x1, waiting for transfers between devices, on_device(): lax.all_to_all(attended, 'img', split_axis=0, concat_axis=0, tiled=True)  14.8 us
    pallas_call x1, Pallas kernels, layer_one(): pl.pallas_call(layer_one_kernel, out_shape=[jax.ShapeDtypeStruct((rows, D...  14.4 us
    pallas_call x2, Pallas kernels, project(): pl.pallas_call(functools.partial(project_kernel, parts=parts, offsets=off...  10.8 us
    pallas_call x1, Pallas kernels, merge(): pl.pallas_call(merge_kernel, out_shape=jax.ShapeDtypeStruct((places, D +...  7.78 us
    all_to_all x1, starting transfers between devices, on_device(): lax.all_to_all(attended, 'img', split_axis=0, concat_axis=0, tiled=True)  5.99 us
  transfers between devices with their start and end apart: 12, of which 5 were waited for; matrix products, arithmetic and copies ran while one was open for 0% of the time, Pallas kernels for 9%

profile of v5, /device:TPU:1, one launch (start us, length us, event | category | flops | bytes accessed | tf_op | source)
XLA Modules:
  0.0 237.3 jit_solution(2002577169668063351)
XLA Ops:
  0.0 2.5 %collective-permute-start.1 = (bf16[240,1280]{1,0:T(8,128)(2,1)}, bf16[240,1280]{1,0:T(8,128)(2,1)S(1)}, u32[]{:S(2)}, u32[]{:S(2)}) collective-permute-start(bf16[240,1280]{1,0:T(8,128)(2,1)} %bitcast.10), channel_id=1, source_target_pairs={{0,2},{1,3},{2,4},{3,5},{4,6},{5,7},{6,0},{7,1},{8,10},{9,11},{10,... | collective-permute-start | bytes 1843208 | tf_op jit(solution)/shard_map/ppermute | solution.py:171
  2.5 2.1 collective-permute-start.3
  4.6 2.5 %collective-permute-start.5 = (bf16[240,1280]{1,0:T(8,128)(2,1)}, bf16[240,1280]{1,0:T(8,128)(2,1)S(1)}, u32[]{:S(2)}, u32[]{:S(2)}) collective-permute-start(bf16[240,1280]{1,0:T(8,128)(2,1)} %bitcast.12), channel_id=1, source_target_pairs={{0,72},{1,73},{2,74},{3,75},{4,76},{5,77},{6,78},{7,79},{8,64},{9,... | collective-permute-start | bytes 1843208 | tf_op jit(solution)/shard_map/ppermute | solution.py:173
  7.1 14.4 %shard_map.109 = (bf16[384,1280]{1,0:T(8,128)(2,1)}, bf16[384,1280]{1,0:T(8,128)(2,1)}) custom-call(s32[1,384]{1,0:T(1,128)} %ids_ref.1, bf16[1,384,1280]{2,1,0:T(8,128)(2,1)} %x_ref.1, bf16[1280]{0:T(1024)(128)(2,1)} %gain_one_ref.1, bf16[1280]{0:T(1024)(128)(2,1)} %gain_two_ref.1, bf16[3,1280,1280]{2,1,0:T(8,128)(2,1)} %w_qkv_ref.1, ...), custom_call_target="tpu_custom_call" | custom-call | flops 6000000000 | bytes 16000000 | tf_op jit(solution)/shard_map/pallas_call | solution.py:123
  21.5 1.3 collective-permute-start
  22.8 0.1 collective-permute-start.2
  23.0 2.7 %collective-permute-start.4 = (bf16[112,1280]{1,0:T(8,128)(2,1)S(1)}, bf16[112,1280]{1,0:T(8,128)(2,1)S(1)}, u32[]{:S(2)}, u32[]{:S(2)}) collective-permute-start(bf16[112,1280]{1,0:T(8,128)(2,1)S(1)} %slice.9), channel_id=1, source_target_pairs={{0,6},{1,7},{2,0},{3,1},{4,2},{5,3},{6,4},{7,5},{8,14},{9,15},{10,... | collective-permute-start | bytes 860168 | tf_op jit(solution)/shard_map/ppermute | solution.py:181
  25.7 0.0 collective-permute-done.5.refs_3_
  25.7 5.9 %collective-permute-done.4.refs_5_ = bf16[112,1280]{1,0:T(8,128)(2,1)S(1)} collective-permute-done((bf16[112,1280]{1,0:T(8,128)(2,1)S(1)}, bf16[112,1280]{1,0:T(8,128)(2,1)S(1)}, u32[]{:S(2)}, u32[]{:S(2)}) %collective-permute-start.4) | collective-permute-done | bytes 286752 | tf_op jit(solution)/shard_map/ppermute | solution.py:181
  31.6 1.8 collective-permute-done.2.refs_4_
  33.4 2.7 %collective-permute-start.7 = (bf16[240,1280]{1,0:T(8,128)(2,1)S(1)}, bf16[240,1280]{1,0:T(8,128)(2,1)S(1)}, u32[]{:S(2)}, u32[]{:S(2)}) collective-permute-start(bf16[240,1280]{1,0:T(8,128)(2,1)S(1)} %collective-permute-done.5.refs_3_), channel_id=1, source_target_pairs={{0,6},{1,7},{2,0},{3,1},{4,2},{5,3},{6,4},{7,5},{8,14},{9,15},{10,... | collective-permute-start | bytes 1843208 | tf_op jit(solution)/shard_map/ppermute | solution.py:186
  36.1 0.2 collective-permute-start.8
  36.3 2.5 %collective-permute-start.9 = (bf16[112,1280]{1,0:T(8,128)(2,1)S(1)}, bf16[112,1280]{1,0:T(8,128)(2,1)S(1)}, u32[]{:S(2)}, u32[]{:S(2)}) collective-permute-start(bf16[112,1280]{1,0:T(8,128)(2,1)S(1)} %collective-permute-done.4.refs_5_), channel_id=1, source_target_pairs={{0,72},{1,73},{2,74},{3,75},{4,76},{5,77},{6,78},{7,79},{8,64},{9,... | collective-permute-start | bytes 860168 | tf_op jit(solution)/shard_map/ppermute | solution.py:184
  38.8 0.9 copy-done.1
  39.8 6.1 %shard_map.110.refs_4_ = bf16[8,240,768]{2,1,0:T(8,128)(2,1)} custom-call(bf16[384,1280]{1,0:T(8,128)(2,1)} %get-tuple-element.13.h_own_ref, bf16[384,1280]{1,0:T(8,128)(2,1)} %copy-done.1, bf16[240,1280]{1,0:T(8,128)(2,1)} %bitcast.13, bf16[240,1280]{1,0:T(8,128)(2,1)} %copy-done.3, bf16[240,1280]{1,0:T(8,128)(2,1)} %copy-done.4, ...), custom_call_target="tpu_custom_call" | custom-call | flops 2000000000 | bytes 6000000 | tf_op jit(solution)/shard_map/pallas_call | solution.py:223
  45.9 5.4 %collective-permute-done.9.refs_3_ = bf16[112,1280]{1,0:T(8,128)(2,1)S(1)} collective-permute-done((bf16[112,1280]{1,0:T(8,128)(2,1)S(1)}, bf16[112,1280]{1,0:T(8,128)(2,1)S(1)}, u32[]{:S(2)}, u32[]{:S(2)}) %collective-permute-start.9) | collective-permute-done | bytes 286752 | tf_op jit(solution)/shard_map/ppermute | solution.py:184
  51.3 0.7 copy-done.11
  52.0 0.1 copy-done.9
  52.1 0.2 copy-done.6
  52.4 0.8 copy-done.7
  53.2 4.6 %shard_map.111 = bf16[8,240,768]{2,1,0:T(8,128)(2,1)} custom-call(bf16[384,1280]{1,0:T(8,128)(2,1)} %get-tuple-element.13.h_own_ref, bf16[384,1280]{1,0:T(8,128)(2,1)} %copy-done.1, bf16[240,1280]{1,0:T(8,128)(2,1)} %copy-done.6, bf16[240,1280]{1,0:T(8,128)(2,1)} %copy-done.7, bf16[128,1280]{1,0:T(8,128)(2,1)} %copy-done.9, ...), custom_call_target="tpu_custom_call", output_to_operand_aliasing={{}: (6, {})} | custom-call | flops 2000000000 | bytes 6000000 | tf_op jit(solution)/shard_map/pallas_call | solution.py:223
  57.9 3.9 %all-to-all-start = ((bf16[8,240,768]{2,1,0:T(8,128)(2,1)}), bf16[8,240,768]{2,1,0:T(8,128)(2,1)S(1)}, u32[]{:S(2)}, u32[]{:S(2)}) async-start(bf16[8,240,768]{2,1,0:T(8,128)(2,1)} %shard_map.111), calls=%async_computation | async-start | bytes 5898240 | tf_op jit(solution)/shard_map/all_to_all | solution.py:439
  62.4 34.3 %all-to-all-done.q_ref.all_ref = bf16[8,240,768]{2,1,0:T(8,128)(2,1)S(1)} async-done(((bf16[8,240,768]{2,1,0:T(8,128)(2,1)}), bf16[8,240,768]{2,1,0:T(8,128)(2,1)S(1)}, u32[]{:S(2)}, u32[]{:S(2)}) %all-to-all-start) | async-done | bytes 2949152 | tf_op jit(solution)/shard_map/all_to_all | solution.py:439
  96.7 1.6 copy-done
  98.3 59.4 %shard_map.113 = bf16[16,80,384]{2,1,0:T(8,128)(2,1)} custom-call(s32[1]{0:T(128)S(6)} %copy.14.count_ref, bf16[8,240,768]{2,1,0:T(8,128)(2,1)} %copy-done, bf16[8,240,768]{2,1,0:T(8,128)(2,1)} %copy-done), custom_call_target="tpu_custom_call" | custom-call | tf_op jit(solution)/shard_map/pallas_call | solution.py:322
  157.7 6.0 %all-to-all-start.1 = ((bf16[16,80,384]{2,1,0:T(8,128)(2,1)}), bf16[16,80,384]{2,1,0:T(8,128)(2,1)S(1)}, u32[]{:S(2)}, u32[]{:S(2)}) async-start(bf16[16,80,384]{2,1,0:T(8,128)(2,1)} %shard_map.113), calls=%async_computation.1 | async-start | bytes 1966080 | tf_op jit(solution)/shard_map/all_to_all | solution.py:445
  163.7 1.7 shard_map.112
  165.3 14.8 %all-to-all-done.1 = bf16[16,80,384]{2,1,0:T(8,128)(2,1)S(1)} async-done(((bf16[16,80,384]{2,1,0:T(8,128)(2,1)}), bf16[16,80,384]{2,1,0:T(8,128)(2,1)S(1)}, u32[]{:S(2)}, u32[]{:S(2)}) %all-to-all-start.1) | async-done | bytes 983072 | tf_op jit(solution)/shard_map/all_to_all | solution.py:445
  180.2 1.0 copy-done.2
  181.1 7.8 %shard_map.114 = bf16[1024,1408]{1,0:T(8,128)(2,1)} custom-call(s32[1,384]{1,0:T(1,128)} %get-tuple-element.18.bucket_ref, bf16[384,128]{1,0:T(8,128)(2,1)} %get-tuple-element.19.tag_ref, bf16[1280,384]{1,0:T(8,128)(2,1)} %bitcast.9, bf16[384,1280]{1,0:T(8,128)(2,1)} %get-tuple-element.20.x_ref, bf16[1280,1280]{1,0:T(8,128)(2,1)} %w_ref.1, ...), custom_call_target="tpu_custom_call" | custom-call | tf_op jit(solution)/shard_map/pallas_call | solution.py:356
  188.9 44.4 %all_to_all.15 = bf16[128,8,1408]{2,1,0:T(8,128)(2,1)} all-to-all(bf16[128,8,1408]{2,1,0:T(8,128)(2,1)} %bitcast.7), channel_id=1, replica_groups=mesh['ctx'=8,'img'=16] {'ctx','img'}, dimensions={0} | all-to-all | bytes 5767168 | tf_op jit(solution)/shard_map/all_to_all | solution.py:448
  233.3 4.0 %shard_map.115 = bf16[96,5120]{1,0:T(8,128)(2,1)} custom-call(bf16[1024,1408]{1,0:T(8,128)(2,1)} %bitcast.8), custom_call_target="tpu_custom_call" | custom-call | tf_op jit(solution)/shard_map/pallas_call | solution.py:379
  (26 shorter events, 0.1 us)
Async XLA Ops:
  0.0 22.8 %collective-permute-start.1 = (bf16[240,1280]{1,0:T(8,128)(2,1)}, bf16[240,1280]{1,0:T(8,128)(2,1)S(1)}, u32[]{:S(2)}, u32[]{:S(2)}) collective-permute-start(bf16[240,1280]{1,0:T(8,128)(2,1)} %bitcast.10), channel_id=1, source_target_pairs={{0,2},{1,3},{2,4},{3,5},{4,6},{5,7},{6,0},{7,1},{8,10},{9,11},{10,... | collective-permute-start | bytes 1843208 | tf_op jit(solution)/shard_map/ppermute | solution.py:171
  2.5 20.5 %collective-permute-start.3 = (bf16[240,1280]{1,0:T(8,128)(2,1)}, bf16[240,1280]{1,0:T(8,128)(2,1)S(1)}, u32[]{:S(2)}, u32[]{:S(2)}) collective-permute-start(bf16[240,1280]{1,0:T(8,128)(2,1)} %bitcast.11), channel_id=1, source_target_pairs={{0,6},{1,7},{2,0},{3,1},{4,2},{5,3},{6,4},{7,5},{8,14},{9,15},{10,... | collective-permute-start | bytes 1843208 | tf_op jit(solution)/shard_map/ppermute | solution.py:172
  4.6 21.1 %collective-permute-start.5 = (bf16[240,1280]{1,0:T(8,128)(2,1)}, bf16[240,1280]{1,0:T(8,128)(2,1)S(1)}, u32[]{:S(2)}, u32[]{:S(2)}) collective-permute-start(bf16[240,1280]{1,0:T(8,128)(2,1)} %bitcast.12), channel_id=1, source_target_pairs={{0,72},{1,73},{2,74},{3,75},{4,76},{5,77},{6,78},{7,79},{8,64},{9,... | collective-permute-start | bytes 1843208 | tf_op jit(solution)/shard_map/ppermute | solution.py:173
  21.5 17.3 %collective-permute-start = (bf16[384,1280]{1,0:T(8,128)(2,1)}, bf16[384,1280]{1,0:T(8,128)(2,1)S(1)}, u32[]{:S(2)}, u32[]{:S(2)}) collective-permute-start(bf16[384,1280]{1,0:T(8,128)(2,1)} %get-tuple-element.13.h_own_ref), channel_id=1, source_target_pairs={{0,1},{1,0},{2,3},{3,2},{4,5},{5,4},{6,7},{7,6},{8,9},{9,8},{10,11... | collective-permute-start | bytes 2949128 | tf_op jit(solution)/shard_map/ppermute | solution.py:435
  22.8 16.0 %copy-start.3 = (bf16[240,1280]{1,0:T(8,128)(2,1)}, bf16[240,1280]{1,0:T(8,128)(2,1)S(1)}, u32[]{:S(2)}) copy-start(bf16[240,1280]{1,0:T(8,128)(2,1)S(1)} %collective-permute-done.1.refs_1_) | copy-start | bytes 1843204
  22.8 10.6 %collective-permute-start.2 = (bf16[128,1280]{1,0:T(8,128)(2,1)S(1)}, bf16[128,1280]{1,0:T(8,128)(2,1)S(1)}, u32[]{:S(2)}, u32[]{:S(2)}) collective-permute-start(bf16[128,1280]{1,0:T(8,128)(2,1)S(1)} %slice.8), channel_id=1, source_target_pairs={{0,2},{1,3},{2,4},{3,5},{4,6},{5,7},{6,0},{7,1},{8,10},{9,11},{10,... | collective-permute-start | bytes 983048 | tf_op jit(solution)/shard_map/ppermute | solution.py:180
  22.9 15.9 %copy-start.4 = (bf16[240,1280]{1,0:T(8,128)(2,1)}, bf16[240,1280]{1,0:T(8,128)(2,1)S(1)}, u32[]{:S(2)}) copy-start(bf16[240,1280]{1,0:T(8,128)(2,1)S(1)} %collective-permute-done.3.refs_2_) | copy-start | bytes 1843204
  23.0 8.6 %collective-permute-start.4 = (bf16[112,1280]{1,0:T(8,128)(2,1)S(1)}, bf16[112,1280]{1,0:T(8,128)(2,1)S(1)}, u32[]{:S(2)}, u32[]{:S(2)}) collective-permute-start(bf16[112,1280]{1,0:T(8,128)(2,1)S(1)} %slice.9), channel_id=1, source_target_pairs={{0,6},{1,7},{2,0},{3,1},{4,2},{5,3},{6,4},{7,5},{8,14},{9,15},{10,... | collective-permute-start | bytes 860168 | tf_op jit(solution)/shard_map/ppermute | solution.py:181
  25.7 13.1 %copy-start.5 = (bf16[240,1280]{1,0:T(8,128)(2,1)}, bf16[240,1280]{1,0:T(8,128)(2,1)S(1)}, u32[]{:S(2)}) copy-start(bf16[240,1280]{1,0:T(8,128)(2,1)S(1)} %collective-permute-done.5.refs_3_) | copy-start | bytes 1843204
  31.6 7.2 %copy-start.10 = (bf16[112,1280]{1,0:T(8,128)(2,1)}, bf16[112,1280]{1,0:T(8,128)(2,1)S(1)}, u32[]{:S(2)}) copy-start(bf16[112,1280]{1,0:T(8,128)(2,1)S(1)} %collective-permute-done.4.refs_5_) | copy-start | bytes 860164
  33.4 5.4 %copy-start.8 = (bf16[128,1280]{1,0:T(8,128)(2,1)}, bf16[128,1280]{1,0:T(8,128)(2,1)S(1)}, u32[]{:S(2)}) copy-start(bf16[128,1280]{1,0:T(8,128)(2,1)S(1)} %collective-permute-done.2.refs_4_) | copy-start | bytes 983044
  33.4 17.9 %collective-permute-start.6 = (bf16[240,1280]{1,0:T(8,128)(2,1)S(1)}, bf16[240,1280]{1,0:T(8,128)(2,1)S(1)}, u32[]{:S(2)}, u32[]{:S(2)}) collective-permute-start(bf16[240,1280]{1,0:T(8,128)(2,1)S(1)} %collective-permute-done.5.refs_3_), channel_id=1, source_target_pairs={{0,2},{1,3},{2,4},{3,5},{4,6},{5,7},{6,0},{7,1},{8,10},{9,11},{10,... | collective-permute-start | bytes 1843208 | tf_op jit(solution)/shard_map/ppermute | solution.py:185
  33.4 17.9 %collective-permute-start.7 = (bf16[240,1280]{1,0:T(8,128)(2,1)S(1)}, bf16[240,1280]{1,0:T(8,128)(2,1)S(1)}, u32[]{:S(2)}, u32[]{:S(2)}) collective-permute-start(bf16[240,1280]{1,0:T(8,128)(2,1)S(1)} %collective-permute-done.5.refs_3_), channel_id=1, source_target_pairs={{0,6},{1,7},{2,0},{3,1},{4,2},{5,3},{6,4},{7,5},{8,14},{9,15},{10,... | collective-permute-start | bytes 1843208 | tf_op jit(solution)/shard_map/ppermute | solution.py:186
  36.1 15.2 %collective-permute-start.8 = (bf16[128,1280]{1,0:T(8,128)(2,1)S(1)}, bf16[128,1280]{1,0:T(8,128)(2,1)S(1)}, u32[]{:S(2)}, u32[]{:S(2)}) collective-permute-start(bf16[128,1280]{1,0:T(8,128)(2,1)S(1)} %collective-permute-done.2.refs_4_), channel_id=1, source_target_pairs={{0,72},{1,73},{2,74},{3,75},{4,76},{5,77},{6,78},{7,79},{8,64},{9,... | collective-permute-start | bytes 983048 | tf_op jit(solution)/shard_map/ppermute | solution.py:183
  36.3 15.0 %collective-permute-start.9 = (bf16[112,1280]{1,0:T(8,128)(2,1)S(1)}, bf16[112,1280]{1,0:T(8,128)(2,1)S(1)}, u32[]{:S(2)}, u32[]{:S(2)}) collective-permute-start(bf16[112,1280]{1,0:T(8,128)(2,1)S(1)} %collective-permute-done.4.refs_5_), channel_id=1, source_target_pairs={{0,72},{1,73},{2,74},{3,75},{4,76},{5,77},{6,78},{7,79},{8,64},{9,... | collective-permute-start | bytes 860168 | tf_op jit(solution)/shard_map/ppermute | solution.py:184
  38.8 0.9 copy-start.1
  51.3 0.7 copy-start.11
  51.3 0.9 copy-start.9
  51.3 1.1 copy-start.6
  52.4 0.8 copy-start.7
  57.9 38.8 %all-to-all-start = ((bf16[8,240,768]{2,1,0:T(8,128)(2,1)}), bf16[8,240,768]{2,1,0:T(8,128)(2,1)S(1)}, u32[]{:S(2)}, u32[]{:S(2)}) async-start(bf16[8,240,768]{2,1,0:T(8,128)(2,1)} %shard_map.111), calls=%async_computation | async-start | bytes 5898240 | tf_op jit(solution)/shard_map/all_to_all | solution.py:439
  96.7 1.6 copy-start
  157.7 22.5 %all-to-all-start.1 = ((bf16[16,80,384]{2,1,0:T(8,128)(2,1)}), bf16[16,80,384]{2,1,0:T(8,128)(2,1)S(1)}, u32[]{:S(2)}, u32[]{:S(2)}) async-start(bf16[16,80,384]{2,1,0:T(8,128)(2,1)} %shard_map.113), calls=%async_computation.1 | async-start | bytes 1966080 | tf_op jit(solution)/shard_map/all_to_all | solution.py:445
  180.2 1.0 copy-start.2

commit v6 on v5

--- a/solution.py
+++ b/solution.py
@@ -21,6 +21,7 @@
 SAFE_BOUND = 64.0
 SAFE_VALUE = 2.0**40
 VMEM_LIMIT = 56 * 1024 * 1024
+VMEM_ALL = 63 * 1024 * 1024
 NT = (((1,), (1,)), ((), ()))
 TN = (((0,), (0,)), ((), ()))
 
@@ -192,17 +193,23 @@
     me = lax.axis_index("img")
     my_x, my_z, core = me // 8, me // 2 % 4, me % 2
     weights_refs = refs[:count]
-    out_hbm, w_ref, h_ref, done_ref, sem = refs[count + aliased :]
+    out_hbm, w_ref, h_ref, done_ref, sem, in_sem = refs[count + aliased :]
     rows = h_own_ref.shape[0]
     wide = 3 * HEAD_DIM
+    loads = []
+    at = 0
+    for n, weights_ref in enumerate(weights_refs):
+        end = at + weights_ref.shape[0]
+        load = pltpu.make_async_copy(weights_ref, w_ref.at[at:end], in_sem.at[n])
+        load.start()
+        loads.append(load)
+        at = end
     for side, ref in ((core, h_own_ref), (1 - core, h_partner_ref)):
         h_ref[pl.ds(pl.multiple_of(side * rows, 16), rows), :] = ref[...]
-    at = 0
-    for weights_ref in weights_refs:
-        w_ref[at : at + weights_ref.shape[0], :] = weights_ref[...]
-        at += weights_ref.shape[0]
     part = lax.broadcasted_iota(jnp.int32, (len(parts) * wide, 1), 0) % wide
     scale = jnp.where(part < HEAD_DIM, Q_SCALE, 1.0).astype(F32)
+    for load in loads:
+        load.wait()
     product = lax.dot_general(w_ref[...], h_ref[...], NT, preferred_element_type=F32)
     product = (product * scale).astype(BF16)
     copies = []
@@ -225,36 +232,47 @@
             project_kernel, parts=parts, offsets=offsets, aliased=aliased
         ),
         out_shape=jax.ShapeDtypeStruct((8, wide, 2 * rows), BF16),
-        in_specs=whole(2 + len(shards))
-        + [pl.BlockSpec(memory_space=pl.ANY)] * aliased,
+        in_specs=whole(2) + [pl.BlockSpec(memory_space=pl.ANY)] * (len(shards) + aliased),
         out_specs=pl.BlockSpec(memory_space=pl.ANY),
         scratch_shapes=[
             pltpu.VMEM((len(parts) * wide, D), BF16),
             pltpu.VMEM((2 * rows, D), BF16),
             pltpu.VMEM((len(parts), wide, 2 * rows), BF16),
             pltpu.SemaphoreType.DMA((len(parts),)),
+            pltpu.SemaphoreType.DMA((len(shards),)),
         ],
         input_output_aliases={2 + len(shards): 0} if aliased else {},
-        compiler_params=pltpu.CompilerParams(vmem_limit_bytes=VMEM_LIMIT),
+        compiler_params=pltpu.CompilerParams(vmem_limit_bytes=VMEM_ALL),
         cost_estimate=pl.CostEstimate(
             flops=2 * 10**9, bytes_accessed=6 * 10**6, transcendentals=0
         ),
     )(h_own, h_partner, *shards, *([into] if aliased else []))
 
 
-def attention_kernel(count_ref, q_ref, all_ref, out_ref, k_ref, v_ref, bound_ref, *, block):
+def attention_kernel(
+    count_ref, all_hbm, out_ref, all_ref, k_ref, v_ref, bound_ref, sem, *, block, taken
+):
     chips, features, rows = all_ref.shape
     total = chips * rows
     depth = HEAD_DIM
 
     @pl.when(pl.program_id(0) == 0)
     def _():
+        copies = [
+            pltpu.make_async_copy(all_hbm.at[chip], all_ref.at[chip], sem.at[chip])
+            for chip in range(chips)
+        ]
+        for copy in copies:
+            copy.start()
         count = count_ref[0]
+        copies[0].wait()
         key_zero = all_ref[0, depth : 2 * depth, 0:1].astype(F32)
         q_most = jnp.zeros((1, rows), F32)
         k_most = jnp.zeros((1, rows), F32)
         v_most = jnp.zeros((HEAD_DIM, rows), F32)
         for chip in range(chips):
+            if chip:
+                copies[chip].wait()
             position = chip * rows + lax.broadcasted_iota(jnp.int32, (1, rows), 1)
             valid = position < count
             keys = jnp.where(valid, all_ref[chip, depth : 2 * depth, :].astype(F32), key_zero)
@@ -272,8 +290,8 @@
         bound_ref[0] = jnp.max(q_most) * jnp.max(k_most)
         bound_ref[1] = jnp.max(v_most)
 
-    taken = q_ref.shape[0]
-    queries = jnp.concatenate([q_ref[n, 0:depth, :] for n in range(taken)], axis=1)
+    first = taken * pl.program_id(0)
+    queries = jnp.concatenate([all_ref[first + n, 0:depth, :] for n in range(taken)], axis=1)
     queries = jnp.concatenate([queries, jnp.zeros((128 - depth, taken * rows), BF16)], axis=0)
     small = (bound_ref[0] < SAFE_BOUND * SAFE_BOUND) & (bound_ref[1] < SAFE_VALUE)
 
@@ -320,22 +338,23 @@
     total = chips * rows
     taken = 2
     return pl.pallas_call(
-        functools.partial(attention_kernel, block=512),
+        functools.partial(attention_kernel, block=512, taken=taken),
         out_shape=jax.ShapeDtypeStruct((2 * chips, HEAD_DIM, rows // 2), BF16),
         grid=(chips // taken,),
         in_specs=[
             pl.BlockSpec(memory_space=pltpu.SMEM),
-            pl.BlockSpec((taken, features, rows), lambda i: (i, 0, 0)),
-            pl.BlockSpec(memory_space=pltpu.VMEM),
+            pl.BlockSpec(memory_space=pl.ANY),
         ],
         out_specs=pl.BlockSpec((2 * taken, HEAD_DIM, rows // 2), lambda i: (i, 0, 0)),
         scratch_shapes=[
+            pltpu.VMEM(received.shape, BF16),
             pltpu.VMEM((total, 128), BF16),
             pltpu.VMEM((HEAD_DIM + 16, total), BF16),
             pltpu.SMEM((2,), F32),
+            pltpu.SemaphoreType.DMA((chips,)),
         ],
-        compiler_params=pltpu.CompilerParams(vmem_limit_bytes=VMEM_LIMIT),
-    )(count, received, received)
+        compiler_params=pltpu.CompilerParams(vmem_limit_bytes=VMEM_ALL),
+    )(count, received)
 
 
 def merge_kernel(bucket_ref, tag_ref, a_ref, x_ref, w_ref, gain_ref, out_ref):

time: 238 us -> 235 us (0.987)
  local copies, waits for them, and re-layouts: 5.45 us -> 1.97 us
    unnamed x24 -> x8, local copies, waits for them, and re-layouts: 5.4 us -> 1.92 us
  transfers between devices with their start and end apart: 12 -> 12, of which waited for: 5 -> 5; matrix products, arithmetic and copies ran while one was open for 0% -> 0% of each run, Pallas kernels for 9% -> 10%
where the time goes in v6:
time: 235 us
  Pallas kernels  98.6 us (42%)
  waiting for transfers between devices  62 us (26%)
  blocking collectives  44.4 us (19%)
  starting transfers between devices  27.2 us (12%)
    pallas_call x1, Pallas kernels, attend_full(): pl.pallas_call(functools.partial(attention_kernel, block=512, taken=taken...  58.3 us
    all_to_all x1, blocking collectives, on_device(): lax.all_to_all(send.reshape(128, 8, D + TAG), BOTH, split_axis=0, concat_...  44.4 us
    all_to_all x1, waiting for transfers between devices, on_device(): lax.all_to_all(projected, 'img', split_axis=0, concat_axis=0, tiled=True,...  34.4 us
    all_to_all x1, waiting for transfers between devices, on_device(): lax.all_to_all(attended, 'img', split_axis=0, concat_axis=0, tiled=True)  14.8 us
    pallas_call x1, Pallas kernels, layer_one(): pl.pallas_call(layer_one_kernel, out_shape=[jax.ShapeDtypeStruct((rows, D...  14.4 us
    pallas_call x2, Pallas kernels, project(): pl.pallas_call(functools.partial(project_kernel, parts=parts, offsets=off...  12.5 us
    pallas_call x1, Pallas kernels, merge(): pl.pallas_call(merge_kernel, out_shape=jax.ShapeDtypeStruct((places, D +...  7.8 us
    all_to_all x1, starting transfers between devices, on_device(): lax.all_to_all(attended, 'img', split_axis=0, concat_axis=0, tiled=True)  6.01 us
  transfers between devices with their start and end apart: 12, of which 5 were waited for; matrix products, arithmetic and copies ran while one was open for 0% of the time, Pallas kernels for 10%

profile of v6, /device:TPU:1, one launch (start us, length us, event | category | flops | bytes accessed | tf_op | source)
XLA Modules:
  0.0 234.9 jit_solution(18265266780048745232)
XLA Ops:
  0.0 2.5 %collective-permute-start.1 = (bf16[240,1280]{1,0:T(8,128)(2,1)}, bf16[240,1280]{1,0:T(8,128)(2,1)S(1)}, u32[]{:S(2)}, u32[]{:S(2)}) collective-permute-start(bf16[240,1280]{1,0:T(8,128)(2,1)} %bitcast.10), channel_id=1, source_target_pairs={{0,2},{1,3},{2,4},{3,5},{4,6},{5,7},{6,0},{7,1},{8,10},{9,11},{10,... | collective-permute-start | bytes 1843208 | tf_op jit(solution)/shard_map/ppermute | solution.py:172
  2.5 2.1 collective-permute-start.3
  4.6 2.5 %collective-permute-start.5 = (bf16[240,1280]{1,0:T(8,128)(2,1)}, bf16[240,1280]{1,0:T(8,128)(2,1)}, u32[]{:S(2)}, u32[]{:S(2)}) collective-permute-start(bf16[240,1280]{1,0:T(8,128)(2,1)} %bitcast.12), channel_id=1, source_target_pairs={{0,72},{1,73},{2,74},{3,75},{4,76},{5,77},{6,78},{7,79},{8,64},{9,... | collective-permute-start | bytes 1843208 | tf_op jit(solution)/shard_map/ppermute | solution.py:174
  7.1 14.4 %shard_map.109 = (bf16[384,1280]{1,0:T(8,128)(2,1)}, bf16[384,1280]{1,0:T(8,128)(2,1)}) custom-call(s32[1,384]{1,0:T(1,128)} %ids_ref.1, bf16[1,384,1280]{2,1,0:T(8,128)(2,1)} %x_ref.1, bf16[1280]{0:T(1024)(128)(2,1)} %gain_one_ref.1, bf16[1280]{0:T(1024)(128)(2,1)} %gain_two_ref.1, bf16[3,1280,1280]{2,1,0:T(8,128)(2,1)} %w_qkv_ref.1, ...), custom_call_target="tpu_custom_call" | custom-call | flops 6000000000 | bytes 16000000 | tf_op jit(solution)/shard_map/pallas_call | solution.py:124
  21.5 1.3 collective-permute-start
  22.8 0.0 collective-permute-done.1.refs_1_
  22.8 0.1 collective-permute-start.2
  22.9 0.0 collective-permute-done.3.refs_2_
  23.0 2.7 %collective-permute-start.4 = (bf16[112,1280]{1,0:T(8,128)(2,1)S(1)}, bf16[112,1280]{1,0:T(8,128)(2,1)}, u32[]{:S(2)}, u32[]{:S(2)}) collective-permute-start(bf16[112,1280]{1,0:T(8,128)(2,1)S(1)} %slice.9), channel_id=1, source_target_pairs={{0,6},{1,7},{2,0},{3,1},{4,2},{5,3},{6,4},{7,5},{8,14},{9,15},{10,... | collective-permute-start | bytes 860168 | tf_op jit(solution)/shard_map/ppermute | solution.py:182
  25.7 0.0 collective-permute-done.5.refs_3_
  25.7 5.9 %collective-permute-done.4.refs_5_ = bf16[112,1280]{1,0:T(8,128)(2,1)} collective-permute-done((bf16[112,1280]{1,0:T(8,128)(2,1)S(1)}, bf16[112,1280]{1,0:T(8,128)(2,1)}, u32[]{:S(2)}, u32[]{:S(2)}) %collective-permute-start.4) | collective-permute-done | bytes 286752 | tf_op jit(solution)/shard_map/ppermute | solution.py:182
  31.6 1.9 collective-permute-done.2.refs_4_
  33.5 0.0 collective-permute-start.6
  33.5 2.7 %collective-permute-start.7 = (bf16[240,1280]{1,0:T(8,128)(2,1)}, bf16[240,1280]{1,0:T(8,128)(2,1)}, u32[]{:S(2)}, u32[]{:S(2)}) collective-permute-start(bf16[240,1280]{1,0:T(8,128)(2,1)} %collective-permute-done.5.refs_3_), channel_id=1, source_target_pairs={{0,6},{1,7},{2,0},{3,1},{4,2},{5,3},{6,4},{7,5},{8,14},{9,15},{10,... | collective-permute-start | bytes 1843208 | tf_op jit(solution)/shard_map/ppermute | solution.py:187
  36.2 0.2 collective-permute-start.8
  36.4 2.5 %collective-permute-start.9 = (bf16[112,1280]{1,0:T(8,128)(2,1)}, bf16[112,1280]{1,0:T(8,128)(2,1)}, u32[]{:S(2)}, u32[]{:S(2)}) collective-permute-start(bf16[112,1280]{1,0:T(8,128)(2,1)} %collective-permute-done.4.refs_5_), channel_id=1, source_target_pairs={{0,72},{1,73},{2,74},{3,75},{4,76},{5,77},{6,78},{7,79},{8,64},{9,... | collective-permute-start | bytes 860168 | tf_op jit(solution)/shard_map/ppermute | solution.py:185
  38.9 0.0 collective-permute-done.h_partner_ref
  38.9 1.0 copy-done
  39.8 7.0 %shard_map.110.refs_4_ = bf16[8,240,768]{2,1,0:T(8,128)(2,1)} custom-call(bf16[384,1280]{1,0:T(8,128)(2,1)} %get-tuple-element.13.h_own_ref, bf16[384,1280]{1,0:T(8,128)(2,1)} %copy-done, bf16[240,1280]{1,0:T(8,128)(2,1)} %bitcast.13, bf16[240,1280]{1,0:T(8,128)(2,1)} %copy-done.2, bf16[240,1280]{1,0:T(8,128)(2,1)} %copy-done.3, ...), custom_call_target="tpu_custom_call" | custom-call | flops 2000000000 | bytes 6000000 | tf_op jit(solution)/shard_map/pallas_call | solution.py:230
  46.8 4.9 %collective-permute-done.9.refs_3_ = bf16[112,1280]{1,0:T(8,128)(2,1)} collective-permute-done((bf16[112,1280]{1,0:T(8,128)(2,1)}, bf16[112,1280]{1,0:T(8,128)(2,1)}, u32[]{:S(2)}, u32[]{:S(2)}) %collective-permute-start.9) | collective-permute-done | bytes 286752 | tf_op jit(solution)/shard_map/ppermute | solution.py:185
  51.7 0.0 collective-permute-done.8.refs_2_
  51.7 5.5 %shard_map.111 = bf16[8,240,768]{2,1,0:T(8,128)(2,1)} custom-call(bf16[384,1280]{1,0:T(8,128)(2,1)} %get-tuple-element.13.h_own_ref, bf16[384,1280]{1,0:T(8,128)(2,1)} %copy-done, bf16[240,1280]{1,0:T(8,128)(2,1)} %collective-permute-done.6.refs_0_, bf16[240,1280]{1,0:T(8,128)(2,1)} %collective-permute-done.7.refs_1_, ...), custom_call_target="tpu_custom_call", output_to_operand_aliasing={{}: (6, {})} | custom-call | flops 2000000000 | bytes 6000000 | tf_op jit(solution)/shard_map/pallas_call | solution.py:230
  57.2 4.7 %all-to-all-start = ((bf16[8,240,768]{2,1,0:T(8,128)(2,1)}), bf16[8,240,768]{2,1,0:T(8,128)(2,1)}, u32[]{:S(2)}, u32[]{:S(2)}) async-start(bf16[8,240,768]{2,1,0:T(8,128)(2,1)} %shard_map.111), calls=%async_computation | async-start | bytes 5898240 | tf_op jit(solution)/shard_map/all_to_all | solution.py:458
  62.6 34.4 %all-to-all-done.all_hbm = bf16[8,240,768]{2,1,0:T(8,128)(2,1)} async-done(((bf16[8,240,768]{2,1,0:T(8,128)(2,1)}), bf16[8,240,768]{2,1,0:T(8,128)(2,1)}, u32[]{:S(2)}, u32[]{:S(2)}) %all-to-all-start) | async-done | bytes 2949152 | tf_op jit(solution)/shard_map/all_to_all | solution.py:458
  96.9 58.3 %shard_map.113 = bf16[16,80,384]{2,1,0:T(8,128)(2,1)} custom-call(s32[1]{0:T(128)S(6)} %copy.14.count_ref, bf16[8,240,768]{2,1,0:T(8,128)(2,1)} %all-to-all-done.all_hbm), custom_call_target="tpu_custom_call" | custom-call | tf_op jit(solution)/shard_map/pallas_call | solution.py:340
  155.2 6.0 %all-to-all-start.1 = ((bf16[16,80,384]{2,1,0:T(8,128)(2,1)}), bf16[16,80,384]{2,1,0:T(8,128)(2,1)S(1)}, u32[]{:S(2)}, u32[]{:S(2)}) async-start(bf16[16,80,384]{2,1,0:T(8,128)(2,1)} %shard_map.113), calls=%async_computation.1 | async-start | bytes 1966080 | tf_op jit(solution)/shard_map/all_to_all | solution.py:464
  161.2 1.7 shard_map.112
  162.9 14.8 %all-to-all-done.1 = bf16[16,80,384]{2,1,0:T(8,128)(2,1)S(1)} async-done(((bf16[16,80,384]{2,1,0:T(8,128)(2,1)}), bf16[16,80,384]{2,1,0:T(8,128)(2,1)S(1)}, u32[]{:S(2)}, u32[]{:S(2)}) %all-to-all-start.1) | async-done | bytes 983072 | tf_op jit(solution)/shard_map/all_to_all | solution.py:464
  177.7 1.0 copy-done.1
  178.7 7.8 %shard_map.114 = bf16[1024,1408]{1,0:T(8,128)(2,1)} custom-call(s32[1,384]{1,0:T(1,128)} %get-tuple-element.18.bucket_ref, bf16[384,128]{1,0:T(8,128)(2,1)} %get-tuple-element.19.tag_ref, bf16[1280,384]{1,0:T(8,128)(2,1)} %bitcast.9, bf16[384,1280]{1,0:T(8,128)(2,1)} %get-tuple-element.20.x_ref, bf16[1280,1280]{1,0:T(8,128)(2,1)} %w_ref.1, ...), custom_call_target="tpu_custom_call" | custom-call | tf_op jit(solution)/shard_map/pallas_call | solution.py:375
  186.5 44.4 %all_to_all.15 = bf16[128,8,1408]{2,1,0:T(8,128)(2,1)} all-to-all(bf16[128,8,1408]{2,1,0:T(8,128)(2,1)} %bitcast.7), channel_id=1, replica_groups=mesh['ctx'=8,'img'=16] {'ctx','img'}, dimensions={0} | all-to-all | bytes 5767168 | tf_op jit(solution)/shard_map/all_to_all | solution.py:467
  230.9 4.0 %shard_map.115 = bf16[96,5120]{1,0:T(8,128)(2,1)} custom-call(bf16[1024,1408]{1,0:T(8,128)(2,1)} %bitcast.8), custom_call_target="tpu_custom_call" | custom-call | tf_op jit(solution)/shard_map/pallas_call | solution.py:398
  (10 shorter events, 0.1 us)
Async XLA Ops:
  0.0 22.8 %collective-permute-start.1 = (bf16[240,1280]{1,0:T(8,128)(2,1)}, bf16[240,1280]{1,0:T(8,128)(2,1)S(1)}, u32[]{:S(2)}, u32[]{:S(2)}) collective-permute-start(bf16[240,1280]{1,0:T(8,128)(2,1)} %bitcast.10), channel_id=1, source_target_pairs={{0,2},{1,3},{2,4},{3,5},{4,6},{5,7},{6,0},{7,1},{8,10},{9,11},{10,... | collective-permute-start | bytes 1843208 | tf_op jit(solution)/shard_map/ppermute | solution.py:172
  2.5 20.4 %collective-permute-start.3 = (bf16[240,1280]{1,0:T(8,128)(2,1)}, bf16[240,1280]{1,0:T(8,128)(2,1)S(1)}, u32[]{:S(2)}, u32[]{:S(2)}) collective-permute-start(bf16[240,1280]{1,0:T(8,128)(2,1)} %bitcast.11), channel_id=1, source_target_pairs={{0,6},{1,7},{2,0},{3,1},{4,2},{5,3},{6,4},{7,5},{8,14},{9,15},{10,... | collective-permute-start | bytes 1843208 | tf_op jit(solution)/shard_map/ppermute | solution.py:173
  4.6 21.1 %collective-permute-start.5 = (bf16[240,1280]{1,0:T(8,128)(2,1)}, bf16[240,1280]{1,0:T(8,128)(2,1)}, u32[]{:S(2)}, u32[]{:S(2)}) collective-permute-start(bf16[240,1280]{1,0:T(8,128)(2,1)} %bitcast.12), channel_id=1, source_target_pairs={{0,72},{1,73},{2,74},{3,75},{4,76},{5,77},{6,78},{7,79},{8,64},{9,... | collective-permute-start | bytes 1843208 | tf_op jit(solution)/shard_map/ppermute | solution.py:174
  21.5 17.4 %collective-permute-start = (bf16[384,1280]{1,0:T(8,128)(2,1)}, bf16[384,1280]{1,0:T(8,128)(2,1)S(1)}, u32[]{:S(2)}, u32[]{:S(2)}) collective-permute-start(bf16[384,1280]{1,0:T(8,128)(2,1)} %get-tuple-element.13.h_own_ref), channel_id=1, source_target_pairs={{0,1},{1,0},{2,3},{3,2},{4,5},{5,4},{6,7},{7,6},{8,9},{9,8},{10,11... | collective-permute-start | bytes 2949128 | tf_op jit(solution)/shard_map/ppermute | solution.py:454
  22.8 13.6 %copy-start.2 = (bf16[240,1280]{1,0:T(8,128)(2,1)}, bf16[240,1280]{1,0:T(8,128)(2,1)S(1)}, u32[]{:S(2)}) copy-start(bf16[240,1280]{1,0:T(8,128)(2,1)S(1)} %collective-permute-done.1.refs_1_) | copy-start | bytes 1843204
  22.8 10.7 %collective-permute-start.2 = (bf16[128,1280]{1,0:T(8,128)(2,1)S(1)}, bf16[128,1280]{1,0:T(8,128)(2,1)}, u32[]{:S(2)}, u32[]{:S(2)}) collective-permute-start(bf16[128,1280]{1,0:T(8,128)(2,1)S(1)} %slice.8), channel_id=1, source_target_pairs={{0,2},{1,3},{2,4},{3,5},{4,6},{5,7},{6,0},{7,1},{8,10},{9,11},{10,... | collective-permute-start | bytes 983048 | tf_op jit(solution)/shard_map/ppermute | solution.py:181
  22.9 16.0 %copy-start.3 = (bf16[240,1280]{1,0:T(8,128)(2,1)}, bf16[240,1280]{1,0:T(8,128)(2,1)S(1)}, u32[]{:S(2)}) copy-start(bf16[240,1280]{1,0:T(8,128)(2,1)S(1)} %collective-permute-done.3.refs_2_) | copy-start | bytes 1843204
  23.0 8.6 %collective-permute-start.4 = (bf16[112,1280]{1,0:T(8,128)(2,1)S(1)}, bf16[112,1280]{1,0:T(8,128)(2,1)}, u32[]{:S(2)}, u32[]{:S(2)}) collective-permute-start(bf16[112,1280]{1,0:T(8,128)(2,1)S(1)} %slice.9), channel_id=1, source_target_pairs={{0,6},{1,7},{2,0},{3,1},{4,2},{5,3},{6,4},{7,5},{8,14},{9,15},{10,... | collective-permute-start | bytes 860168 | tf_op jit(solution)/shard_map/ppermute | solution.py:182
  33.5 18.2 %collective-permute-start.6 = (bf16[240,1280]{1,0:T(8,128)(2,1)}, bf16[240,1280]{1,0:T(8,128)(2,1)}, u32[]{:S(2)}, u32[]{:S(2)}) collective-permute-start(bf16[240,1280]{1,0:T(8,128)(2,1)} %collective-permute-done.5.refs_3_), channel_id=1, source_target_pairs={{0,2},{1,3},{2,4},{3,5},{4,6},{5,7},{6,0},{7,1},{8,10},{9,11},{10,... | collective-permute-start | bytes 1843208 | tf_op jit(solution)/shard_map/ppermute | solution.py:186
  33.5 18.2 %collective-permute-start.7 = (bf16[240,1280]{1,0:T(8,128)(2,1)}, bf16[240,1280]{1,0:T(8,128)(2,1)}, u32[]{:S(2)}, u32[]{:S(2)}) collective-permute-start(bf16[240,1280]{1,0:T(8,128)(2,1)} %collective-permute-done.5.refs_3_), channel_id=1, source_target_pairs={{0,6},{1,7},{2,0},{3,1},{4,2},{5,3},{6,4},{7,5},{8,14},{9,15},{10,... | collective-permute-start | bytes 1843208 | tf_op jit(solution)/shard_map/ppermute | solution.py:187
  36.2 15.5 %collective-permute-start.8 = (bf16[128,1280]{1,0:T(8,128)(2,1)}, bf16[128,1280]{1,0:T(8,128)(2,1)}, u32[]{:S(2)}, u32[]{:S(2)}) collective-permute-start(bf16[128,1280]{1,0:T(8,128)(2,1)} %collective-permute-done.2.refs_4_), channel_id=1, source_target_pairs={{0,72},{1,73},{2,74},{3,75},{4,76},{5,77},{6,78},{7,79},{8,64},{9,... | collective-permute-start | bytes 983048 | tf_op jit(solution)/shard_map/ppermute | solution.py:184
  36.4 15.3 %collective-permute-start.9 = (bf16[112,1280]{1,0:T(8,128)(2,1)}, bf16[112,1280]{1,0:T(8,128)(2,1)}, u32[]{:S(2)}, u32[]{:S(2)}) collective-permute-start(bf16[112,1280]{1,0:T(8,128)(2,1)} %collective-permute-done.4.refs_5_), channel_id=1, source_target_pairs={{0,72},{1,73},{2,74},{3,75},{4,76},{5,77},{6,78},{7,79},{8,64},{9,... | collective-permute-start | bytes 860168 | tf_op jit(solution)/shard_map/ppermute | solution.py:185
  38.9 1.0 copy-start
  57.2 39.7 %all-to-all-start = ((bf16[8,240,768]{2,1,0:T(8,128)(2,1)}), bf16[8,240,768]{2,1,0:T(8,128)(2,1)}, u32[]{:S(2)}, u32[]{:S(2)}) async-start(bf16[8,240,768]{2,1,0:T(8,128)(2,1)} %shard_map.111), calls=%async_computation | async-start | bytes 5898240 | tf_op jit(solution)/shard_map/all_to_all | solution.py:458
  155.2 22.5 %all-to-all-start.1 = ((bf16[16,80,384]{2,1,0:T(8,128)(2,1)}), bf16[16,80,384]{2,1,0:T(8,128)(2,1)S(1)}, u32[]{:S(2)}, u32[]{:S(2)}) async-start(bf16[16,80,384]{2,1,0:T(8,128)(2,1)} %shard_map.113), calls=%async_computation.1 | async-start | bytes 1966080 | tf_op jit(solution)/shard_map/all_to_all | solution.py:464
  177.7 1.0 copy-start.1

commit v7 on v6

--- a/solution.py
+++ b/solution.py
@@ -204,8 +204,12 @@
         load.start()
         loads.append(load)
         at = end
-    for side, ref in ((core, h_own_ref), (1 - core, h_partner_ref)):
-        h_ref[pl.ds(pl.multiple_of(side * rows, 16), rows), :] = ref[...]
+    for n, (side, ref) in enumerate(((core, h_own_ref), (1 - core, h_partner_ref))):
+        load = pltpu.make_async_copy(
+            ref, h_ref.at[pl.ds(pl.multiple_of(side * rows, 16), rows)], in_sem.at[count + n]
+        )
+        load.start()
+        loads.append(load)
     part = lax.broadcasted_iota(jnp.int32, (len(parts) * wide, 1), 0) % wide
     scale = jnp.where(part < HEAD_DIM, Q_SCALE, 1.0).astype(F32)
     for load in loads:
@@ -232,14 +236,14 @@
             project_kernel, parts=parts, offsets=offsets, aliased=aliased
         ),
         out_shape=jax.ShapeDtypeStruct((8, wide, 2 * rows), BF16),
-        in_specs=whole(2) + [pl.BlockSpec(memory_space=pl.ANY)] * (len(shards) + aliased),
+        in_specs=[pl.BlockSpec(memory_space=pl.ANY)] * (2 + len(shards) + aliased),
         out_specs=pl.BlockSpec(memory_space=pl.ANY),
         scratch_shapes=[
             pltpu.VMEM((len(parts) * wide, D), BF16),
             pltpu.VMEM((2 * rows, D), BF16),
             pltpu.VMEM((len(parts), wide, 2 * rows), BF16),
             pltpu.SemaphoreType.DMA((len(parts),)),
-            pltpu.SemaphoreType.DMA((len(shards),)),
+            pltpu.SemaphoreType.DMA((len(shards) + 2,)),
         ],
         input_output_aliases={2 + len(shards): 0} if aliased else {},
         compiler_params=pltpu.CompilerParams(vmem_limit_bytes=VMEM_ALL),

time: 235 us -> 235 us (level)
  transfers between devices with their start and end apart: 12 -> 12, of which waited for: 5 -> 5; matrix products, arithmetic and copies ran while one was open for 0% -> 0% of each run, Pallas kernels for 10% -> 9%
where the time goes in v7:
time: 235 us; the launch traced here: 234 us
  Pallas kernels  97 us (41%)
  waiting for transfers between devices  62.8 us (27%)
  blocking collectives  44.4 us (19%)
  starting transfers between devices  27.2 us (12%)
    pallas_call x1, Pallas kernels, attend_full(): pl.pallas_call(functools.partial(attention_kernel, block=512, taken=taken...  58.3 us
    all_to_all x1, blocking collectives, on_device(): lax.all_to_all(send.reshape(128, 8, D + TAG), BOTH, split_axis=0, concat_...  44.4 us
    all_to_all x1, waiting for transfers between devices, on_device(): lax.all_to_all(projected, 'img', split_axis=0, concat_axis=0, tiled=True,...  34.4 us
    all_to_all x1, waiting for transfers between devices, on_device(): lax.all_to_all(attended, 'img', split_axis=0, concat_axis=0, tiled=True)  14.8 us
    pallas_call x1, Pallas kernels, layer_one(): pl.pallas_call(layer_one_kernel, out_shape=[jax.ShapeDtypeStruct((rows, D...  14.4 us
    pallas_call x2, Pallas kernels, project(): pl.pallas_call(functools.partial(project_kernel, parts=parts, offsets=off...  10.8 us
    pallas_call x1, Pallas kernels, merge(): pl.pallas_call(merge_kernel, out_shape=jax.ShapeDtypeStruct((places, D +...  7.8 us
    all_to_all x1, starting transfers between devices, on_device(): lax.all_to_all(attended, 'img', split_axis=0, concat_axis=0, tiled=True)  6.01 us
  transfers between devices with their start and end apart: 12, of which 5 were waited for; matrix products, arithmetic and copies ran while one was open for 0% of the time, Pallas kernels for 9%

profile of v7, /device:TPU:1, one launch (start us, length us, event | category | flops | bytes accessed | tf_op | source)
XLA Modules:
  0.0 234.1 jit_solution(6117156738406124361)
XLA Ops:
  0.0 2.5 %collective-permute-start.1 = (bf16[240,1280]{1,0:T(8,128)(2,1)}, bf16[240,1280]{1,0:T(8,128)(2,1)S(1)}, u32[]{:S(2)}, u32[]{:S(2)}) collective-permute-start(bf16[240,1280]{1,0:T(8,128)(2,1)} %bitcast.10), channel_id=1, source_target_pairs={{0,2},{1,3},{2,4},{3,5},{4,6},{5,7},{6,0},{7,1},{8,10},{9,11},{10,... | collective-permute-start | bytes 1843208 | tf_op jit(solution)/shard_map/ppermute | solution.py:172
  2.5 2.1 collective-permute-start.3
  4.6 2.5 %collective-permute-start.5 = (bf16[240,1280]{1,0:T(8,128)(2,1)}, bf16[240,1280]{1,0:T(8,128)(2,1)}, u32[]{:S(2)}, u32[]{:S(2)}) collective-permute-start(bf16[240,1280]{1,0:T(8,128)(2,1)} %bitcast.12), channel_id=1, source_target_pairs={{0,72},{1,73},{2,74},{3,75},{4,76},{5,77},{6,78},{7,79},{8,64},{9,... | collective-permute-start | bytes 1843208 | tf_op jit(solution)/shard_map/ppermute | solution.py:174
  7.1 14.4 %shard_map.109 = (bf16[384,1280]{1,0:T(8,128)(2,1)}, bf16[384,1280]{1,0:T(8,128)(2,1)}) custom-call(s32[1,384]{1,0:T(1,128)} %ids_ref.1, bf16[1,384,1280]{2,1,0:T(8,128)(2,1)} %x_ref.1, bf16[1280]{0:T(1024)(128)(2,1)} %gain_one_ref.1, bf16[1280]{0:T(1024)(128)(2,1)} %gain_two_ref.1, bf16[3,1280,1280]{2,1,0:T(8,128)(2,1)} %w_qkv_ref.1, ...), custom_call_target="tpu_custom_call" | custom-call | flops 6000000000 | bytes 16000000 | tf_op jit(solution)/shard_map/pallas_call | solution.py:124
  21.5 1.3 collective-permute-start
  22.8 0.0 collective-permute-done.1.refs_1_
  22.8 0.1 collective-permute-start.2
  22.9 0.0 collective-permute-done.3.refs_2_
  23.0 2.7 %collective-permute-start.4 = (bf16[112,1280]{1,0:T(8,128)(2,1)S(1)}, bf16[112,1280]{1,0:T(8,128)(2,1)}, u32[]{:S(2)}, u32[]{:S(2)}) collective-permute-start(bf16[112,1280]{1,0:T(8,128)(2,1)S(1)} %slice.9), channel_id=1, source_target_pairs={{0,6},{1,7},{2,0},{3,1},{4,2},{5,3},{6,4},{7,5},{8,14},{9,15},{10,... | collective-permute-start | bytes 860168 | tf_op jit(solution)/shard_map/ppermute | solution.py:182
  25.7 0.0 collective-permute-done.5.refs_3_
  25.7 5.9 %collective-permute-done.4.refs_5_ = bf16[112,1280]{1,0:T(8,128)(2,1)} collective-permute-done((bf16[112,1280]{1,0:T(8,128)(2,1)S(1)}, bf16[112,1280]{1,0:T(8,128)(2,1)}, u32[]{:S(2)}, u32[]{:S(2)}) %collective-permute-start.4) | collective-permute-done | bytes 286752 | tf_op jit(solution)/shard_map/ppermute | solution.py:182
  31.6 1.9 collective-permute-done.2.refs_4_
  33.5 0.0 collective-permute-start.6
  33.5 2.7 %collective-permute-start.7 = (bf16[240,1280]{1,0:T(8,128)(2,1)}, bf16[240,1280]{1,0:T(8,128)(2,1)}, u32[]{:S(2)}, u32[]{:S(2)}) collective-permute-start(bf16[240,1280]{1,0:T(8,128)(2,1)} %collective-permute-done.5.refs_3_), channel_id=1, source_target_pairs={{0,6},{1,7},{2,0},{3,1},{4,2},{5,3},{6,4},{7,5},{8,14},{9,15},{10,... | collective-permute-start | bytes 1843208 | tf_op jit(solution)/shard_map/ppermute | solution.py:187
  36.2 0.2 collective-permute-start.8
  36.4 2.5 %collective-permute-start.9 = (bf16[112,1280]{1,0:T(8,128)(2,1)}, bf16[112,1280]{1,0:T(8,128)(2,1)}, u32[]{:S(2)}, u32[]{:S(2)}) collective-permute-start(bf16[112,1280]{1,0:T(8,128)(2,1)} %collective-permute-done.4.refs_5_), channel_id=1, source_target_pairs={{0,72},{1,73},{2,74},{3,75},{4,76},{5,77},{6,78},{7,79},{8,64},{9,... | collective-permute-start | bytes 860168 | tf_op jit(solution)/shard_map/ppermute | solution.py:185
  38.9 0.0 collective-permute-done.h_partner_ref
  38.9 1.0 copy-done
  39.8 6.1 %shard_map.110.refs_4_ = bf16[8,240,768]{2,1,0:T(8,128)(2,1)} custom-call(bf16[384,1280]{1,0:T(8,128)(2,1)} %get-tuple-element.13.h_own_ref, bf16[384,1280]{1,0:T(8,128)(2,1)} %copy-done, bf16[240,1280]{1,0:T(8,128)(2,1)} %bitcast.13, bf16[240,1280]{1,0:T(8,128)(2,1)} %copy-done.2, bf16[240,1280]{1,0:T(8,128)(2,1)} %copy-done.3, ...), custom_call_target="tpu_custom_call" | custom-call | flops 2000000000 | bytes 6000000 | tf_op jit(solution)/shard_map/pallas_call | solution.py:234
  46.0 5.7 %collective-permute-done.9.refs_3_ = bf16[112,1280]{1,0:T(8,128)(2,1)} collective-permute-done((bf16[112,1280]{1,0:T(8,128)(2,1)}, bf16[112,1280]{1,0:T(8,128)(2,1)}, u32[]{:S(2)}, u32[]{:S(2)}) %collective-permute-start.9) | collective-permute-done | bytes 286752 | tf_op jit(solution)/shard_map/ppermute | solution.py:185
  51.7 0.0 collective-permute-done.8.refs_2_
  51.7 4.7 %shard_map.111 = bf16[8,240,768]{2,1,0:T(8,128)(2,1)} custom-call(bf16[384,1280]{1,0:T(8,128)(2,1)} %get-tuple-element.13.h_own_ref, bf16[384,1280]{1,0:T(8,128)(2,1)} %copy-done, bf16[240,1280]{1,0:T(8,128)(2,1)} %collective-permute-done.6.refs_0_, bf16[240,1280]{1,0:T(8,128)(2,1)} %collective-permute-done.7.refs_1_, ...), custom_call_target="tpu_custom_call", output_to_operand_aliasing={{}: (6, {})} | custom-call | flops 2000000000 | bytes 6000000 | tf_op jit(solution)/shard_map/pallas_call | solution.py:234
  56.4 4.7 %all-to-all-start = ((bf16[8,240,768]{2,1,0:T(8,128)(2,1)}), bf16[8,240,768]{2,1,0:T(8,128)(2,1)}, u32[]{:S(2)}, u32[]{:S(2)}) async-start(bf16[8,240,768]{2,1,0:T(8,128)(2,1)} %shard_map.111), calls=%async_computation | async-start | bytes 5898240 | tf_op jit(solution)/shard_map/all_to_all | solution.py:462
  61.7 34.4 %all-to-all-done.all_hbm = bf16[8,240,768]{2,1,0:T(8,128)(2,1)} async-done(((bf16[8,240,768]{2,1,0:T(8,128)(2,1)}), bf16[8,240,768]{2,1,0:T(8,128)(2,1)}, u32[]{:S(2)}, u32[]{:S(2)}) %all-to-all-start) | async-done | bytes 2949152 | tf_op jit(solution)/shard_map/all_to_all | solution.py:462
  96.1 58.3 %shard_map.113 = bf16[16,80,384]{2,1,0:T(8,128)(2,1)} custom-call(s32[1]{0:T(128)S(6)} %copy.14.count_ref, bf16[8,240,768]{2,1,0:T(8,128)(2,1)} %all-to-all-done.all_hbm), custom_call_target="tpu_custom_call" | custom-call | tf_op jit(solution)/shard_map/pallas_call | solution.py:344
  154.4 6.0 %all-to-all-start.1 = ((bf16[16,80,384]{2,1,0:T(8,128)(2,1)}), bf16[16,80,384]{2,1,0:T(8,128)(2,1)S(1)}, u32[]{:S(2)}, u32[]{:S(2)}) async-start(bf16[16,80,384]{2,1,0:T(8,128)(2,1)} %shard_map.113), calls=%async_computation.1 | async-start | bytes 1966080 | tf_op jit(solution)/shard_map/all_to_all | solution.py:468
  160.4 1.7 shard_map.112
  162.1 14.8 %all-to-all-done.1 = bf16[16,80,384]{2,1,0:T(8,128)(2,1)S(1)} async-done(((bf16[16,80,384]{2,1,0:T(8,128)(2,1)}), bf16[16,80,384]{2,1,0:T(8,128)(2,1)S(1)}, u32[]{:S(2)}, u32[]{:S(2)}) %all-to-all-start.1) | async-done | bytes 983072 | tf_op jit(solution)/shard_map/all_to_all | solution.py:468
  176.9 1.0 copy-done.1
  177.9 7.8 %shard_map.114 = bf16[1024,1408]{1,0:T(8,128)(2,1)} custom-call(s32[1,384]{1,0:T(1,128)} %get-tuple-element.18.bucket_ref, bf16[384,128]{1,0:T(8,128)(2,1)} %get-tuple-element.19.tag_ref, bf16[1280,384]{1,0:T(8,128)(2,1)} %bitcast.9, bf16[384,1280]{1,0:T(8,128)(2,1)} %get-tuple-element.20.x_ref, bf16[1280,1280]{1,0:T(8,128)(2,1)} %w_ref.1, ...), custom_call_target="tpu_custom_call" | custom-call | tf_op jit(solution)/shard_map/pallas_call | solution.py:379
  185.7 44.4 %all_to_all.15 = bf16[128,8,1408]{2,1,0:T(8,128)(2,1)} all-to-all(bf16[128,8,1408]{2,1,0:T(8,128)(2,1)} %bitcast.7), channel_id=1, replica_groups=mesh['ctx'=8,'img'=16] {'ctx','img'}, dimensions={0} | all-to-all | bytes 5767168 | tf_op jit(solution)/shard_map/all_to_all | solution.py:471
  230.1 4.0 %shard_map.115 = bf16[96,5120]{1,0:T(8,128)(2,1)} custom-call(bf16[1024,1408]{1,0:T(8,128)(2,1)} %bitcast.8), custom_call_target="tpu_custom_call" | custom-call | tf_op jit(solution)/shard_map/pallas_call | solution.py:402
  (10 shorter events, 0.1 us)
Async XLA Ops:
  0.0 22.8 %collective-permute-start.1 = (bf16[240,1280]{1,0:T(8,128)(2,1)}, bf16[240,1280]{1,0:T(8,128)(2,1)S(1)}, u32[]{:S(2)}, u32[]{:S(2)}) collective-permute-start(bf16[240,1280]{1,0:T(8,128)(2,1)} %bitcast.10), channel_id=1, source_target_pairs={{0,2},{1,3},{2,4},{3,5},{4,6},{5,7},{6,0},{7,1},{8,10},{9,11},{10,... | collective-permute-start | bytes 1843208 | tf_op jit(solution)/shard_map/ppermute | solution.py:172
  2.5 20.4 %collective-permute-start.3 = (bf16[240,1280]{1,0:T(8,128)(2,1)}, bf16[240,1280]{1,0:T(8,128)(2,1)S(1)}, u32[]{:S(2)}, u32[]{:S(2)}) collective-permute-start(bf16[240,1280]{1,0:T(8,128)(2,1)} %bitcast.11), channel_id=1, source_target_pairs={{0,6},{1,7},{2,0},{3,1},{4,2},{5,3},{6,4},{7,5},{8,14},{9,15},{10,... | collective-permute-start | bytes 1843208 | tf_op jit(solution)/shard_map/ppermute | solution.py:173
  4.6 21.1 %collective-permute-start.5 = (bf16[240,1280]{1,0:T(8,128)(2,1)}, bf16[240,1280]{1,0:T(8,128)(2,1)}, u32[]{:S(2)}, u32[]{:S(2)}) collective-permute-start(bf16[240,1280]{1,0:T(8,128)(2,1)} %bitcast.12), channel_id=1, source_target_pairs={{0,72},{1,73},{2,74},{3,75},{4,76},{5,77},{6,78},{7,79},{8,64},{9,... | collective-permute-start | bytes 1843208 | tf_op jit(solution)/shard_map/ppermute | solution.py:174
  21.5 17.4 %collective-permute-start = (bf16[384,1280]{1,0:T(8,128)(2,1)}, bf16[384,1280]{1,0:T(8,128)(2,1)S(1)}, u32[]{:S(2)}, u32[]{:S(2)}) collective-permute-start(bf16[384,1280]{1,0:T(8,128)(2,1)} %get-tuple-element.13.h_own_ref), channel_id=1, source_target_pairs={{0,1},{1,0},{2,3},{3,2},{4,5},{5,4},{6,7},{7,6},{8,9},{9,8},{10,11... | collective-permute-start | bytes 2949128 | tf_op jit(solution)/shard_map/ppermute | solution.py:458
  22.8 13.6 %copy-start.2 = (bf16[240,1280]{1,0:T(8,128)(2,1)}, bf16[240,1280]{1,0:T(8,128)(2,1)S(1)}, u32[]{:S(2)}) copy-start(bf16[240,1280]{1,0:T(8,128)(2,1)S(1)} %collective-permute-done.1.refs_1_) | copy-start | bytes 1843204
  22.8 10.7 %collective-permute-start.2 = (bf16[128,1280]{1,0:T(8,128)(2,1)S(1)}, bf16[128,1280]{1,0:T(8,128)(2,1)}, u32[]{:S(2)}, u32[]{:S(2)}) collective-permute-start(bf16[128,1280]{1,0:T(8,128)(2,1)S(1)} %slice.8), channel_id=1, source_target_pairs={{0,2},{1,3},{2,4},{3,5},{4,6},{5,7},{6,0},{7,1},{8,10},{9,11},{10,... | collective-permute-start | bytes 983048 | tf_op jit(solution)/shard_map/ppermute | solution.py:181
  22.9 16.0 %copy-start.3 = (bf16[240,1280]{1,0:T(8,128)(2,1)}, bf16[240,1280]{1,0:T(8,128)(2,1)S(1)}, u32[]{:S(2)}) copy-start(bf16[240,1280]{1,0:T(8,128)(2,1)S(1)} %collective-permute-done.3.refs_2_) | copy-start | bytes 1843204
  23.0 8.6 %collective-permute-start.4 = (bf16[112,1280]{1,0:T(8,128)(2,1)S(1)}, bf16[112,1280]{1,0:T(8,128)(2,1)}, u32[]{:S(2)}, u32[]{:S(2)}) collective-permute-start(bf16[112,1280]{1,0:T(8,128)(2,1)S(1)} %slice.9), channel_id=1, source_target_pairs={{0,6},{1,7},{2,0},{3,1},{4,2},{5,3},{6,4},{7,5},{8,14},{9,15},{10,... | collective-permute-start | bytes 860168 | tf_op jit(solution)/shard_map/ppermute | solution.py:182
  33.5 18.2 %collective-permute-start.6 = (bf16[240,1280]{1,0:T(8,128)(2,1)}, bf16[240,1280]{1,0:T(8,128)(2,1)}, u32[]{:S(2)}, u32[]{:S(2)}) collective-permute-start(bf16[240,1280]{1,0:T(8,128)(2,1)} %collective-permute-done.5.refs_3_), channel_id=1, source_target_pairs={{0,2},{1,3},{2,4},{3,5},{4,6},{5,7},{6,0},{7,1},{8,10},{9,11},{10,... | collective-permute-start | bytes 1843208 | tf_op jit(solution)/shard_map/ppermute | solution.py:186
  33.5 18.2 %collective-permute-start.7 = (bf16[240,1280]{1,0:T(8,128)(2,1)}, bf16[240,1280]{1,0:T(8,128)(2,1)}, u32[]{:S(2)}, u32[]{:S(2)}) collective-permute-start(bf16[240,1280]{1,0:T(8,128)(2,1)} %collective-permute-done.5.refs_3_), channel_id=1, source_target_pairs={{0,6},{1,7},{2,0},{3,1},{4,2},{5,3},{6,4},{7,5},{8,14},{9,15},{10,... | collective-permute-start | bytes 1843208 | tf_op jit(solution)/shard_map/ppermute | solution.py:187
  36.2 15.5 %collective-permute-start.8 = (bf16[128,1280]{1,0:T(8,128)(2,1)}, bf16[128,1280]{1,0:T(8,128)(2,1)}, u32[]{:S(2)}, u32[]{:S(2)}) collective-permute-start(bf16[128,1280]{1,0:T(8,128)(2,1)} %collective-permute-done.2.refs_4_), channel_id=1, source_target_pairs={{0,72},{1,73},{2,74},{3,75},{4,76},{5,77},{6,78},{7,79},{8,64},{9,... | collective-permute-start | bytes 983048 | tf_op jit(solution)/shard_map/ppermute | solution.py:184
  36.4 15.3 %collective-permute-start.9 = (bf16[112,1280]{1,0:T(8,128)(2,1)}, bf16[112,1280]{1,0:T(8,128)(2,1)}, u32[]{:S(2)}, u32[]{:S(2)}) collective-permute-start(bf16[112,1280]{1,0:T(8,128)(2,1)} %collective-permute-done.4.refs_5_), channel_id=1, source_target_pairs={{0,72},{1,73},{2,74},{3,75},{4,76},{5,77},{6,78},{7,79},{8,64},{9,... | collective-permute-start | bytes 860168 | tf_op jit(solution)/shard_map/ppermute | solution.py:185
  38.9 1.0 copy-start
  56.4 39.7 %all-to-all-start = ((bf16[8,240,768]{2,1,0:T(8,128)(2,1)}), bf16[8,240,768]{2,1,0:T(8,128)(2,1)}, u32[]{:S(2)}, u32[]{:S(2)}) async-start(bf16[8,240,768]{2,1,0:T(8,128)(2,1)} %shard_map.111), calls=%async_computation | async-start | bytes 5898240 | tf_op jit(solution)/shard_map/all_to_all | solution.py:462
  154.4 22.5 %all-to-all-start.1 = ((bf16[16,80,384]{2,1,0:T(8,128)(2,1)}), bf16[16,80,384]{2,1,0:T(8,128)(2,1)S(1)}, u32[]{:S(2)}, u32[]{:S(2)}) async-start(bf16[16,80,384]{2,1,0:T(8,128)(2,1)} %shard_map.113), calls=%async_computation.1 | async-start | bytes 1966080 | tf_op jit(solution)/shard_map/all_to_all | solution.py:468
  176.9 1.0 copy-start.1

commit v8 on v7

--- a/solution.py
+++ b/solution.py
@@ -180,11 +180,12 @@
     half = 128
     far_top = lax.ppermute(below[:half], BOTH, Z_UP)
     far_bottom = lax.ppermute(above[half:], BOTH, Z_DOWN)
-    far_top, far_bottom, other = lax.optimization_barrier((far_top, far_bottom, other))
+    far_top, other_up = lax.optimization_barrier((far_top, other))
+    far_bottom, other_down = lax.optimization_barrier((far_bottom, other))
     other_far_top = lax.ppermute(far_top, BOTH, X_OTHER)
+    other_below = lax.ppermute(other_up, BOTH, Z_UP)
     other_far_bottom = lax.ppermute(far_bottom, BOTH, X_OTHER)
-    other_below = lax.ppermute(other, BOTH, Z_UP)
-    other_above = lax.ppermute(other, BOTH, Z_DOWN)
+    other_above = lax.ppermute(other_down, BOTH, Z_DOWN)
     return [far_top, far_bottom], [other_below, other_above, other_far_top, other_far_bottom]
 
 

time: 235 us -> 233 us (level)
  transfers between devices with their start and end apart: 12 -> 12, of which waited for: 5 -> 4; matrix products, arithmetic and copies ran while one was open for 0% -> 0% of each run, Pallas kernels for 9% -> 10%
where the time goes in v8:
time: 233 us
  Pallas kernels  97 us (42%)
  waiting for transfers between devices  60.8 us (26%)
  blocking collectives  44.4 us (19%)
  starting transfers between devices  28 us (12%)
    pallas_call x1, Pallas kernels, attend_full(): pl.pallas_call(functools.partial(attention_kernel, block=512, taken=taken...  58.3 us
    all_to_all x1, blocking collectives, on_device(): lax.all_to_all(send.reshape(128, 8, D + TAG), BOTH, split_axis=0, concat_...  44.4 us
    all_to_all x1, waiting for transfers between devices, on_device(): lax.all_to_all(projected, 'img', split_axis=0, concat_axis=0, tiled=True,...  34.4 us
    all_to_all x1, waiting for transfers between devices, on_device(): lax.all_to_all(attended, 'img', split_axis=0, concat_axis=0, tiled=True)  14.8 us
    pallas_call x1, Pallas kernels, layer_one(): pl.pallas_call(layer_one_kernel, out_shape=[jax.ShapeDtypeStruct((rows, D...  14.4 us
    pallas_call x2, Pallas kernels, project(): pl.pallas_call(functools.partial(project_kernel, parts=parts, offsets=off...  10.8 us
    pallas_call x1, Pallas kernels, merge(): pl.pallas_call(merge_kernel, out_shape=jax.ShapeDtypeStruct((places, D +...  7.8 us
    all_to_all x1, starting transfers between devices, on_device(): lax.all_to_all(attended, 'img', split_axis=0, concat_axis=0, tiled=True)  6 us
  transfers between devices with their start and end apart: 12, of which 4 were waited for; matrix products, arithmetic and copies ran while one was open for 0% of the time, Pallas kernels for 10%

profile of v8, /device:TPU:1, one launch (start us, length us, event | category | flops | bytes accessed | tf_op | source)
XLA Modules:
  0.0 233.0 jit_solution(17743438748269225627)
XLA Ops:
  0.0 3.3 %collective-permute-start.3 = (bf16[240,1280]{1,0:T(8,128)(2,1)}, bf16[240,1280]{1,0:T(8,128)(2,1)}, u32[]{:S(2)}, u32[]{:S(2)}) collective-permute-start(bf16[240,1280]{1,0:T(8,128)(2,1)} %bitcast.10), channel_id=1, source_target_pairs={{0,72},{1,73},{2,74},{3,75},{4,76},{5,77},{6,78},{7,79},{8,64},{9,... | collective-permute-start | bytes 1843208 | tf_op jit(solution)/shard_map/ppermute | solution.py:174
  3.3 1.6 collective-permute-start.1
  4.9 2.1 collective-permute-start.5
  7.1 14.4 %shard_map.109 = (bf16[384,1280]{1,0:T(8,128)(2,1)}, bf16[384,1280]{1,0:T(8,128)(2,1)}) custom-call(s32[1,384]{1,0:T(1,128)} %ids_ref.1, bf16[1,384,1280]{2,1,0:T(8,128)(2,1)} %x_ref.1, bf16[1280]{0:T(1024)(128)(2,1)} %gain_one_ref.1, bf16[1280]{0:T(1024)(128)(2,1)} %gain_two_ref.1, bf16[3,1280,1280]{2,1,0:T(8,128)(2,1)} %w_qkv_ref.1, ...), custom_call_target="tpu_custom_call" | custom-call | flops 6000000000 | bytes 16000000 | tf_op jit(solution)/shard_map/pallas_call | solution.py:124
  21.5 1.3 collective-permute-start
  22.8 0.1 collective-permute-start.2
  22.9 0.0 collective-permute-done.5.refs_2_
  23.0 2.7 %collective-permute-start.6 = (bf16[112,1280]{1,0:T(8,128)(2,1)S(1)}, bf16[112,1280]{1,0:T(8,128)(2,1)}, u32[]{:S(2)}, u32[]{:S(2)}) collective-permute-start(bf16[112,1280]{1,0:T(8,128)(2,1)S(1)} %slice.9), channel_id=1, source_target_pairs={{0,6},{1,7},{2,0},{3,1},{4,2},{5,3},{6,4},{7,5},{8,14},{9,15},{10,... | collective-permute-start | bytes 860168 | tf_op jit(solution)/shard_map/ppermute | solution.py:182
  25.7 0.0 collective-permute-done.3.refs_3_
  25.7 5.9 %collective-permute-done.6.refs_5_ = bf16[112,1280]{1,0:T(8,128)(2,1)} collective-permute-done((bf16[112,1280]{1,0:T(8,128)(2,1)S(1)}, bf16[112,1280]{1,0:T(8,128)(2,1)}, u32[]{:S(2)}, u32[]{:S(2)}) %collective-permute-start.6) | collective-permute-done | bytes 286752 | tf_op jit(solution)/shard_map/ppermute | solution.py:182
  31.6 3.5 %collective-permute-start.7 = (bf16[240,1280]{1,0:T(8,128)(2,1)}, bf16[240,1280]{1,0:T(8,128)(2,1)}, u32[]{:S(2)}, u32[]{:S(2)}) collective-permute-start(bf16[240,1280]{1,0:T(8,128)(2,1)} %collective-permute-done.3.refs_3_), channel_id=1, source_target_pairs={{0,6},{1,7},{2,0},{3,1},{4,2},{5,3},{6,4},{7,5},{8,14},{9,15},{10,... | collective-permute-start | bytes 1843208 | tf_op jit(solution)/shard_map/ppermute | solution.py:188
  35.1 0.0 collective-permute-done.2.refs_4_
  35.1 0.0 collective-permute-start.4
  35.1 0.2 collective-permute-start.8
  35.3 2.5 %collective-permute-start.9 = (bf16[112,1280]{1,0:T(8,128)(2,1)}, bf16[112,1280]{1,0:T(8,128)(2,1)}, u32[]{:S(2)}, u32[]{:S(2)}) collective-permute-start(bf16[112,1280]{1,0:T(8,128)(2,1)} %collective-permute-done.6.refs_5_), channel_id=1, source_target_pairs={{0,72},{1,73},{2,74},{3,75},{4,76},{5,77},{6,78},{7,79},{8,64},{9,... | collective-permute-start | bytes 860168 | tf_op jit(solution)/shard_map/ppermute | solution.py:187
  37.8 1.0 copy-done
  38.7 6.1 %shard_map.110.refs_4_ = bf16[8,240,768]{2,1,0:T(8,128)(2,1)} custom-call(bf16[384,1280]{1,0:T(8,128)(2,1)} %get-tuple-element.14.h_own_ref, bf16[384,1280]{1,0:T(8,128)(2,1)} %copy-done, bf16[240,1280]{1,0:T(8,128)(2,1)} %bitcast.13, bf16[240,1280]{1,0:T(8,128)(2,1)} %copy-done.2, bf16[240,1280]{1,0:T(8,128)(2,1)} %copy-done.3, ...), custom_call_target="tpu_custom_call" | custom-call | flops 2000000000 | bytes 6000000 | tf_op jit(solution)/shard_map/pallas_call | solution.py:235
  44.9 5.7 %collective-permute-done.9.refs_3_ = bf16[112,1280]{1,0:T(8,128)(2,1)} collective-permute-done((bf16[112,1280]{1,0:T(8,128)(2,1)}, bf16[112,1280]{1,0:T(8,128)(2,1)}, u32[]{:S(2)}, u32[]{:S(2)}) %collective-permute-start.9) | collective-permute-done | bytes 286752 | tf_op jit(solution)/shard_map/ppermute | solution.py:187
  50.6 0.0 collective-permute-done.8.refs_2_
  50.6 0.0 collective-permute-done.7.refs_1_
  50.6 0.0 collective-permute-done.4.refs_0_
  50.6 4.7 %shard_map.111 = bf16[8,240,768]{2,1,0:T(8,128)(2,1)} custom-call(bf16[384,1280]{1,0:T(8,128)(2,1)} %get-tuple-element.14.h_own_ref, bf16[384,1280]{1,0:T(8,128)(2,1)} %copy-done, bf16[240,1280]{1,0:T(8,128)(2,1)} %collective-permute-done.4.refs_0_, bf16[240,1280]{1,0:T(8,128)(2,1)} %collective-permute-done.7.refs_1_, ...), custom_call_target="tpu_custom_call", output_to_operand_aliasing={{}: (6, {})} | custom-call | flops 2000000000 | bytes 6000000 | tf_op jit(solution)/shard_map/pallas_call | solution.py:235
  55.3 4.7 %all-to-all-start = ((bf16[8,240,768]{2,1,0:T(8,128)(2,1)}), bf16[8,240,768]{2,1,0:T(8,128)(2,1)}, u32[]{:S(2)}, u32[]{:S(2)}) async-start(bf16[8,240,768]{2,1,0:T(8,128)(2,1)} %shard_map.111), calls=%async_computation | async-start | bytes 5898240 | tf_op jit(solution)/shard_map/all_to_all | solution.py:463
  60.6 34.4 %all-to-all-done.all_hbm = bf16[8,240,768]{2,1,0:T(8,128)(2,1)} async-done(((bf16[8,240,768]{2,1,0:T(8,128)(2,1)}), bf16[8,240,768]{2,1,0:T(8,128)(2,1)}, u32[]{:S(2)}, u32[]{:S(2)}) %all-to-all-start) | async-done | bytes 2949152 | tf_op jit(solution)/shard_map/all_to_all | solution.py:463
  95.0 58.3 %shard_map.113 = bf16[16,80,384]{2,1,0:T(8,128)(2,1)} custom-call(s32[1]{0:T(128)S(6)} %copy.14.count_ref, bf16[8,240,768]{2,1,0:T(8,128)(2,1)} %all-to-all-done.all_hbm), custom_call_target="tpu_custom_call" | custom-call | tf_op jit(solution)/shard_map/pallas_call | solution.py:345
  153.3 6.0 %all-to-all-start.1 = ((bf16[16,80,384]{2,1,0:T(8,128)(2,1)}), bf16[16,80,384]{2,1,0:T(8,128)(2,1)S(1)}, u32[]{:S(2)}, u32[]{:S(2)}) async-start(bf16[16,80,384]{2,1,0:T(8,128)(2,1)} %shard_map.113), calls=%async_computation.1 | async-start | bytes 1966080 | tf_op jit(solution)/shard_map/all_to_all | solution.py:469
  159.3 1.7 shard_map.112
  160.9 14.8 %all-to-all-done.1 = bf16[16,80,384]{2,1,0:T(8,128)(2,1)S(1)} async-done(((bf16[16,80,384]{2,1,0:T(8,128)(2,1)}), bf16[16,80,384]{2,1,0:T(8,128)(2,1)S(1)}, u32[]{:S(2)}, u32[]{:S(2)}) %all-to-all-start.1) | async-done | bytes 983072 | tf_op jit(solution)/shard_map/all_to_all | solution.py:469
  175.8 1.0 copy-done.1
  176.7 7.8 %shard_map.114 = bf16[1024,1408]{1,0:T(8,128)(2,1)} custom-call(s32[1,384]{1,0:T(1,128)} %get-tuple-element.20.bucket_ref, bf16[384,128]{1,0:T(8,128)(2,1)} %get-tuple-element.21.tag_ref, bf16[1280,384]{1,0:T(8,128)(2,1)} %bitcast.9, bf16[384,1280]{1,0:T(8,128)(2,1)} %get-tuple-element.22.x_ref, bf16[1280,1280]{1,0:T(8,128)(2,1)} %w_ref.1, ...), custom_call_target="tpu_custom_call" | custom-call | tf_op jit(solution)/shard_map/pallas_call | solution.py:380
  184.5 44.4 %all_to_all.15 = bf16[128,8,1408]{2,1,0:T(8,128)(2,1)} all-to-all(bf16[128,8,1408]{2,1,0:T(8,128)(2,1)} %bitcast.7), channel_id=1, replica_groups=mesh['ctx'=8,'img'=16] {'ctx','img'}, dimensions={0} | all-to-all | bytes 5767168 | tf_op jit(solution)/shard_map/all_to_all | solution.py:472
  229.0 4.0 %shard_map.115 = bf16[96,5120]{1,0:T(8,128)(2,1)} custom-call(bf16[1024,1408]{1,0:T(8,128)(2,1)} %bitcast.8), custom_call_target="tpu_custom_call" | custom-call | tf_op jit(solution)/shard_map/pallas_call | solution.py:403
  (10 shorter events, 0.1 us)
Async XLA Ops:
  0.0 25.7 %collective-permute-start.3 = (bf16[240,1280]{1,0:T(8,128)(2,1)}, bf16[240,1280]{1,0:T(8,128)(2,1)}, u32[]{:S(2)}, u32[]{:S(2)}) collective-permute-start(bf16[240,1280]{1,0:T(8,128)(2,1)} %bitcast.10), channel_id=1, source_target_pairs={{0,72},{1,73},{2,74},{3,75},{4,76},{5,77},{6,78},{7,79},{8,64},{9,... | collective-permute-start | bytes 1843208 | tf_op jit(solution)/shard_map/ppermute | solution.py:174
  3.3 19.5 %collective-permute-start.1 = (bf16[240,1280]{1,0:T(8,128)(2,1)}, bf16[240,1280]{1,0:T(8,128)(2,1)S(1)}, u32[]{:S(2)}, u32[]{:S(2)}) collective-permute-start(bf16[240,1280]{1,0:T(8,128)(2,1)} %bitcast.11), channel_id=1, source_target_pairs={{0,2},{1,3},{2,4},{3,5},{4,6},{5,7},{6,0},{7,1},{8,10},{9,11},{10,... | collective-permute-start | bytes 1843208 | tf_op jit(solution)/shard_map/ppermute | solution.py:172
  4.9 18.0 %collective-permute-start.5 = (bf16[240,1280]{1,0:T(8,128)(2,1)}, bf16[240,1280]{1,0:T(8,128)(2,1)S(1)}, u32[]{:S(2)}, u32[]{:S(2)}) collective-permute-start(bf16[240,1280]{1,0:T(8,128)(2,1)} %bitcast.12), channel_id=1, source_target_pairs={{0,6},{1,7},{2,0},{3,1},{4,2},{5,3},{6,4},{7,5},{8,14},{9,15},{10,... | collective-permute-start | bytes 1843208 | tf_op jit(solution)/shard_map/ppermute | solution.py:173
  21.5 16.3 %collective-permute-start = (bf16[384,1280]{1,0:T(8,128)(2,1)}, bf16[384,1280]{1,0:T(8,128)(2,1)S(1)}, u32[]{:S(2)}, u32[]{:S(2)}) collective-permute-start(bf16[384,1280]{1,0:T(8,128)(2,1)} %get-tuple-element.14.h_own_ref), channel_id=1, source_target_pairs={{0,1},{1,0},{2,3},{3,2},{4,5},{5,4},{6,7},{7,6},{8,9},{9,8},{10,11... | collective-permute-start | bytes 2949128 | tf_op jit(solution)/shard_map/ppermute | solution.py:459
  22.8 12.5 %copy-start.2 = (bf16[240,1280]{1,0:T(8,128)(2,1)}, bf16[240,1280]{1,0:T(8,128)(2,1)S(1)}, u32[]{:S(2)}) copy-start(bf16[240,1280]{1,0:T(8,128)(2,1)S(1)} %collective-permute-done.1.refs_1_) | copy-start | bytes 1843204
  22.8 12.3 %collective-permute-start.2 = (bf16[128,1280]{1,0:T(8,128)(2,1)S(1)}, bf16[128,1280]{1,0:T(8,128)(2,1)}, u32[]{:S(2)}, u32[]{:S(2)}) collective-permute-start(bf16[128,1280]{1,0:T(8,128)(2,1)S(1)} %slice.8), channel_id=1, source_target_pairs={{0,2},{1,3},{2,4},{3,5},{4,6},{5,7},{6,0},{7,1},{8,10},{9,11},{10,... | collective-permute-start | bytes 983048 | tf_op jit(solution)/shard_map/ppermute | solution.py:181
  22.9 14.9 %copy-start.3 = (bf16[240,1280]{1,0:T(8,128)(2,1)}, bf16[240,1280]{1,0:T(8,128)(2,1)S(1)}, u32[]{:S(2)}) copy-start(bf16[240,1280]{1,0:T(8,128)(2,1)S(1)} %collective-permute-done.5.refs_2_) | copy-start | bytes 1843204
  23.0 8.6 %collective-permute-start.6 = (bf16[112,1280]{1,0:T(8,128)(2,1)S(1)}, bf16[112,1280]{1,0:T(8,128)(2,1)}, u32[]{:S(2)}, u32[]{:S(2)}) collective-permute-start(bf16[112,1280]{1,0:T(8,128)(2,1)S(1)} %slice.9), channel_id=1, source_target_pairs={{0,6},{1,7},{2,0},{3,1},{4,2},{5,3},{6,4},{7,5},{8,14},{9,15},{10,... | collective-permute-start | bytes 860168 | tf_op jit(solution)/shard_map/ppermute | solution.py:182
  31.6 19.0 %collective-permute-start.7 = (bf16[240,1280]{1,0:T(8,128)(2,1)}, bf16[240,1280]{1,0:T(8,128)(2,1)}, u32[]{:S(2)}, u32[]{:S(2)}) collective-permute-start(bf16[240,1280]{1,0:T(8,128)(2,1)} %collective-permute-done.3.refs_3_), channel_id=1, source_target_pairs={{0,6},{1,7},{2,0},{3,1},{4,2},{5,3},{6,4},{7,5},{8,14},{9,15},{10,... | collective-permute-start | bytes 1843208 | tf_op jit(solution)/shard_map/ppermute | solution.py:188
  35.1 15.5 %collective-permute-start.4 = (bf16[240,1280]{1,0:T(8,128)(2,1)}, bf16[240,1280]{1,0:T(8,128)(2,1)}, u32[]{:S(2)}, u32[]{:S(2)}) collective-permute-start(bf16[240,1280]{1,0:T(8,128)(2,1)} %collective-permute-done.3.refs_3_), channel_id=1, source_target_pairs={{0,2},{1,3},{2,4},{3,5},{4,6},{5,7},{6,0},{7,1},{8,10},{9,11},{10,... | collective-permute-start | bytes 1843208 | tf_op jit(solution)/shard_map/ppermute | solution.py:186
  35.1 15.5 %collective-permute-start.8 = (bf16[128,1280]{1,0:T(8,128)(2,1)}, bf16[128,1280]{1,0:T(8,128)(2,1)}, u32[]{:S(2)}, u32[]{:S(2)}) collective-permute-start(bf16[128,1280]{1,0:T(8,128)(2,1)} %collective-permute-done.2.refs_4_), channel_id=1, source_target_pairs={{0,72},{1,73},{2,74},{3,75},{4,76},{5,77},{6,78},{7,79},{8,64},{9,... | collective-permute-start | bytes 983048 | tf_op jit(solution)/shard_map/ppermute | solution.py:185
  35.3 15.3 %collective-permute-start.9 = (bf16[112,1280]{1,0:T(8,128)(2,1)}, bf16[112,1280]{1,0:T(8,128)(2,1)}, u32[]{:S(2)}, u32[]{:S(2)}) collective-permute-start(bf16[112,1280]{1,0:T(8,128)(2,1)} %collective-permute-done.6.refs_5_), channel_id=1, source_target_pairs={{0,72},{1,73},{2,74},{3,75},{4,76},{5,77},{6,78},{7,79},{8,64},{9,... | collective-permute-start | bytes 860168 | tf_op jit(solution)/shard_map/ppermute | solution.py:187
  37.8 1.0 copy-start
  55.3 39.7 %all-to-all-start = ((bf16[8,240,768]{2,1,0:T(8,128)(2,1)}), bf16[8,240,768]{2,1,0:T(8,128)(2,1)}, u32[]{:S(2)}, u32[]{:S(2)}) async-start(bf16[8,240,768]{2,1,0:T(8,128)(2,1)} %shard_map.111), calls=%async_computation | async-start | bytes 5898240 | tf_op jit(solution)/shard_map/all_to_all | solution.py:463
  153.3 22.5 %all-to-all-start.1 = ((bf16[16,80,384]{2,1,0:T(8,128)(2,1)}), bf16[16,80,384]{2,1,0:T(8,128)(2,1)S(1)}, u32[]{:S(2)}, u32[]{:S(2)}) async-start(bf16[16,80,384]{2,1,0:T(8,128)(2,1)} %shard_map.113), calls=%async_computation.1 | async-start | bytes 1966080 | tf_op jit(solution)/shard_map/all_to_all | solution.py:469
  175.8 1.0 copy-start.1

commit v9 on v8

--- a/solution.py
+++ b/solution.py
@@ -175,18 +175,19 @@
     return [shard, below, above, other]
 
 
-def far_shards(near):
+def far_shards(near, partner):
     shard, below, above, other = near
     half = 128
     far_top = lax.ppermute(below[:half], BOTH, Z_UP)
     far_bottom = lax.ppermute(above[half:], BOTH, Z_DOWN)
-    far_top, other_up = lax.optimization_barrier((far_top, other))
-    far_bottom, other_down = lax.optimization_barrier((far_bottom, other))
     other_far_top = lax.ppermute(far_top, BOTH, X_OTHER)
+    other_far_bottom = lax.ppermute(far_bottom, BOTH, X_OTHER)
+    far_top, other_up, partner = lax.optimization_barrier((far_top, other, partner))
+    far_bottom, other_down, partner = lax.optimization_barrier((far_bottom, other, partner))
     other_below = lax.ppermute(other_up, BOTH, Z_UP)
-    other_far_bottom = lax.ppermute(far_bottom, BOTH, X_OTHER)
     other_above = lax.ppermute(other_down, BOTH, Z_DOWN)
-    return [far_top, far_bottom], [other_below, other_above, other_far_top, other_far_bottom]
+    last = [other_below, other_above, other_far_top, other_far_bottom]
+    return [far_top, far_bottom], last, partner
 
 
 def project_kernel(h_own_ref, h_partner_ref, *refs, parts, offsets, aliased):
@@ -452,11 +453,11 @@
 ):
     shard = jnp.swapaxes(w_qkv2, 1, 2).reshape(3 * HEAD_DIM, D)
     near = near_shards(shard)
-    far, last = far_shards(near)
 
     second, hidden = layer_one(window_ids, patches, gain_one, gain_two, w_qkv1, w_out1)
 
     partner = lax.ppermute(hidden, BOTH, CORE_SWAP)
+    far, last, partner = far_shards(near, partner)
     projected = project(NEAR_OFFSETS, hidden, partner, near + far, (1, 1, 1, 1, 2))
     projected = project(FAR_OFFSETS, hidden, partner, last, (1, 1, 2), into=projected)
     groups = [[2 * chip + core for chip in range(8)] for core in range(2)]

time: 233 us -> 245 us (1.052)
  waiting for transfers between devices: 60.8 us -> 74.5 us
  starting transfers between devices: 28 us -> 25.5 us
    ppermute x1, waiting for transfers between devices: 0.01 us -> 11.8 us  [near_shards(): below = lax.ppermute(shard, BOTH, Z_UP)]
    ppermute x1, waiting for transfers between devices: 0.01 us -> 7.24 us  [far_shards(): far_top = lax.ppermute(below[:half], BOTH, Z_UP)]
    ppermute x1, waiting for transfers between devices: 5.91 us -> 0.01 us  [far_shards(): far_bottom = lax.ppermute(above[half:], BOTH, Z_DOWN)]
  transfers between devices with their start and end apart: 12 -> 12, of which waited for: 4 -> 5; matrix products, arithmetic and copies ran while one was open for 0% -> 0% of each run, Pallas kernels for 10% -> 3%
where the time goes in v9:
time: 245 us
  Pallas kernels  97 us (40%)
  waiting for transfers between devices  74.5 us (30%)
  blocking collectives  46 us (19%)
  starting transfers between devices  25.5 us (10%)
    pallas_call x1, Pallas kernels, attend_full(): pl.pallas_call(functools.partial(attention_kernel, block=512, taken=taken...  58.3 us
    all_to_all x1, blocking collectives, on_device(): lax.all_to_all(send.reshape(128, 8, D + TAG), BOTH, split_axis=0, concat_...  46 us
    all_to_all x1, waiting for transfers between devices, on_device(): lax.all_to_all(projected, 'img', split_axis=0, concat_axis=0, tiled=True,...  34.7 us
    all_to_all x1, waiting for transfers between devices, on_device(): lax.all_to_all(attended, 'img', split_axis=0, concat_axis=0, tiled=True)  14.8 us
    pallas_call x1, Pallas kernels, layer_one(): pl.pallas_call(layer_one_kernel, out_shape=[jax.ShapeDtypeStruct((rows, D...  14.4 us
    ppermute x1, waiting for transfers between devices, near_shards(): below = lax.ppermute(shard, BOTH, Z_UP)  11.8 us
    pallas_call x2, Pallas kernels, project(): pl.pallas_call(functools.partial(project_kernel, parts=parts, offsets=off...  10.8 us
    pallas_call x1, Pallas kernels, merge(): pl.pallas_call(merge_kernel, out_shape=jax.ShapeDtypeStruct((places, D +...  7.8 us
  transfers between devices with their start and end apart: 12, of which 5 were waited for; matrix products, arithmetic and copies ran while one was open for 0% of the time, Pallas kernels for 3%

profile of v9, /device:TPU:1, one launch (start us, length us, event | category | flops | bytes accessed | tf_op | source)
XLA Modules:
  0.0 244.8 jit_solution(9483074044968751272)
XLA Ops:
  0.0 14.4 %shard_map.109 = (bf16[384,1280]{1,0:T(8,128)(2,1)}, bf16[384,1280]{1,0:T(8,128)(2,1)}) custom-call(s32[1,384]{1,0:T(1,128)} %ids_ref.1, bf16[1,384,1280]{2,1,0:T(8,128)(2,1)} %x_ref.1, bf16[1280]{0:T(1024)(128)(2,1)} %gain_one_ref.1, bf16[1280]{0:T(1024)(128)(2,1)} %gain_two_ref.1, bf16[3,1280,1280]{2,1,0:T(8,128)(2,1)} %w_qkv_ref.1, ...), custom_call_target="tpu_custom_call" | custom-call | flops 6000000000 | bytes 16000000 | tf_op jit(solution)/shard_map/pallas_call | solution.py:124
  14.5 1.5 collective-permute-start.5
  16.0 1.7 collective-permute-start.3
  17.7 2.1 collective-permute-start
  19.8 2.5 %collective-permute-start.2 = (bf16[240,1280]{1,0:T(8,128)(2,1)S(1)}, bf16[240,1280]{1,0:T(8,128)(2,1)}, u32[]{:S(2)}, u32[]{:S(2)}) collective-permute-start(bf16[240,1280]{1,0:T(8,128)(2,1)S(1)} %bitcast.13), channel_id=1, source_target_pairs={{0,72},{1,73},{2,74},{3,75},{4,76},{5,77},{6,78},{7,79},{8,64},{9,... | collective-permute-start | bytes 1843208 | tf_op jit(solution)/shard_map/ppermute | solution.py:174
  22.3 11.8 %collective-permute-done.3.refs_1_ = bf16[240,1280]{1,0:T(8,128)(2,1)S(1)} collective-permute-done((bf16[240,1280]{1,0:T(8,128)(2,1)S(1)}, bf16[240,1280]{1,0:T(8,128)(2,1)S(1)}, u32[]{:S(2)}, u32[]{:S(2)}) %collective-permute-start.3) | collective-permute-done | bytes 614432 | tf_op jit(solution)/shard_map/ppermute | solution.py:172
  34.1 0.1 collective-permute-start.4
  34.2 0.0 collective-permute-done.refs_2_
  34.2 2.7 %collective-permute-start.1 = (bf16[112,1280]{1,0:T(8,128)(2,1)S(1)}, bf16[112,1280]{1,0:T(8,128)(2,1)}, u32[]{:S(2)}, u32[]{:S(2)}) collective-permute-start(bf16[112,1280]{1,0:T(8,128)(2,1)S(1)} %slice.8), channel_id=1, source_target_pairs={{0,6},{1,7},{2,0},{3,1},{4,2},{5,3},{6,4},{7,5},{8,14},{9,15},{10,... | collective-permute-start | bytes 860168 | tf_op jit(solution)/shard_map/ppermute | solution.py:182
  36.9 0.0 collective-permute-done.2.refs_3_
  36.9 7.2 %collective-permute-done.4.refs_4_ = bf16[128,1280]{1,0:T(8,128)(2,1)} collective-permute-done((bf16[128,1280]{1,0:T(8,128)(2,1)S(1)}, bf16[128,1280]{1,0:T(8,128)(2,1)}, u32[]{:S(2)}, u32[]{:S(2)}) %collective-permute-start.4) | collective-permute-done | bytes 327712 | tf_op jit(solution)/shard_map/ppermute | solution.py:181
  44.2 0.0 collective-permute-done.5.h_partner_ref
  44.2 1.6 collective-permute-start.7
  45.7 0.0 collective-permute-start.6
  45.7 2.5 %collective-permute-start.8 = (bf16[128,1280]{1,0:T(8,128)(2,1)}, bf16[128,1280]{1,0:T(8,128)(2,1)}, u32[]{:S(2)}, u32[]{:S(2)}) collective-permute-start(bf16[128,1280]{1,0:T(8,128)(2,1)} %collective-permute-done.4.refs_4_), channel_id=1, source_target_pairs={{0,72},{1,73},{2,74},{3,75},{4,76},{5,77},{6,78},{7,79},{8,64},{9,... | collective-permute-start | bytes 983048 | tf_op jit(solution)/shard_map/ppermute | solution.py:183
  48.2 0.2 collective-permute-start.9
  48.4 6.1 %shard_map.110.refs_4_ = bf16[8,240,768]{2,1,0:T(8,128)(2,1)} custom-call(bf16[384,1280]{1,0:T(8,128)(2,1)} %get-tuple-element.16.h_own_ref, bf16[384,1280]{1,0:T(8,128)(2,1)} %copy-done, bf16[240,1280]{1,0:T(8,128)(2,1)} %bitcast.10, bf16[240,1280]{1,0:T(8,128)(2,1)} %copy-done.2, bf16[240,1280]{1,0:T(8,128)(2,1)} %copy-done.3, ...), custom_call_target="tpu_custom_call" | custom-call | flops 2000000000 | bytes 6000000 | tf_op jit(solution)/shard_map/pallas_call | solution.py:236
  54.6 6.0 %collective-permute-done.9.refs_3_ = bf16[112,1280]{1,0:T(8,128)(2,1)} collective-permute-done((bf16[112,1280]{1,0:T(8,128)(2,1)}, bf16[112,1280]{1,0:T(8,128)(2,1)}, u32[]{:S(2)}, u32[]{:S(2)}) %collective-permute-start.9) | collective-permute-done | bytes 286752 | tf_op jit(solution)/shard_map/ppermute | solution.py:184
  60.6 0.0 collective-permute-done.8.refs_2_
  60.6 0.0 collective-permute-done.7.refs_1_
  60.6 0.0 collective-permute-done.6.refs_0_
  60.6 4.7 %shard_map.111 = bf16[8,240,768]{2,1,0:T(8,128)(2,1)} custom-call(bf16[384,1280]{1,0:T(8,128)(2,1)} %get-tuple-element.16.h_own_ref, bf16[384,1280]{1,0:T(8,128)(2,1)} %copy-done, bf16[240,1280]{1,0:T(8,128)(2,1)} %collective-permute-done.6.refs_0_, bf16[240,1280]{1,0:T(8,128)(2,1)} %collective-permute-done.7.refs_1_, ...), custom_call_target="tpu_custom_call", output_to_operand_aliasing={{}: (6, {})} | custom-call | flops 2000000000 | bytes 6000000 | tf_op jit(solution)/shard_map/pallas_call | solution.py:236
  65.3 4.6 %all-to-all-start = ((bf16[8,240,768]{2,1,0:T(8,128)(2,1)}), bf16[8,240,768]{2,1,0:T(8,128)(2,1)}, u32[]{:S(2)}, u32[]{:S(2)}) async-start(bf16[8,240,768]{2,1,0:T(8,128)(2,1)} %shard_map.111), calls=%async_computation | async-start | bytes 5898240 | tf_op jit(solution)/shard_map/all_to_all | solution.py:464
  70.6 34.7 %all-to-all-done.all_hbm = bf16[8,240,768]{2,1,0:T(8,128)(2,1)} async-done(((bf16[8,240,768]{2,1,0:T(8,128)(2,1)}), bf16[8,240,768]{2,1,0:T(8,128)(2,1)}, u32[]{:S(2)}, u32[]{:S(2)}) %all-to-all-start) | async-done | bytes 2949152 | tf_op jit(solution)/shard_map/all_to_all | solution.py:464
  105.3 58.3 %shard_map.113 = bf16[16,80,384]{2,1,0:T(8,128)(2,1)} custom-call(s32[1]{0:T(128)S(6)} %copy.14.count_ref, bf16[8,240,768]{2,1,0:T(8,128)(2,1)} %all-to-all-done.all_hbm), custom_call_target="tpu_custom_call" | custom-call | tf_op jit(solution)/shard_map/pallas_call | solution.py:346
  163.5 6.0 %all-to-all-start.1 = ((bf16[16,80,384]{2,1,0:T(8,128)(2,1)}), bf16[16,80,384]{2,1,0:T(8,128)(2,1)S(1)}, u32[]{:S(2)}, u32[]{:S(2)}) async-start(bf16[16,80,384]{2,1,0:T(8,128)(2,1)} %shard_map.113), calls=%async_computation.1 | async-start | bytes 1966080 | tf_op jit(solution)/shard_map/all_to_all | solution.py:470
  169.6 1.7 shard_map.112
  171.3 14.8 %all-to-all-done.1 = bf16[16,80,384]{2,1,0:T(8,128)(2,1)S(1)} async-done(((bf16[16,80,384]{2,1,0:T(8,128)(2,1)}), bf16[16,80,384]{2,1,0:T(8,128)(2,1)S(1)}, u32[]{:S(2)}, u32[]{:S(2)}) %all-to-all-start.1) | async-done | bytes 983072 | tf_op jit(solution)/shard_map/all_to_all | solution.py:470
  186.1 1.0 copy-done.1
  187.0 7.8 %shard_map.114 = bf16[1024,1408]{1,0:T(8,128)(2,1)} custom-call(s32[1,384]{1,0:T(1,128)} %get-tuple-element.24.bucket_ref, bf16[384,128]{1,0:T(8,128)(2,1)} %get-tuple-element.25.tag_ref, bf16[1280,384]{1,0:T(8,128)(2,1)} %bitcast.9, bf16[384,1280]{1,0:T(8,128)(2,1)} %get-tuple-element.26.x_ref, bf16[1280,1280]{1,0:T(8,128)(2,1)} %w_ref.1, ...), custom_call_target="tpu_custom_call" | custom-call | tf_op jit(solution)/shard_map/pallas_call | solution.py:381
  194.8 46.0 %all_to_all.15 = bf16[128,8,1408]{2,1,0:T(8,128)(2,1)} all-to-all(bf16[128,8,1408]{2,1,0:T(8,128)(2,1)} %bitcast.7), channel_id=1, replica_groups=mesh['ctx'=8,'img'=16] {'ctx','img'}, dimensions={0} | all-to-all | bytes 5767168 | tf_op jit(solution)/shard_map/all_to_all | solution.py:473
  240.8 4.0 %shard_map.115 = bf16[96,5120]{1,0:T(8,128)(2,1)} custom-call(bf16[1024,1408]{1,0:T(8,128)(2,1)} %bitcast.8), custom_call_target="tpu_custom_call" | custom-call | tf_op jit(solution)/shard_map/pallas_call | solution.py:404
  (12 shorter events, 0.1 us)
Async XLA Ops:
  0.0 16.0 %copy-start.4 = (bf16[3,1280,80]{1,2,0:T(8,128)(2,1)S(1)}, bf16[3,1280,80]{1,2,0:T(8,128)(2,1)}, u32[]{:S(2)}) copy-start(bf16[3,1280,80]{1,2,0:T(8,128)(2,1)} %param.18) | copy-start | bytes 1843204
  14.5 29.7 %collective-permute-start.5 = (bf16[384,1280]{1,0:T(8,128)(2,1)}, bf16[384,1280]{1,0:T(8,128)(2,1)S(1)}, u32[]{:S(2)}, u32[]{:S(2)}) collective-permute-start(bf16[384,1280]{1,0:T(8,128)(2,1)} %get-tuple-element.16.h_own_ref), channel_id=1, source_target_pairs={{0,1},{1,0},{2,3},{3,2},{4,5},{5,4},{6,7},{7,6},{8,9},{9,8},{10,11... | collective-permute-start | bytes 2949128 | tf_op jit(solution)/shard_map/ppermute | solution.py:459
  16.0 18.1 %collective-permute-start.3 = (bf16[240,1280]{1,0:T(8,128)(2,1)S(1)}, bf16[240,1280]{1,0:T(8,128)(2,1)S(1)}, u32[]{:S(2)}, u32[]{:S(2)}) collective-permute-start(bf16[240,1280]{1,0:T(8,128)(2,1)S(1)} %bitcast.11), channel_id=1, source_target_pairs={{0,2},{1,3},{2,4},{3,5},{4,6},{5,7},{6,0},{7,1},{8,10},{9,11},{10,... | collective-permute-start | bytes 1843208 | tf_op jit(solution)/shard_map/ppermute | solution.py:172
  17.7 16.5 %collective-permute-start = (bf16[240,1280]{1,0:T(8,128)(2,1)S(1)}, bf16[240,1280]{1,0:T(8,128)(2,1)S(1)}, u32[]{:S(2)}, u32[]{:S(2)}) collective-permute-start(bf16[240,1280]{1,0:T(8,128)(2,1)S(1)} %bitcast.12), channel_id=1, source_target_pairs={{0,6},{1,7},{2,0},{3,1},{4,2},{5,3},{6,4},{7,5},{8,14},{9,15},{10,... | collective-permute-start | bytes 1843208 | tf_op jit(solution)/shard_map/ppermute | solution.py:173
  19.8 17.1 %collective-permute-start.2 = (bf16[240,1280]{1,0:T(8,128)(2,1)S(1)}, bf16[240,1280]{1,0:T(8,128)(2,1)}, u32[]{:S(2)}, u32[]{:S(2)}) collective-permute-start(bf16[240,1280]{1,0:T(8,128)(2,1)S(1)} %bitcast.13), channel_id=1, source_target_pairs={{0,72},{1,73},{2,74},{3,75},{4,76},{5,77},{6,78},{7,79},{8,64},{9,... | collective-permute-start | bytes 1843208 | tf_op jit(solution)/shard_map/ppermute | solution.py:174
  34.0 10.1 %copy-start.2 = (bf16[240,1280]{1,0:T(8,128)(2,1)}, bf16[240,1280]{1,0:T(8,128)(2,1)S(1)}, u32[]{:S(2)}) copy-start(bf16[240,1280]{1,0:T(8,128)(2,1)S(1)} %collective-permute-done.3.refs_1_) | copy-start | bytes 1843204
  34.1 10.1 %collective-permute-start.4 = (bf16[128,1280]{1,0:T(8,128)(2,1)S(1)}, bf16[128,1280]{1,0:T(8,128)(2,1)}, u32[]{:S(2)}, u32[]{:S(2)}) collective-permute-start(bf16[128,1280]{1,0:T(8,128)(2,1)S(1)} %slice.9), channel_id=1, source_target_pairs={{0,2},{1,3},{2,4},{3,5},{4,6},{5,7},{6,0},{7,1},{8,10},{9,11},{10,... | collective-permute-start | bytes 983048 | tf_op jit(solution)/shard_map/ppermute | solution.py:181
  34.2 10.0 %copy-start.3 = (bf16[240,1280]{1,0:T(8,128)(2,1)}, bf16[240,1280]{1,0:T(8,128)(2,1)S(1)}, u32[]{:S(2)}) copy-start(bf16[240,1280]{1,0:T(8,128)(2,1)S(1)} %collective-permute-done.refs_2_) | copy-start | bytes 1843204
  34.2 10.0 %collective-permute-start.1 = (bf16[112,1280]{1,0:T(8,128)(2,1)S(1)}, bf16[112,1280]{1,0:T(8,128)(2,1)}, u32[]{:S(2)}, u32[]{:S(2)}) collective-permute-start(bf16[112,1280]{1,0:T(8,128)(2,1)S(1)} %slice.8), channel_id=1, source_target_pairs={{0,6},{1,7},{2,0},{3,1},{4,2},{5,3},{6,4},{7,5},{8,14},{9,15},{10,... | collective-permute-start | bytes 860168 | tf_op jit(solution)/shard_map/ppermute | solution.py:182
  44.2 4.3 %copy-start = (bf16[384,1280]{1,0:T(8,128)(2,1)}, bf16[384,1280]{1,0:T(8,128)(2,1)S(1)}, u32[]{:S(2)}) copy-start(bf16[384,1280]{1,0:T(8,128)(2,1)S(1)} %collective-permute-done.5.h_partner_ref) | copy-start | bytes 2949124
  44.2 16.4 %collective-permute-start.7 = (bf16[240,1280]{1,0:T(8,128)(2,1)}, bf16[240,1280]{1,0:T(8,128)(2,1)}, u32[]{:S(2)}, u32[]{:S(2)}) collective-permute-start(bf16[240,1280]{1,0:T(8,128)(2,1)} %collective-permute-done.2.refs_3_), channel_id=1, source_target_pairs={{0,6},{1,7},{2,0},{3,1},{4,2},{5,3},{6,4},{7,5},{8,14},{9,15},{10,... | collective-permute-start | bytes 1843208 | tf_op jit(solution)/shard_map/ppermute | solution.py:188
  45.7 14.9 %collective-permute-start.6 = (bf16[240,1280]{1,0:T(8,128)(2,1)}, bf16[240,1280]{1,0:T(8,128)(2,1)}, u32[]{:S(2)}, u32[]{:S(2)}) collective-permute-start(bf16[240,1280]{1,0:T(8,128)(2,1)} %collective-permute-done.2.refs_3_), channel_id=1, source_target_pairs={{0,2},{1,3},{2,4},{3,5},{4,6},{5,7},{6,0},{7,1},{8,10},{9,11},{10,... | collective-permute-start | bytes 1843208 | tf_op jit(solution)/shard_map/ppermute | solution.py:187
  45.7 14.9 %collective-permute-start.8 = (bf16[128,1280]{1,0:T(8,128)(2,1)}, bf16[128,1280]{1,0:T(8,128)(2,1)}, u32[]{:S(2)}, u32[]{:S(2)}) collective-permute-start(bf16[128,1280]{1,0:T(8,128)(2,1)} %collective-permute-done.4.refs_4_), channel_id=1, source_target_pairs={{0,72},{1,73},{2,74},{3,75},{4,76},{5,77},{6,78},{7,79},{8,64},{9,... | collective-permute-start | bytes 983048 | tf_op jit(solution)/shard_map/ppermute | solution.py:183
  48.2 12.4 %collective-permute-start.9 = (bf16[112,1280]{1,0:T(8,128)(2,1)}, bf16[112,1280]{1,0:T(8,128)(2,1)}, u32[]{:S(2)}, u32[]{:S(2)}) collective-permute-start(bf16[112,1280]{1,0:T(8,128)(2,1)} %collective-permute-done.1.refs_5_), channel_id=1, source_target_pairs={{0,72},{1,73},{2,74},{3,75},{4,76},{5,77},{6,78},{7,79},{8,64},{9,... | collective-permute-start | bytes 860168 | tf_op jit(solution)/shard_map/ppermute | solution.py:184
  65.3 40.0 %all-to-all-start = ((bf16[8,240,768]{2,1,0:T(8,128)(2,1)}), bf16[8,240,768]{2,1,0:T(8,128)(2,1)}, u32[]{:S(2)}, u32[]{:S(2)}) async-start(bf16[8,240,768]{2,1,0:T(8,128)(2,1)} %shard_map.111), calls=%async_computation | async-start | bytes 5898240 | tf_op jit(solution)/shard_map/all_to_all | solution.py:464
  163.5 22.5 %all-to-all-start.1 = ((bf16[16,80,384]{2,1,0:T(8,128)(2,1)}), bf16[16,80,384]{2,1,0:T(8,128)(2,1)S(1)}, u32[]{:S(2)}, u32[]{:S(2)}) async-start(bf16[16,80,384]{2,1,0:T(8,128)(2,1)} %shard_map.113), calls=%async_computation.1 | async-start | bytes 1966080 | tf_op jit(solution)/shard_map/all_to_all | solution.py:470
  186.1 1.0 copy-start.1

commit v10 on v8

--- a/solution.py
+++ b/solution.py
@@ -177,7 +177,7 @@
 
 def far_shards(near):
     shard, below, above, other = near
-    half = 128
+    half = 144
     far_top = lax.ppermute(below[:half], BOTH, Z_UP)
     far_bottom = lax.ppermute(above[half:], BOTH, Z_DOWN)
     far_top, other_up = lax.optimization_barrier((far_top, other))

time: 233 us -> 233 us (level)
  transfers between devices with their start and end apart: 12 -> 12, of which waited for: 4 -> 5; matrix products, arithmetic and copies ran while one was open for 0% -> 0% of each run, Pallas kernels for 10% -> 10%
where the time goes in v10:
time: 233 us; the launch traced here: 232 us
  Pallas kernels  97 us (42%)
  waiting for transfers between devices  60.3 us (26%)
  blocking collectives  44.4 us (19%)
  starting transfers between devices  28 us (12%)
    pallas_call x1, Pallas kernels, attend_full(): pl.pallas_call(functools.partial(attention_kernel, block=512, taken=taken...  58.3 us
    all_to_all x1, blocking collectives, on_device(): lax.all_to_all(send.reshape(128, 8, D + TAG), BOTH, split_axis=0, concat_...  44.4 us
    all_to_all x1, waiting for transfers between devices, on_device(): lax.all_to_all(projected, 'img', split_axis=0, concat_axis=0, tiled=True,...  34.4 us
    all_to_all x1, waiting for transfers between devices, on_device(): lax.all_to_all(attended, 'img', split_axis=0, concat_axis=0, tiled=True)  14.8 us
    pallas_call x1, Pallas kernels, layer_one(): pl.pallas_call(layer_one_kernel, out_shape=[jax.ShapeDtypeStruct((rows, D...  14.4 us
    pallas_call x2, Pallas kernels, project(): pl.pallas_call(functools.partial(project_kernel, parts=parts, offsets=off...  10.8 us
    pallas_call x1, Pallas kernels, merge(): pl.pallas_call(merge_kernel, out_shape=jax.ShapeDtypeStruct((places, D +...  7.8 us
    all_to_all x1, starting transfers between devices, on_device(): lax.all_to_all(attended, 'img', split_axis=0, concat_axis=0, tiled=True)  6.01 us
  transfers between devices with their start and end apart: 12, of which 5 were waited for; matrix products, arithmetic and copies ran while one was open for 0% of the time, Pallas kernels for 10%

profile of v10, /device:TPU:1, one launch (start us, length us, event | category | flops | bytes accessed | tf_op | source)
XLA Modules:
  0.0 232.4 jit_solution(14555085529843403125)
XLA Ops:
  0.0 3.3 %collective-permute-start.3 = (bf16[240,1280]{1,0:T(8,128)(2,1)}, bf16[240,1280]{1,0:T(8,128)(2,1)}, u32[]{:S(2)}, u32[]{:S(2)}) collective-permute-start(bf16[240,1280]{1,0:T(8,128)(2,1)} %bitcast.10), channel_id=1, source_target_pairs={{0,72},{1,73},{2,74},{3,75},{4,76},{5,77},{6,78},{7,79},{8,64},{9,... | collective-permute-start | bytes 1843208 | tf_op jit(solution)/shard_map/ppermute | solution.py:174
  3.3 1.6 collective-permute-start.1
  4.9 2.1 collective-permute-start.5
  7.1 14.4 %shard_map.109 = (bf16[384,1280]{1,0:T(8,128)(2,1)}, bf16[384,1280]{1,0:T(8,128)(2,1)}) custom-call(s32[1,384]{1,0:T(1,128)} %ids_ref.1, bf16[1,384,1280]{2,1,0:T(8,128)(2,1)} %x_ref.1, bf16[1280]{0:T(1024)(128)(2,1)} %gain_one_ref.1, bf16[1280]{0:T(1024)(128)(2,1)} %gain_two_ref.1, bf16[3,1280,1280]{2,1,0:T(8,128)(2,1)} %w_qkv_ref.1, ...), custom_call_target="tpu_custom_call" | custom-call | flops 6000000000 | bytes 16000000 | tf_op jit(solution)/shard_map/pallas_call | solution.py:124
  21.5 1.3 collective-permute-start
  22.8 0.0 collective-permute-done.1.refs_1_
  22.8 0.1 collective-permute-start.2
  23.0 2.7 %collective-permute-start.6 = (bf16[96,1280]{1,0:T(8,128)(2,1)S(1)}, bf16[96,1280]{1,0:T(8,128)(2,1)}, u32[]{:S(2)}, u32[]{:S(2)}) collective-permute-start(bf16[96,1280]{1,0:T(8,128)(2,1)S(1)} %slice.9), channel_id=1, source_target_pairs={{0,6},{1,7},{2,0},{3,1},{4,2},{5,3},{6,4},{7,5},{8,14},{9,15},{10,... | collective-permute-start | bytes 737288 | tf_op jit(solution)/shard_map/ppermute | solution.py:182
  25.7 0.0 collective-permute-done.3.refs_3_
  25.7 5.0 %collective-permute-done.6.refs_5_ = bf16[96,1280]{1,0:T(8,128)(2,1)} collective-permute-done((bf16[96,1280]{1,0:T(8,128)(2,1)S(1)}, bf16[96,1280]{1,0:T(8,128)(2,1)}, u32[]{:S(2)}, u32[]{:S(2)}) %collective-permute-start.6) | collective-permute-done | bytes 245792 | tf_op jit(solution)/shard_map/ppermute | solution.py:182
  30.7 3.5 %collective-permute-start.7 = (bf16[240,1280]{1,0:T(8,128)(2,1)}, bf16[240,1280]{1,0:T(8,128)(2,1)}, u32[]{:S(2)}, u32[]{:S(2)}) collective-permute-start(bf16[240,1280]{1,0:T(8,128)(2,1)} %collective-permute-done.3.refs_3_), channel_id=1, source_target_pairs={{0,6},{1,7},{2,0},{3,1},{4,2},{5,3},{6,4},{7,5},{8,14},{9,15},{10,... | collective-permute-start | bytes 1843208 | tf_op jit(solution)/shard_map/ppermute | solution.py:188
  34.2 0.2 collective-permute-done.2.refs_4_
  34.4 0.0 collective-permute-start.4
  34.4 0.2 collective-permute-start.8
  34.6 2.5 %collective-permute-start.9 = (bf16[96,1280]{1,0:T(8,128)(2,1)}, bf16[96,1280]{1,0:T(8,128)(2,1)}, u32[]{:S(2)}, u32[]{:S(2)}) collective-permute-start(bf16[96,1280]{1,0:T(8,128)(2,1)} %collective-permute-done.6.refs_5_), channel_id=1, source_target_pairs={{0,72},{1,73},{2,74},{3,75},{4,76},{5,77},{6,78},{7,79},{8,64},{9,... | collective-permute-start | bytes 737288 | tf_op jit(solution)/shard_map/ppermute | solution.py:187
  37.1 0.0 collective-permute-done.h_partner_ref
  37.1 1.0 copy-done
  38.0 6.1 %shard_map.110.refs_4_ = bf16[8,240,768]{2,1,0:T(8,128)(2,1)} custom-call(bf16[384,1280]{1,0:T(8,128)(2,1)} %get-tuple-element.14.h_own_ref, bf16[384,1280]{1,0:T(8,128)(2,1)} %copy-done, bf16[240,1280]{1,0:T(8,128)(2,1)} %bitcast.13, bf16[240,1280]{1,0:T(8,128)(2,1)} %copy-done.2, bf16[240,1280]{1,0:T(8,128)(2,1)} %copy-done.3, ...), custom_call_target="tpu_custom_call" | custom-call | flops 2000000000 | bytes 6000000 | tf_op jit(solution)/shard_map/pallas_call | solution.py:235
  44.2 5.9 %collective-permute-done.9.refs_3_ = bf16[96,1280]{1,0:T(8,128)(2,1)} collective-permute-done((bf16[96,1280]{1,0:T(8,128)(2,1)}, bf16[96,1280]{1,0:T(8,128)(2,1)}, u32[]{:S(2)}, u32[]{:S(2)}) %collective-permute-start.9) | collective-permute-done | bytes 245792 | tf_op jit(solution)/shard_map/ppermute | solution.py:187
  50.0 0.0 collective-permute-done.8.refs_2_
  50.0 0.0 collective-permute-done.7.refs_1_
  50.0 4.7 %shard_map.111 = bf16[8,240,768]{2,1,0:T(8,128)(2,1)} custom-call(bf16[384,1280]{1,0:T(8,128)(2,1)} %get-tuple-element.14.h_own_ref, bf16[384,1280]{1,0:T(8,128)(2,1)} %copy-done, bf16[240,1280]{1,0:T(8,128)(2,1)} %collective-permute-done.4.refs_0_, bf16[240,1280]{1,0:T(8,128)(2,1)} %collective-permute-done.7.refs_1_, ...), custom_call_target="tpu_custom_call", output_to_operand_aliasing={{}: (6, {})} | custom-call | flops 2000000000 | bytes 6000000 | tf_op jit(solution)/shard_map/pallas_call | solution.py:235
  54.7 4.7 %all-to-all-start = ((bf16[8,240,768]{2,1,0:T(8,128)(2,1)}), bf16[8,240,768]{2,1,0:T(8,128)(2,1)}, u32[]{:S(2)}, u32[]{:S(2)}) async-start(bf16[8,240,768]{2,1,0:T(8,128)(2,1)} %shard_map.111), calls=%async_computation | async-start | bytes 5898240 | tf_op jit(solution)/shard_map/all_to_all | solution.py:463
  60.1 34.4 %all-to-all-done.all_hbm = bf16[8,240,768]{2,1,0:T(8,128)(2,1)} async-done(((bf16[8,240,768]{2,1,0:T(8,128)(2,1)}), bf16[8,240,768]{2,1,0:T(8,128)(2,1)}, u32[]{:S(2)}, u32[]{:S(2)}) %all-to-all-start) | async-done | bytes 2949152 | tf_op jit(solution)/shard_map/all_to_all | solution.py:463
  94.4 58.3 %shard_map.113 = bf16[16,80,384]{2,1,0:T(8,128)(2,1)} custom-call(s32[1]{0:T(128)S(6)} %copy.14.count_ref, bf16[8,240,768]{2,1,0:T(8,128)(2,1)} %all-to-all-done.all_hbm), custom_call_target="tpu_custom_call" | custom-call | tf_op jit(solution)/shard_map/pallas_call | solution.py:345
  152.7 6.0 %all-to-all-start.1 = ((bf16[16,80,384]{2,1,0:T(8,128)(2,1)}), bf16[16,80,384]{2,1,0:T(8,128)(2,1)S(1)}, u32[]{:S(2)}, u32[]{:S(2)}) async-start(bf16[16,80,384]{2,1,0:T(8,128)(2,1)} %shard_map.113), calls=%async_computation.1 | async-start | bytes 1966080 | tf_op jit(solution)/shard_map/all_to_all | solution.py:469
  158.7 1.7 shard_map.112
  160.4 14.8 %all-to-all-done.1 = bf16[16,80,384]{2,1,0:T(8,128)(2,1)S(1)} async-done(((bf16[16,80,384]{2,1,0:T(8,128)(2,1)}), bf16[16,80,384]{2,1,0:T(8,128)(2,1)S(1)}, u32[]{:S(2)}, u32[]{:S(2)}) %all-to-all-start.1) | async-done | bytes 983072 | tf_op jit(solution)/shard_map/all_to_all | solution.py:469
  175.2 1.0 copy-done.1
  176.2 7.8 %shard_map.114 = bf16[1024,1408]{1,0:T(8,128)(2,1)} custom-call(s32[1,384]{1,0:T(1,128)} %get-tuple-element.20.bucket_ref, bf16[384,128]{1,0:T(8,128)(2,1)} %get-tuple-element.21.tag_ref, bf16[1280,384]{1,0:T(8,128)(2,1)} %bitcast.9, bf16[384,1280]{1,0:T(8,128)(2,1)} %get-tuple-element.22.x_ref, bf16[1280,1280]{1,0:T(8,128)(2,1)} %w_ref.1, ...), custom_call_target="tpu_custom_call" | custom-call | tf_op jit(solution)/shard_map/pallas_call | solution.py:380
  184.0 44.4 %all_to_all.15 = bf16[128,8,1408]{2,1,0:T(8,128)(2,1)} all-to-all(bf16[128,8,1408]{2,1,0:T(8,128)(2,1)} %bitcast.7), channel_id=1, replica_groups=mesh['ctx'=8,'img'=16] {'ctx','img'}, dimensions={0} | all-to-all | bytes 5767168 | tf_op jit(solution)/shard_map/all_to_all | solution.py:472
  228.4 4.0 %shard_map.115 = bf16[96,5120]{1,0:T(8,128)(2,1)} custom-call(bf16[1024,1408]{1,0:T(8,128)(2,1)} %bitcast.8), custom_call_target="tpu_custom_call" | custom-call | tf_op jit(solution)/shard_map/pallas_call | solution.py:403
  (10 shorter events, 0.1 us)
Async XLA Ops:
  0.0 25.7 %collective-permute-start.3 = (bf16[240,1280]{1,0:T(8,128)(2,1)}, bf16[240,1280]{1,0:T(8,128)(2,1)}, u32[]{:S(2)}, u32[]{:S(2)}) collective-permute-start(bf16[240,1280]{1,0:T(8,128)(2,1)} %bitcast.10), channel_id=1, source_target_pairs={{0,72},{1,73},{2,74},{3,75},{4,76},{5,77},{6,78},{7,79},{8,64},{9,... | collective-permute-start | bytes 1843208 | tf_op jit(solution)/shard_map/ppermute | solution.py:174
  3.3 19.5 %collective-permute-start.1 = (bf16[240,1280]{1,0:T(8,128)(2,1)}, bf16[240,1280]{1,0:T(8,128)(2,1)S(1)}, u32[]{:S(2)}, u32[]{:S(2)}) collective-permute-start(bf16[240,1280]{1,0:T(8,128)(2,1)} %bitcast.11), channel_id=1, source_target_pairs={{0,2},{1,3},{2,4},{3,5},{4,6},{5,7},{6,0},{7,1},{8,10},{9,11},{10,... | collective-permute-start | bytes 1843208 | tf_op jit(solution)/shard_map/ppermute | solution.py:172
  4.9 18.0 %collective-permute-start.5 = (bf16[240,1280]{1,0:T(8,128)(2,1)}, bf16[240,1280]{1,0:T(8,128)(2,1)S(1)}, u32[]{:S(2)}, u32[]{:S(2)}) collective-permute-start(bf16[240,1280]{1,0:T(8,128)(2,1)} %bitcast.12), channel_id=1, source_target_pairs={{0,6},{1,7},{2,0},{3,1},{4,2},{5,3},{6,4},{7,5},{8,14},{9,15},{10,... | collective-permute-start | bytes 1843208 | tf_op jit(solution)/shard_map/ppermute | solution.py:173
  21.5 15.6 %collective-permute-start = (bf16[384,1280]{1,0:T(8,128)(2,1)}, bf16[384,1280]{1,0:T(8,128)(2,1)S(1)}, u32[]{:S(2)}, u32[]{:S(2)}) collective-permute-start(bf16[384,1280]{1,0:T(8,128)(2,1)} %get-tuple-element.14.h_own_ref), channel_id=1, source_target_pairs={{0,1},{1,0},{2,3},{3,2},{4,5},{5,4},{6,7},{7,6},{8,9},{9,8},{10,11... | collective-permute-start | bytes 2949128 | tf_op jit(solution)/shard_map/ppermute | solution.py:459
  22.8 11.8 %copy-start.2 = (bf16[240,1280]{1,0:T(8,128)(2,1)}, bf16[240,1280]{1,0:T(8,128)(2,1)S(1)}, u32[]{:S(2)}) copy-start(bf16[240,1280]{1,0:T(8,128)(2,1)S(1)} %collective-permute-done.1.refs_1_) | copy-start | bytes 1843204
  22.8 11.6 %collective-permute-start.2 = (bf16[144,1280]{1,0:T(8,128)(2,1)S(1)}, bf16[144,1280]{1,0:T(8,128)(2,1)}, u32[]{:S(2)}, u32[]{:S(2)}) collective-permute-start(bf16[144,1280]{1,0:T(8,128)(2,1)S(1)} %slice.8), channel_id=1, source_target_pairs={{0,2},{1,3},{2,4},{3,5},{4,6},{5,7},{6,0},{7,1},{8,10},{9,11},{10,... | collective-permute-start | bytes 1105928 | tf_op jit(solution)/shard_map/ppermute | solution.py:181
  22.9 14.2 %copy-start.3 = (bf16[240,1280]{1,0:T(8,128)(2,1)}, bf16[240,1280]{1,0:T(8,128)(2,1)S(1)}, u32[]{:S(2)}) copy-start(bf16[240,1280]{1,0:T(8,128)(2,1)S(1)} %collective-permute-done.5.refs_2_) | copy-start | bytes 1843204
  23.0 7.7 %collective-permute-start.6 = (bf16[96,1280]{1,0:T(8,128)(2,1)S(1)}, bf16[96,1280]{1,0:T(8,128)(2,1)}, u32[]{:S(2)}, u32[]{:S(2)}) collective-permute-start(bf16[96,1280]{1,0:T(8,128)(2,1)S(1)} %slice.9), channel_id=1, source_target_pairs={{0,6},{1,7},{2,0},{3,1},{4,2},{5,3},{6,4},{7,5},{8,14},{9,15},{10,... | collective-permute-start | bytes 737288 | tf_op jit(solution)/shard_map/ppermute | solution.py:182
  30.7 19.3 %collective-permute-start.7 = (bf16[240,1280]{1,0:T(8,128)(2,1)}, bf16[240,1280]{1,0:T(8,128)(2,1)}, u32[]{:S(2)}, u32[]{:S(2)}) collective-permute-start(bf16[240,1280]{1,0:T(8,128)(2,1)} %collective-permute-done.3.refs_3_), channel_id=1, source_target_pairs={{0,6},{1,7},{2,0},{3,1},{4,2},{5,3},{6,4},{7,5},{8,14},{9,15},{10,... | collective-permute-start | bytes 1843208 | tf_op jit(solution)/shard_map/ppermute | solution.py:188
  34.4 15.6 %collective-permute-start.4 = (bf16[240,1280]{1,0:T(8,128)(2,1)}, bf16[240,1280]{1,0:T(8,128)(2,1)}, u32[]{:S(2)}, u32[]{:S(2)}) collective-permute-start(bf16[240,1280]{1,0:T(8,128)(2,1)} %collective-permute-done.3.refs_3_), channel_id=1, source_target_pairs={{0,2},{1,3},{2,4},{3,5},{4,6},{5,7},{6,0},{7,1},{8,10},{9,11},{10,... | collective-permute-start | bytes 1843208 | tf_op jit(solution)/shard_map/ppermute | solution.py:186
  34.4 15.6 %collective-permute-start.8 = (bf16[144,1280]{1,0:T(8,128)(2,1)}, bf16[144,1280]{1,0:T(8,128)(2,1)}, u32[]{:S(2)}, u32[]{:S(2)}) collective-permute-start(bf16[144,1280]{1,0:T(8,128)(2,1)} %collective-permute-done.2.refs_4_), channel_id=1, source_target_pairs={{0,72},{1,73},{2,74},{3,75},{4,76},{5,77},{6,78},{7,79},{8,64},{9,... | collective-permute-start | bytes 1105928 | tf_op jit(solution)/shard_map/ppermute | solution.py:185
  34.6 15.4 %collective-permute-start.9 = (bf16[96,1280]{1,0:T(8,128)(2,1)}, bf16[96,1280]{1,0:T(8,128)(2,1)}, u32[]{:S(2)}, u32[]{:S(2)}) collective-permute-start(bf16[96,1280]{1,0:T(8,128)(2,1)} %collective-permute-done.6.refs_5_), channel_id=1, source_target_pairs={{0,72},{1,73},{2,74},{3,75},{4,76},{5,77},{6,78},{7,79},{8,64},{9,... | collective-permute-start | bytes 737288 | tf_op jit(solution)/shard_map/ppermute | solution.py:187
  37.1 1.0 copy-start
  54.7 39.7 %all-to-all-start = ((bf16[8,240,768]{2,1,0:T(8,128)(2,1)}), bf16[8,240,768]{2,1,0:T(8,128)(2,1)}, u32[]{:S(2)}, u32[]{:S(2)}) async-start(bf16[8,240,768]{2,1,0:T(8,128)(2,1)} %shard_map.111), calls=%async_computation | async-start | bytes 5898240 | tf_op jit(solution)/shard_map/all_to_all | solution.py:463
  152.7 22.5 %all-to-all-start.1 = ((bf16[16,80,384]{2,1,0:T(8,128)(2,1)}), bf16[16,80,384]{2,1,0:T(8,128)(2,1)S(1)}, u32[]{:S(2)}, u32[]{:S(2)}) async-start(bf16[16,80,384]{2,1,0:T(8,128)(2,1)} %shard_map.113), calls=%async_computation.1 | async-start | bytes 1966080 | tf_op jit(solution)/shard_map/all_to_all | solution.py:469
  175.2 1.0 copy-start.1
